TPU v7x, 32 devices: a whole 2x2x4 slice. The times are simulated.
32 devices in a mesh: dp: 8 (over z, x), tile: 4 (over y, core).
Axes of the slice: x: 2, y: 2, z: 4, core: 2. Of those that a mesh axis runs over, the one named last changes fastest.
Arguments:
- features: bfloat16 [8, 8, 8, 8, 1584], P('dp', 'tile'), may hold values from -6 to 6
- cotangent: bfloat16 [8, 8, 8, 8, 1584], P('dp', 'tile'), may hold values from -6 to 6
- conv_weight: bfloat16 [29408, 128], P('dp'), may hold values from -0.125 to 0.125
- squeeze_weight: bfloat16 [1584, 363], replicated, may hold values from -0.15625 to 0.15625
- excite_weight: bfloat16 [363, 1584], replicated, may hold values from -0.3125 to 0.3125
- live_count: int32 [8, 4], P('dp', 'tile'), may hold values from 1 to 2, as said below
- neighbours: int32 [8, 8, 8], P('dp', 'tile'), may hold values from -1 to 7, as said below
Outputs:
- output: bfloat16 [8, 8, 8, 8, 1584], P('dp', 'tile')
- grad_features: bfloat16 [8, 8, 8, 8, 1584], P('dp', 'tile')
- grad_conv: float32 [29408, 128], P('dp')
- grad_squeeze: float32 [1584, 363], replicated
- grad_excite: float32 [363, 1584], replicated
Inputs may be any that keep to these rules, and one draw needn't show every extreme that they name: `live_count`: the tiles with tissue on a device fill its first slots; in every slide some device has all 2 slots filled. `neighbours`: an entry is -1 or the index of a tile with tissue of the same slide (device index times 2 plus slot); a slot without tissue lists only -1.
All inputs are finite; a program needn't handle non-finite values.
Results may differ from a plain program's by a relative error of at most 0.006.
Values may be sent and summed in bfloat16 or wider, within the bound.
No kernel may reach another device: no remote copies, remote signals or barrier semaphores. Data moves between devices by JAX's collectives and lax.ppermute only.
A program may use at most 128 MiB of HBM per device.

v0:
```python
import jax
import jax.numpy as jnp
from jax import lax
from jax.sharding import PartitionSpec as P

CG = 264
GROUPS = 6


def make_strips(tile_data):
    return jnp.stack(
        [tile_data[:, 0], tile_data[:, -1], tile_data[:, :, 0], tile_data[:, :, -1]], axis=1
    )


def fetch_rim(piece_all, safe_ids, present, offset):
    fetched = jnp.take(piece_all, safe_ids[:, offset], axis=0)
    keep_row = present[:, offset].reshape((-1,) + (1,) * (fetched.ndim - 1))
    return jnp.where(keep_row, fetched, jnp.zeros_like(fetched))


def pad_tiles(tile_data, strips, neighbor_ids):
    last_pos = tile_data.shape[1] - 1
    present = neighbor_ids >= 0
    safe_ids = jnp.maximum(neighbor_ids, 0)
    corner_tl = fetch_rim(strips[:, 1, last_pos], safe_ids, present, 0)
    top_row = fetch_rim(strips[:, 1], safe_ids, present, 1)
    corner_tr = fetch_rim(strips[:, 1, 0], safe_ids, present, 2)
    left_col = fetch_rim(strips[:, 3], safe_ids, present, 3)
    right_col = fetch_rim(strips[:, 2], safe_ids, present, 4)
    corner_bl = fetch_rim(strips[:, 0, last_pos], safe_ids, present, 5)
    bottom_row = fetch_rim(strips[:, 0], safe_ids, present, 6)
    corner_br = fetch_rim(strips[:, 0, 0], safe_ids, present, 7)
    upper = jnp.concatenate([corner_tl[:, None], top_row, corner_tr[:, None]], axis=1)
    lower = jnp.concatenate([corner_bl[:, None], bottom_row, corner_br[:, None]], axis=1)
    middle = jnp.concatenate([left_col[:, :, None], tile_data, right_col[:, :, None]], axis=2)
    return jnp.concatenate([upper[:, None], middle, lower[:, None]], axis=1)


def unfold(padded):
    edge_len = padded.shape[1] - 2
    parts = [
        padded[:, row_off : row_off + edge_len, col_off : col_off + edge_len]
        for row_off in range(3)
        for col_off in range(3)
    ]
    return jnp.stack(parts, axis=3).reshape(-1, 9, padded.shape[-1])


def fold_back(col_grads, slot_num, edge_len):
    shaped = col_grads.reshape(slot_num, edge_len, edge_len, 9, col_grads.shape[-1])
    grad_pad = jnp.zeros((slot_num, edge_len + 2, edge_len + 2, col_grads.shape[-1]), jnp.float32)
    for tap_pos in range(9):
        row_off, col_off = divmod(tap_pos, 3)
        grad_pad = grad_pad.at[:, row_off : row_off + edge_len, col_off : col_off + edge_len].add(
            shaped[:, :, :, tap_pos]
        )
    return grad_pad


def conv_forward(padded, kernel):
    slot_num = padded.shape[0]
    edge_len = padded.shape[1] - 2
    patches = unfold(padded)
    hidden = jnp.einsum(
        "rkgi,gkio->rgo",
        patches.reshape(patches.shape[0], 9, GROUPS, CG),
        kernel,
        preferred_element_type=jnp.float32,
    )
    return hidden.reshape(slot_num, edge_len, edge_len, GROUPS * CG)


def conv_backward(padded, hidden_grad, kernel):
    slot_num = padded.shape[0]
    edge_len = padded.shape[1] - 2
    patches = unfold(padded)
    grad_rows = hidden_grad.reshape(-1, GROUPS, CG)
    col_grads = jnp.einsum("rgo,gkio->rkgi", grad_rows, kernel, preferred_element_type=jnp.float32)
    grad_pad = fold_back(col_grads.reshape(-1, 9, GROUPS * CG), slot_num, edge_len)
    grad_w = jnp.einsum(
        "rkgi,rgo->gkio",
        patches.reshape(patches.shape[0], 9, GROUPS, CG),
        grad_rows,
        preferred_element_type=jnp.float32,
    )
    return (grad_pad, grad_w)


def border_pieces(grad_pad):
    edges = jnp.stack(
        [grad_pad[:, 0, 1:-1], grad_pad[:, 1:-1, 0], grad_pad[:, 1:-1, -1], grad_pad[:, -1, 1:-1]],
        axis=1,
    )
    corners = jnp.stack(
        [grad_pad[:, 0, 0], grad_pad[:, 0, -1], grad_pad[:, -1, 0], grad_pad[:, -1, -1]], axis=1
    )
    return (edges.astype(jnp.bfloat16), corners.astype(jnp.bfloat16))


def border_in(edges_all, corners_all, ids_all, own_ids, edge_len):
    matches = (ids_all[None, :, :] == own_ids[:, None, None]).astype(jnp.bfloat16)

    def spread_edge(offset, member):
        return jnp.einsum(
            "st,tpc->spc",
            matches[:, :, offset],
            edges_all[:, member],
            preferred_element_type=jnp.float32,
        )

    def spread_corner(offset, member):
        return jnp.einsum(
            "st,tc->sc",
            matches[:, :, offset],
            corners_all[:, member],
            preferred_element_type=jnp.float32,
        )

    last_pos = edge_len - 1
    incoming = jnp.zeros((own_ids.shape[0], edge_len, edge_len, edges_all.shape[-1]), jnp.float32)
    incoming = incoming.at[:, last_pos, :].add(spread_edge(1, 0))
    incoming = incoming.at[:, :, last_pos].add(spread_edge(3, 1))
    incoming = incoming.at[:, :, 0].add(spread_edge(4, 2))
    incoming = incoming.at[:, 0, :].add(spread_edge(6, 3))
    incoming = incoming.at[:, last_pos, last_pos].add(spread_corner(0, 0))
    incoming = incoming.at[:, last_pos, 0].add(spread_corner(2, 1))
    incoming = incoming.at[:, 0, last_pos].add(spread_corner(5, 2))
    incoming = incoming.at[:, 0, 0].add(spread_corner(7, 3))
    return incoming


def dsilu(value):
    sig = jax.nn.sigmoid(value)
    return sig * (1.0 + value * (1.0 - sig))


def shards(features, cotangent, conv_weight, squeeze_weight, excite_weight, live_count, neighbours):
    high = lax.Precision.HIGHEST
    tile_data = features[0]
    slot_num = tile_data.shape[0]
    edge_len = tile_data.shape[1]
    slot_count = live_count[0, 0]
    neighbor_ids = neighbours[0]
    tile_mask = (jnp.arange(slot_num) < slot_count).astype(jnp.float32)[:, None, None, None]
    weights_all = lax.all_gather(conv_weight, "dp", axis=0, tiled=True)
    kernel = weights_all.reshape(-1)[: GROUPS * 9 * CG * CG].reshape(GROUPS, 9, CG, CG)
    strips = lax.all_gather(make_strips(tile_data), "tile", axis=0, tiled=True)
    padded = pad_tiles(tile_data, strips, neighbor_ids)
    hidden = conv_forward(padded, kernel)
    active = (jax.nn.silu(hidden) * tile_mask).astype(jnp.bfloat16)
    active_f = active.astype(jnp.float32)
    pooled_sum, tissue = lax.psum(
        (jnp.sum(active, axis=(0, 1, 2), dtype=jnp.float32), slot_count.astype(jnp.float32)), "tile"
    )
    pixel_total = tissue * (edge_len * edge_len)
    pooled = pooled_sum / pixel_total
    w_squeeze = squeeze_weight.astype(jnp.float32)
    w_excite = excite_weight.astype(jnp.float32)
    squeeze_pre = jnp.dot(pooled, w_squeeze, precision=high)
    squeezed = jax.nn.silu(squeeze_pre)
    excite = jax.nn.sigmoid(jnp.dot(squeezed, w_excite, precision=high))
    output = ((tile_data.astype(jnp.float32) + active_f * excite) * tile_mask).astype(jnp.bfloat16)
    cot_live = cotangent[0].astype(jnp.float32) * tile_mask
    gate_grad = lax.psum(jnp.sum(cot_live * active_f, axis=(0, 1, 2)), "tile")
    excite_pre_grad = gate_grad * excite * (1.0 - excite)
    squeeze_pre_grad = jnp.dot(excite_pre_grad, w_excite.T, precision=high) * dsilu(squeeze_pre)
    pool_grad = jnp.dot(squeeze_pre_grad, w_squeeze.T, precision=high)
    hidden_grad = (
        (cot_live * excite + pool_grad / pixel_total) * dsilu(hidden) * tile_mask
    ).astype(jnp.bfloat16)
    grad_pad, grad_w = conv_backward(padded, hidden_grad, kernel)
    edges, corners = border_pieces(grad_pad)
    edges_all, corners_all, ids_all = (
        lax.all_gather(edges, "tile", axis=0, tiled=True),
        lax.all_gather(corners, "tile", axis=0, tiled=True),
        lax.all_gather(neighbor_ids, "tile", axis=0, tiled=True),
    )
    own_ids = lax.axis_index("tile") * slot_num + jnp.arange(slot_num, dtype=jnp.int32)
    incoming = border_in(edges_all, corners_all, ids_all, own_ids, edge_len)
    grad_in = (
        (cotangent[0].astype(jnp.float32) + grad_pad[:, 1:-1, 1:-1] + incoming) * tile_mask
    ).astype(jnp.bfloat16)
    pooled_all, squeeze_all, squeezed_all, excite_all = (
        lax.all_gather(pooled[None], "dp", axis=0, tiled=True),
        lax.all_gather(squeeze_pre_grad[None], "dp", axis=0, tiled=True),
        lax.all_gather(squeezed[None], "dp", axis=0, tiled=True),
        lax.all_gather(excite_pre_grad[None], "dp", axis=0, tiled=True),
    )
    grad_squeeze = jnp.dot(pooled_all.T, squeeze_all, precision=high)
    grad_excite = jnp.dot(squeezed_all.T, excite_all, precision=high)
    total_rows = conv_weight.shape[0] * lax.axis_size("dp")
    flat_grad = grad_w.reshape(-1)
    flat_grad = jnp.pad(flat_grad, (0, total_rows * 128 - flat_grad.shape[0])).reshape(
        total_rows, 128
    )
    grad_shard = lax.psum_scatter(flat_grad, "dp", scatter_dimension=0, tiled=True)
    grad_shard = lax.psum(grad_shard, "tile")
    return (output[None], grad_in[None], grad_shard, grad_squeeze, grad_excite)


def solution(mesh):
    return jax.shard_map(
        shards,
        mesh=mesh,
        in_specs=(
            P("dp", "tile", None, None, None),
            P("dp", "tile", None, None, None),
            P("dp", None),
            P(),
            P(),
            P("dp", "tile"),
            P("dp", "tile", None),
        ),
        out_specs=(
            P("dp", "tile", None, None, None),
            P("dp", "tile", None, None, None),
            P("dp", None),
            P(),
            P(),
        ),
        check_vma=False,
    )
```

profile of v0, /device:TPU:0, one launch (start us, length us, event | category | flops | bytes accessed | tf_op | source)
XLA Modules:
  0.0 803.2 jit_solution(7853282426224498124)
XLA Ops:
  14.0 10.4 %all_gather.27 = bf16[8,4,8,1584]{3,2,1,0:T(8,128)(2,1)S(1)} all-gather(bf16[2,4,8,1584]{3,2,1,0:T(8,128)(2,1)S(1)} %pad_maximum_fusion.3), channel_id=1, replica_groups=mesh['dp'=8,'tile'=4] {'tile'}, dimensions={0}, use_global_device_ids=true | all-gather | bytes 1013760 | tf_op jit(solution)/shard_map/all_gather | solution.py:148
  101.2 5.6 all-gather
  120.8 6.5 all-gather.8.cloned.1.call-done
  127.3 7.0 reshape.920
  134.3 21.8 %reshape.797 = bf16[6,9,264,264]{3,2,1,0:T(8,128)(2,1)} reshape(bf16[29403,128]{1,0:T(8,128)(2,1)} %bitcast.251) | data formatting | bytes 15054336 | tf_op jit(solution)/shard_map/reshape | solution.py:147
  156.1 9.4 %convert_reduce_fusion = (f32[6,264]{1,0:T(8,128)S(1)}, f32[128,6,264]{0,2,1:T(8,128)}) fusion(f32[128]{0:T(128)S(1)} %mul.144, bf16[128,9,6,264]{0,3,1,2:T(8,128)(2,1)} %constant_dynamic-update-slice_fusion, bf16[6,9,264,264]{3,2,1,0:T(8,128)(2,1)} %reshape.797), kind=kOutput, calls=%fused_computation.53 | convolution fusion | flops 965097920 | bytes 11994560 | tf_op jit(solution)/shard_map/rkgi,gkio->rgo/dot_general | solution.py:65
  170.2 11.1 %all-reduce.10 = (f32[1584]{0:T(1024)S(1)}, f32[]{:T(128)}, f32[1584]{0:T(1024)S(1)}) all-reduce(f32[1584]{0:T(1024)S(1)} %reduce_sum.21, f32[]{:T(128)S(6)} %convert_element_type.82, f32[1584]{0:T(1024)S(1)} %fusion.24), channel_id=1, replica_groups=mesh['dp'=8,'tile'=4] {'tile'}, use_global_device_ids=true, to_apply=%region_1.4 | all-reduce | flops 3169 | bytes 25352 | tf_op jit(solution)/shard_map/psum | solution.py:153
  189.5 11.1 %convolution_bitcast_fusion = f32[128,9,6,264]{0,3,1,2:T(8,128)} fusion(bf16[6,9,264,264]{3,2,1,0:T(8,128)(2,1)} %reshape.797, f32[128,6,264]{0,2,1:T(8,128)S(1)} %copy-done.5, f32[128,6,264]{0,2,1:T(8,128)S(1)} %copy-done.3, f32[6,264]{1,0:T(8,128)S(1)} %add.210, f32[6,264]{1,0:T(8,128)S(1)} %mul.153, f32[128]{0:T(128)S(1)} %mul.144), kind=kOutput, calls=%fused_computation.9 | convolution fusion | flops 966113280 | bytes 16461440 | tf_op jit(solution)/shard_map/rgo,gkio->rkgi/dot_general | solution.py:79
  200.7 11.9 %copy.520 = f32[128,9,6,264]{3,2,0,1:T(8,128)} copy(f32[128,9,6,264]{0,3,1,2:T(8,128)} %convolution_bitcast_fusion) | data formatting | bytes 14598144 | tf_op jit(solution)/shard_map/rgo,gkio->rkgi/transpose | solution.py:79
  212.6 12.7 %reshape_reshape.2 = f32[2,8,8,9,1584]{4,2,1,0,3:T(8,128)} reshape(f32[128,9,6,264]{3,2,0,1:T(8,128)} %copy.520) | data formatting | bytes 14598144 | tf_op jit(solution)/shard_map/reshape;reshape | solution.py:51
  230.1 10.0 %scatter-add.59 = f32[2,10,10,1584]{3,2,1,0:T(8,128)S(1)} dynamic-update-slice(f32[2,10,10,1584]{3,2,1,0:T(8,128)S(1)} %scatter-add.56, f32[2,8,8,1584]{3,2,1,0:T(8,128)} %fusion.22, s32[]{:T(128)} %constant.510.clone.1, s32[]{:T(128)} %bitcast.35, s32[]{:T(128)} %bitcast.36, s32[]{:T(128)} %constant.510.clone.1) | dynamic-update-slice | bytes 1622020 | tf_op jit(solution)/shard_map/scatter-add | solution.py:55
  243.3 9.6 %scatter-add.60 = f32[2,10,10,1584]{3,2,1,0:T(8,128)S(1)} dynamic-update-slice(f32[2,10,10,1584]{3,2,1,0:T(8,128)S(1)} %scatter-add.59, f32[2,8,8,1584]{3,2,1,0:T(8,128)S(1)} %add_select_fusion, s32[]{:T(128)} %constant.510.clone.1, s32[]{:T(128)} %bitcast.38, s32[]{:T(128)} %bitcast.39, s32[]{:T(128)} %constant.510.clone.1) | dynamic-update-slice | bytes 1622020 | tf_op jit(solution)/shard_map/scatter-add | solution.py:55
  255.6 7.7 scatter-add.64
  264.6 7.7 scatter-add.65
  275.0 7.0 scatter-add.69
  284.2 6.9 scatter-add.70
  292.5 13.3 %fusion.26 = f32[6,9,264,264]{3,2,1,0:T(8,128)} fusion(bf16[128,9,6,264]{0,3,1,2:T(8,128)(2,1)} %constant_dynamic-update-slice_fusion, f32[128,6,264]{0,2,1:T(8,128)S(1)} %copy-done.6, f32[128,6,264]{0,2,1:T(8,128)S(1)} %copy-done.4, f32[6,264]{1,0:T(8,128)S(1)} %add.210, f32[6,264]{1,0:T(8,128)S(1)} %mul.153, f32[128]{0:T(128)S(1)} %mul.144), kind=kOutput, calls=%fused_computation.60 | convolution fusion | flops 966113280 | bytes 20339072 | tf_op jit(solution)/shard_map/rkgi,rgo->gkio/dot_general | solution.py:81
  305.9 8.4 %all_gather.30 = bf16[8,4,8,1584]{3,2,1,0:T(8,128)(2,1)S(1)} all-gather(bf16[2,4,8,1584]{3,2,1,0:T(8,128)(2,1)S(1)} %pad_maximum_fusion.4), channel_id=1, replica_groups=mesh['dp'=8,'tile'=4] {'tile'}, dimensions={0}, use_global_device_ids=true | all-gather | bytes 1013760 | tf_op jit(solution)/shard_map/all_gather | solution.py:175
  322.6 5.4 all_gather.31
  332.5 22.8 %reshape.822 = f32[3763584]{0:T(1024)} reshape(f32[6,9,264,264]{3,2,1,0:T(8,128)} %fusion.26) | data formatting | bytes 30108672 | tf_op jit(solution)/shard_map/reshape | solution.py:193
  355.3 11.0 %pad_bitcast_fusion = f32[29408,128]{1,0:T(8,128)} fusion(f32[3763584]{0:T(1024)} %reshape.822), kind=kLoop, calls=%fused_computation.8 | loop fusion | bytes 30111232 | tf_op jit(solution)/shard_map/reshape | solution.py:194
  366.3 293.8 %fusion = f32[3680,128]{1,0:T(8,128)} fusion(f32[29408,128]{1,0:T(8,128)} %pad_bitcast_fusion), kind=kCustom, calls=%all-reduce-scatter | all-reduce-scatter fusion | flops 3768321 | bytes 16941568
  675.4 67.6 %all-reduce.16.cloned.1.call-done = (f32[12672]{0:T(1024)}, f32[2904]{0:T(1024)}, f32[2904]{0:T(1024)}, f32[12672]{0:T(1024)}) async-done(((f32[12672]{0:T(1024)}, f32[2904]{0:T(1024)}, f32[2904]{0:T(1024)}, f32[12672]{0:T(1024)}), (f32[12672]{0:T(1024)}, f32[2904]{0:T(1024)}, f32[2904]{0:T(1024)}, f32[12672]{0:T(1024)})) %all-reduce.16.cloned.1.call-update) | async-done | bytes 124624
  753.5 40.1 %all-reduce.14.cloned.1.call-done = f32[3676,128]{1,0:T(8,128)} async-done(((f32[3676,128]{1,0:T(8,128)}), f32[3676,128]{1,0:T(8,128)}) %all-reduce.14.cloned.1.call-update) | async-done | bytes 1882128 | tf_op jit(solution)/shard_map/psum | solution.py:198
  (264 shorter events, 166.3 us)
Async XLA Ops:
  7.2 178.9 %copy-start = (bf16[363,1584]{0,1:T(8,128)(2,1)S(1)}, bf16[363,1584]{0,1:T(8,128)(2,1)}, u32[]{:S(2)}) copy-start(bf16[363,1584]{0,1:T(8,128)(2,1)} %param.49) | copy-start | bytes 3449956
  7.2 4.7 copy-start.26
  7.2 120.1 %all-gather.8.cloned.1.call-start = ((), (), s32[]{:S(2)}) async-start(), calls=%async_computation.1 | async-start | bytes 8478720 | tf_op jit(solution)/shard_map/all_gather | solution.py:146
  7.9 735.0 %all-reduce.16.cloned.1.call-start = ((), (), s32[]{:S(2)}) async-start(), calls=%async_computation.2 | async-start | bytes 262144
  75.7 6.8 copy-start.13
  88.1 5.1 copy-start.12
  92.0 5.1 copy-start.28
  92.0 7.1 copy-start.9
  99.1 10.1 %copy-start.29 = (s32[4]{0:T(128)S(1)}, s32[4]{0:T(128)}, u32[]{:S(2)}) copy-start(s32[4]{0:T(128)} %constant.522.clone.1) | copy-start | bytes 52
  99.1 10.1 %copy-start.30 = (s32[4]{0:T(128)S(1)}, s32[4]{0:T(128)}, u32[]{:S(2)}) copy-start(s32[4]{0:T(128)} %constant.517.clone.1) | copy-start | bytes 52
  101.2 14.4 %copy-start.15 = (bf16[128,1,6,264]{0,3,1,2:T(8,128)(2,1)S(1)}, bf16[128,1,6,264]{0,3,1,2:T(8,128)(2,1)}, u32[]{:S(2)}) copy-start(bf16[128,1,6,264]{0,3,1,2:T(8,128)(2,1)} %copy.510) | copy-start | bytes 1216516
  101.2 15.3 %copy-start.14 = (bf16[128,1,6,264]{0,3,1,2:T(8,128)(2,1)S(1)}, bf16[128,1,6,264]{0,3,1,2:T(8,128)(2,1)}, u32[]{:S(2)}) copy-start(bf16[128,1,6,264]{0,3,1,2:T(8,128)(2,1)} %copy.511) | copy-start | bytes 1216516
  101.2 16.2 %copy-start.16 = (bf16[128,1,6,264]{0,3,1,2:T(8,128)(2,1)S(1)}, bf16[128,1,6,264]{0,3,1,2:T(8,128)(2,1)}, u32[]{:S(2)}) copy-start(bf16[128,1,6,264]{0,3,1,2:T(8,128)(2,1)} %copy.512) | copy-start | bytes 1216516
  111.9 6.4 copy-start.17
  113.8 5.3 copy-start.18
  115.6 4.3 copy-start.19
  167.3 18.6 %copy-start.2 = (f32[128,6,264]{2,1,0:T(8,128)}, f32[128,6,264]{2,1,0:T(8,128)S(1)}, u32[]{:S(2)}) copy-start(f32[128,6,264]{2,1,0:T(8,128)S(1)} %copy.517) | copy-start | bytes 2433028
  182.0 6.3 copy-start.7
  186.1 14.6 %copy-start.23 = (f32[2904]{0:T(1024)}, f32[2904]{0:T(1024)S(1)}, u32[]{:S(2)}) copy-start(f32[2904]{0:T(1024)S(1)} %get-tuple-element.298) | copy-start | bytes 34852
  187.3 13.4 %copy-start.21 = (f32[12672]{0:T(1024)}, f32[12672]{0:T(1024)S(1)}, u32[]{:S(2)}) copy-start(f32[12672]{0:T(1024)S(1)} %get-tuple-element.254) | copy-start | bytes 152068
  188.2 12.5 %copy-start.22 = (f32[2904]{0:T(1024)}, f32[2904]{0:T(1024)S(1)}, u32[]{:S(2)}) copy-start(f32[2904]{0:T(1024)S(1)} %get-tuple-element.256) | copy-start | bytes 34852
  660.8 6.4 collective-permute-start
  667.1 126.4 %all-reduce.14.cloned.1.call-start = ((), (), s32[]{:S(2)}) async-start(), calls=%async_computation | async-start | bytes 3768320 | tf_op jit(solution)/shard_map/psum | solution.py:198
  749.9 46.5 %copy-start.1 = (bf16[363,1584]{0,1:T(8,128)(2,1)S(1)}, bf16[363,1584]{0,1:T(8,128)(2,1)}, u32[]{:S(2)}) copy-start(bf16[363,1584]{0,1:T(8,128)(2,1)} %param.49) | copy-start | bytes 3449956
  (11 other events, 19.3 us)
Sparse Core Ops, SparseCore 0:
  10.2 117.0 all-gather.7
  667.2 75.6 all-reduce.15
  746.0 47.4 all-reduce.13
where the time goes:
time: 811 us; the launch traced here: 803 us
  blocking collectives  335 us (41%)
  local copies, waits for them, and re-layouts  244 us (30%)
  waiting for transfers between devices  115 us (14%)
  matrix products  46.9 us (6%)
  other arithmetic  43.1 us (5%)
  between operations  18.2 us (2%)
    unnamed x1, blocking collectives  294 us
    unnamed x5, waiting for transfers between devices  68.3 us
    scatter-add x7, local copies, waits for them, and re-layouts, fold_back(): grad_pad.at[:, row_off:row_off + edge_len, col_off:col_off + edge_len]  48.9 us
    psum x1, waiting for transfers between devices, shards(): grad_shard = lax.psum(grad_shard, 'tile')  40.1 us
    another operation x19, local copies, waits for them, and re-layouts, unfold(): return jnp.stack(parts, axis=3).reshape(-1, 9, padded.shape[-1])  34 us
    unnamed x87, local copies, waits for them, and re-layouts  31 us
    reshape x1, local copies, waits for them, and re-layouts, shards(): flat_grad = grad_w.reshape(-1)  22.8 us
    reshape x1, local copies, waits for them, and re-layouts, shards(): weights_all.reshape(-1)[:GROUPS * 9 * CG * CG].reshape(GROUPS, 9, CG, CG)  21.8 us
  transfers between devices with their start and end apart: 4, of which 3 were waited for; matrix products, arithmetic and copies ran while one was open for 14% of the time, Pallas kernels for 0%

commit v1 on v0

v1 whole, which is shorter than its diff:
```python
import functools

import jax
import jax.numpy as jnp
from jax import lax
from jax.experimental import pallas as pl
from jax.experimental.pallas import tpu as pltpu
from jax.sharding import Mesh, PartitionSpec as P

CG = 264
HALF = 3 * CG
TAPROWS = 27 * CG
LEAD = 33 * (TAPROWS // 16)
CH = 2 * HALF
F32 = jnp.float32
BF16 = jnp.bfloat16
SWAP = [(0, 1), (1, 0)]
PCH = 64
NCH = 7
OROWS = 16 * PCH * NCH + 8
VMEM = pl.BlockSpec(memory_space=pltpu.VMEM)
SMEM = pl.BlockSpec(memory_space=pltpu.SMEM)
HBM = pl.BlockSpec(memory_space=pl.ANY)


def params():
    return pltpu.CompilerParams(vmem_limit_bytes=56 * 1024 * 1024)


def swap(value, axis):
    return lax.ppermute(value, axis, SWAP)


class Sizes:
    def __init__(self, rows, dl_num):
        self.rows = rows
        self.dl_num = dl_num
        self.bound = rows * dl_num - LEAD
        self.top = -(-self.bound // 16) * 16
        self.half = -(-rows // 64) * 32
        self.second = rows - self.half
        self.quarter = self.half // 2
        self.piece = -(-(self.quarter + self.top) // 48) * 48
        self.flat = self.top + 33 * PCH * NCH + 8


def split_body(sc, x_ref, mine_ref, send_ref):
    low = sc[0] == 0
    for slot in range(2):
        x = x_ref[64 * slot : 64 * slot + 64, :]
        x = jnp.where(slot < sc[4], x, jnp.zeros_like(x))
        first, second = x[:, :HALF], x[:, HALF:]
        mine_ref[slot] = jnp.where(low, first, second)
        send_ref[slot] = jnp.where(low, second, first)


def split_halves(sc, x):
    shape = jax.ShapeDtypeStruct((2, 64, HALF), BF16)
    return pl.pallas_call(
        split_body,
        out_shape=(shape, shape),
        in_specs=[SMEM, VMEM],
        out_specs=(VMEM, VMEM),
        compiler_params=params(),
        name="split_halves",
    )(sc, x)


def join_body(sc, a_ref, b_ref, out_ref, wide):
    low = sc[0] == 0
    for slot in range(2):
        a = a_ref[slot].astype(F32)
        b = b_ref[slot].astype(F32)
        live = slot < sc[4]
        first = jnp.where(low, a, b)
        second = jnp.where(low, b, a)
        wide[:, :HALF] = jnp.where(live, first, 0.0)
        wide[:, HALF:] = jnp.where(live, second, 0.0)
        out_ref[64 * slot : 64 * slot + 64, :] = wide[...].astype(BF16)


def join_halves(sc, a, b):
    return pl.pallas_call(
        join_body,
        out_shape=jax.ShapeDtypeStruct((128, CH), BF16),
        in_specs=[SMEM, VMEM, VMEM],
        out_specs=VMEM,
        scratch_shapes=[pltpu.VMEM((64, CH), F32)],
        compiler_params=params(),
        name="join_halves",
    )(sc, a, b)


def strips_body(own_ref, other_ref, out_ref):
    for t in range(4):
        ref = own_ref if t < 2 else other_ref
        x = ref[t % 2].astype(F32)
        cube = x.reshape(8, 8, HALF)
        out = jnp.concatenate([x[:8], x[56:], cube[:, 0, :], cube[:, 7, :]], axis=0)
        out_ref[t] = out.astype(BF16)


def make_strips(own, other):
    return pl.pallas_call(
        strips_body,
        out_shape=jax.ShapeDtypeStruct((4, 32, HALF), BF16),
        in_specs=[VMEM, VMEM],
        out_specs=VMEM,
        compiler_params=params(),
        name="make_strips",
    )(own, other)


def pad_body(sc, ids, own_ref, other_ref, s0, s1, s2, s3, x3_ref, strips, pad):
    for rel, ref in enumerate((s0, s1, s2, s3)):
        strips[rel] = ref[...]
    for t in range(4):
        ref = own_ref if t < 2 else other_ref
        x = ref[t % 2].astype(F32)
        for i in range(8):
            pad[1 + i, t, 1:9, :] = x[8 * i : 8 * i + 8]

        def piece(offset, member):
            n = ids[t, offset]
            safe = jnp.maximum(n, 0)
            rel = jnp.bitwise_xor(lax.shift_right_logical(safe, 1), sc[5])
            other = 2 * (t // 2) + jnp.bitwise_and(safe, 1)
            got = strips[rel, other].astype(F32)[8 * member : 8 * member + 8]
            return jnp.where(n >= 0, got, 0.0)

        pad[0, t, 0:1, :] = piece(0, 1)[7:8]
        pad[0, t, 1:9, :] = piece(1, 1)
        pad[0, t, 9:10, :] = piece(2, 1)[0:1]
        left = piece(3, 3)
        right = piece(4, 2)
        for i in range(8):
            pad[1 + i, t, 0:1, :] = left[i : i + 1]
            pad[1 + i, t, 9:10, :] = right[i : i + 1]
        pad[9, t, 0:1, :] = piece(5, 0)[7:8]
        pad[9, t, 1:9, :] = piece(6, 0)
        pad[9, t, 9:10, :] = piece(7, 0)[0:1]
    for i in range(10):
        for dx in range(3):
            row = pad[i, :, dx : dx + 8, :].reshape(32, HALF)
            for g in range(3):
                x3_ref[g, dx, i] = row[:, CG * g : CG * g + CG].astype(BF16)


def pad_tiles(sc, ids, own, other, strips):
    return pl.pallas_call(
        pad_body,
        out_shape=jax.ShapeDtypeStruct((3, 3, 10, 32, CG), BF16),
        in_specs=[SMEM, SMEM] + [VMEM] * 6,
        out_specs=VMEM,
        scratch_shapes=[
            pltpu.VMEM((4, 4, 32, HALF), BF16),
            pltpu.VMEM((10, 4, 16, HALF), F32),
        ],
        compiler_params=params(),
        name="pad_tiles",
    )(sc, ids, own, other, *strips)


def regroup_body(own_ref, other_ref, out_ref):
    x = [(own_ref if t < 2 else other_ref)[t % 2].astype(F32) for t in range(4)]
    for i in range(8):
        row = jnp.concatenate([x[t][8 * i : 8 * i + 8] for t in range(4)], axis=0)
        for g in range(3):
            out_ref[g, 32 * i : 32 * i + 32, :] = row[:, CG * g : CG * g + CG].astype(BF16)


def regroup(own, other):
    return pl.pallas_call(
        regroup_body,
        out_shape=jax.ShapeDtypeStruct((3, 256, CG), BF16),
        in_specs=[VMEM, VMEM],
        out_specs=VMEM,
        compiler_params=params(),
        name="regroup",
    )(own, other)


def weight_body(sizes, plan, sc, *refs):
    count = len(plan)
    srcs = refs[: count]
    bnd_ref, w_ref, land, flat, o0, o1, o2, sems = refs[count:]
    copies = []
    for pos, (rel, slot) in enumerate(plan):
        if rel is None:
            dst = land.at[:, slot]
        else:
            part = jnp.bitwise_xor(sc[2], slot[1]) if isinstance(slot, tuple) else slot
            dl = jnp.bitwise_xor(sc[1], rel)
            dst = land.at[dl, part]
            if isinstance(slot, tuple) and slot[0] is not None:
                dst = land.at[dl, part, pl.ds(slot[0] * sizes.quarter, sizes.quarter)]
        copies.append(pltpu.make_async_copy(srcs[pos], dst, sems.at[pos]))
        copies[-1].start()
    flat[: sizes.top, :] = bnd_ref[...].astype(F32)
    for copy in copies:
        copy.wait()
    for dl in range(sizes.dl_num):
        start = sizes.top + sizes.rows * dl
        flat[start : start + sizes.half, :] = land[dl, 0].astype(F32)
        start += sizes.second
        flat[start : start + sizes.half, :] = land[dl, 1].astype(F32)
    base = jnp.where(sc[0] == 0, sizes.top, sizes.top - sizes.bound)

    @pl.loop(0, NCH)
    def _(ch):
        start = base + ch * (33 * PCH)
        for k in range(16):
            rows = [flat[pl.ds(start + 2 * k + j, PCH, stride=33), :] for j in range(3)]
            x = jnp.concatenate(rows, axis=1)
            if k:
                x = pltpu.roll(x, 384 - 8 * k, axis=1)
            for col, ref in enumerate((o0, o1, o2)):
                ref[pl.ds(ch * (16 * PCH) + k, PCH, stride=16), :] = x[:, 128 * col : 128 * col + 128]

    off = jnp.where(sc[0] == 0, 0, 8)
    for g in range(3):
        for tap in range(9):
            here = pl.ds(pl.multiple_of(off + CG * (9 * g + tap), 8), CG)
            w_ref[g, tap, :, :128] = o0[here, :].astype(BF16)
            w_ref[g, tap, :, 128:256] = o1[here, :].astype(BF16)
            w_ref[g, tap, :, 256:] = o2[here, :8].astype(BF16)


def unpack_weight(sizes, sc, plan, arrays, bnd):
    return pl.pallas_call(
        functools.partial(weight_body, sizes, plan),
        out_shape=jax.ShapeDtypeStruct((3, 9, CG, CG), BF16),
        in_specs=[SMEM] + [HBM] * len(plan) + [VMEM],
        out_specs=VMEM,
        scratch_shapes=[
            pltpu.VMEM((sizes.dl_num, 2, sizes.half, 128), BF16),
            pltpu.VMEM((sizes.flat, 128), F32),
            pltpu.VMEM((OROWS, 128), F32),
            pltpu.VMEM((OROWS, 128), F32),
            pltpu.VMEM((OROWS, 128), F32),
            pltpu.SemaphoreType.DMA((len(plan),)),
        ],
        compiler_params=params(),
        name="unpack_weight",
    )(sc, *arrays, bnd)


def forward_body(sc, x3_ref, cot_ref, w_ref, hid_ref, sums_ref):
    acc = jnp.zeros((256, CG), F32)
    for dx in range(3):
        for dy in range(3):
            x = x3_ref[0, dx, dy : dy + 8].reshape(256, CG)
            acc += jnp.dot(x, w_ref[0, 3 * dy + dx], preferred_element_type=F32)
    hid_ref[0] = acc
    active = (acc * jax.nn.sigmoid(acc)).astype(BF16).astype(F32)
    gate = active * cot_ref[0].astype(F32)
    act4 = active.reshape(8, 4, 8, CG)
    gate4 = gate.reshape(8, 4, 8, CG)
    sums_ref[0] = jnp.full((8, CG), sc[4].astype(F32), F32)
    for row, (value, slide) in enumerate(((act4, 0), (act4, 1), (gate4, 0), (gate4, 1))):
        part = value[:, 2 * slide] + value[:, 2 * slide + 1]
        sums_ref[0, row : row + 1, :] = jnp.sum(jnp.sum(part, axis=0), axis=0, keepdims=True)


def forward(sc, x3, cot, w):
    return pl.pallas_call(
        forward_body,
        grid=(3,),
        out_shape=(
            jax.ShapeDtypeStruct((3, 256, CG), F32),
            jax.ShapeDtypeStruct((3, 8, CG), F32),
        ),
        in_specs=[
            SMEM,
            pl.BlockSpec((1, 3, 10, 32, CG), lambda g: (g, 0, 0, 0, 0)),
            pl.BlockSpec((1, 256, CG), lambda g: (g, 0, 0)),
            pl.BlockSpec((1, 9, CG, CG), lambda g: (g, 0, 0, 0)),
        ],
        out_specs=(
            pl.BlockSpec((1, 256, CG), lambda g: (g, 0, 0)),
            pl.BlockSpec((1, 8, CG), lambda g: (g, 0, 0)),
        ),
        compiler_params=params(),
        name="forward_conv",
    )(sc, x3, cot, w)


def thirds(x):
    hi = x.astype(BF16).astype(F32)
    mid = (x - hi).astype(BF16).astype(F32)
    low = (x - hi - mid).astype(BF16).astype(F32)
    return hi, mid, low


def exact_dot(x, w, contract):
    parts = jnp.concatenate([*thirds(x), jnp.zeros((10, x.shape[1]), F32)], axis=0).astype(BF16)
    out = lax.dot_general(parts, w, (((1,), (contract,)), ((), ())), preferred_element_type=F32)
    return out[0:2] + out[2:4] + out[4:6]


def gate_body(sc, mine_ref, other_ref, sq_ref, ex_ref, gate_ref, fin_ref, wide):
    low = sc[0] == 0
    for g in range(3):
        a = mine_ref[g]
        b = other_ref[g]
        a = a[0:4]
        b = jnp.concatenate([b[1:2], b[0:1], b[3:4], b[2:3]], axis=0)
        wide[0:4, CG * g : CG * g + CG] = jnp.where(low, a, b)
        wide[0:4, HALF + CG * g : HALF + CG * g + CG] = jnp.where(low, b, a)
    counts = jnp.concatenate([mine_ref[0][4:5, 0:1], other_ref[0][4:5, 0:1]], axis=0)
    total = counts * 64.0
    pooled = wide[0:2, :] / total
    gate = wide[2:4, :]
    w_squeeze = sq_ref[...]
    w_excite = ex_ref[...]
    pre = exact_dot(pooled, w_squeeze, 0)
    sig = jax.nn.sigmoid(pre)
    squeezed = pre * sig
    excite = jax.nn.sigmoid(exact_dot(squeezed, w_excite, 0))
    excite_grad = gate * excite * (1.0 - excite)
    slope = sig * (1.0 + pre * (1.0 - sig))
    squeeze_grad = exact_dot(excite_grad, w_excite, 1) * slope
    pool = exact_dot(squeeze_grad, w_squeeze, 1) / total
    half_e = jnp.where(low, excite[:, :HALF], excite[:, HALF:])
    half_p = jnp.where(low, pool[:, :HALF], pool[:, HALF:])
    for g in range(3):
        gate_ref[g, 0:2, :] = half_e[:, CG * g : CG * g + CG]
        gate_ref[g, 2:4, :] = half_p[:, CG * g : CG * g + CG]

    def ordered(x):
        return jnp.where(low, x, jnp.concatenate([x[1:2], x[0:1]], axis=0))

    fin_ref[...] = jnp.zeros_like(fin_ref)
    fin_ref[:, 0:CH] = ordered(pooled)
    fin_ref[:, 1664 : 1664 + CH] = ordered(excite_grad)
    width = squeezed.shape[1]
    fin_ref[:, 3328 : 3328 + width] = ordered(squeezed)
    fin_ref[:, 3712 : 3712 + width] = ordered(squeeze_grad)


def gate_stage(sc, mine, other, w_squeeze, w_excite):
    return pl.pallas_call(
        gate_body,
        out_shape=(
            jax.ShapeDtypeStruct((3, 8, CG), F32),
            jax.ShapeDtypeStruct((2, 4096), F32),
        ),
        in_specs=[SMEM] + [VMEM] * 4,
        out_specs=(VMEM, VMEM),
        scratch_shapes=[pltpu.VMEM((8, CH), F32)],
        compiler_params=params(),
        name="gate_stage",
    )(sc, mine, other, w_squeeze, w_excite)


def outer_dot(a, b):
    ah, am, al = thirds(a)
    bh, bm, bl = thirds(b)
    left = jnp.concatenate([ah, ah, ah, am, am, al], axis=0).astype(BF16)
    right = jnp.concatenate([bh, bm, bl, bh, bm, bh], axis=0).astype(BF16)
    return lax.dot_general(left, right, (((0,), (0,)), ((), ())), preferred_element_type=F32)


def outer_body(width, fin_ref, sq_ref, ex_ref):
    pooled = fin_ref[:, 0:CH]
    excite_grad = fin_ref[:, 1664 : 1664 + CH]
    squeezed = fin_ref[:, 3328 : 3328 + width]
    squeeze_grad = fin_ref[:, 3712 : 3712 + width]
    sq_ref[...] = outer_dot(pooled, squeeze_grad)
    ex_ref[...] = outer_dot(squeezed, excite_grad)


def outer_stage(fin, width):
    return pl.pallas_call(
        functools.partial(outer_body, width),
        out_shape=(
            jax.ShapeDtypeStruct((CH, width), F32),
            jax.ShapeDtypeStruct((width, CH), F32),
        ),
        in_specs=[VMEM],
        out_specs=(VMEM, VMEM),
        compiler_params=params(),
        name="outer_stage",
    )(fin)


def output_body(hid_ref, x3_ref, gate_ref, own_ref, other_ref, wide):
    for g in range(3):
        gate = gate_ref[g]
        by_slide = jnp.concatenate(
            [jnp.broadcast_to(gate[s : s + 1], (16, CG)) for s in range(2)], axis=0
        )
        for i in range(8):
            hidden = hid_ref[g, 32 * i : 32 * i + 32, :]
            active = (hidden * jax.nn.sigmoid(hidden)).astype(BF16).astype(F32)
            value = x3_ref[g, 1, 1 + i].astype(F32) + active * by_slide
            for t in range(4):
                wide[t, 8 * i : 8 * i + 8, CG * g : CG * g + CG] = value[8 * t : 8 * t + 8]
    for t in range(4):
        (own_ref if t < 2 else other_ref)[t % 2] = wide[t].astype(BF16)


def output_stage(hidden, x3, gate):
    shape = jax.ShapeDtypeStruct((2, 64, HALF), BF16)
    return pl.pallas_call(
        output_body,
        out_shape=(shape, shape),
        in_specs=[VMEM] * 3,
        out_specs=(VMEM, VMEM),
        scratch_shapes=[pltpu.VMEM((4, 64, HALF), F32)],
        compiler_params=params(),
        name="output_stage",
    )(hidden, x3, gate)


def backward_body(sizes, sc, hid_ref, x3_ref, cot_ref, w_ref, gate_ref, keep_ref, send_ref, inner_ref, rim_ref,
                  o0, o1, o2, flat, pads, cols):
    g = pl.program_id(0)

    @pl.when(g == 0)
    def _():
        for ref in (o0, o1, o2):
            ref[0:8, :] = jnp.zeros((8, 128), F32)
            ref[TAPROWS:, :] = jnp.zeros((OROWS - TAPROWS, 128), F32)
        pads[...] = jnp.zeros_like(pads)

    hidden = hid_ref[0]
    gate = gate_ref[0]

    def spread(row):
        pair = [jnp.broadcast_to(gate[row + s : row + s + 1], (16, CG)) for s in range(2)]
        both = jnp.concatenate(pair, axis=0)
        return jnp.broadcast_to(both[None], (8, 32, CG)).reshape(256, CG)

    sig = jax.nn.sigmoid(hidden)
    slope = sig * (1.0 + hidden * (1.0 - sig))
    grad = ((cot_ref[0].astype(F32) * spread(0) + spread(2)) * slope).astype(BF16)
    off = jnp.where(sc[0] == 0, 0, 8) + g * (9 * CG)
    zeros = jnp.zeros((CG, 120), F32)
    for dx in range(3):
        for dy in range(3):
            tap = 3 * dy + dx
            x = x3_ref[0, dx, dy : dy + 8].reshape(256, CG)
            res = lax.dot_general(x, grad, (((0,), (0,)), ((), ())), preferred_element_type=F32)
            here = pl.ds(pl.multiple_of(off + CG * tap, 8), CG)
            o0[here, :] = res[:, :128]
            o1[here, :] = res[:, 128:256]
            o2[here, :] = jnp.concatenate([res[:, 256:], zeros], axis=1)
    for dx in range(3):
        cols[...] = jnp.zeros_like(cols)
        for dy in range(3):
            d = lax.dot_general(grad, w_ref[0, 3 * dy + dx], (((1,), (1,)), ((), ())), preferred_element_type=F32)
            cols[dy : dy + 8] += d.reshape(8, 32, CG)
        for value in range(3):
            @pl.when(g == value)
            def _():
                lanes = slice(CG * value, CG * value + CG)
                pads[:, :, dx : dx + 8, lanes] += cols[...].reshape(10, 4, 8, CG)

    @pl.when(g == 2)
    def _():
        for t in range(4):
            for i in range(8):
                inner_ref[t, 8 * i : 8 * i + 8, :] = pads[1 + i, t, 1:9, :]
            left = jnp.concatenate([pads[1 + i, t, 0:1, :] for i in range(8)], axis=0)
            right = jnp.concatenate([pads[1 + i, t, 9:10, :] for i in range(8)], axis=0)
            corners = [pads[0, t, 0:1, :], pads[0, t, 9:10, :], pads[9, t, 0:1, :], pads[9, t, 9:10, :]]
            parts = [pads[0, t, 1:9, :], left, right, pads[9, t, 1:9, :], *corners, jnp.zeros((4, HALF), F32)]
            rim_ref[t] = jnp.concatenate(parts, axis=0).astype(BF16)
        flat[: sizes.top, :] = jnp.zeros((sizes.top, 128), F32)
        base = jnp.where(sc[0] == 0, sizes.top, sizes.top - sizes.bound)

        @pl.loop(0, NCH)
        def _(ch):
            start = base + ch * (33 * PCH)
            carry = None
            for k in range(16):
                where = pl.ds(ch * (16 * PCH) + k, PCH, stride=16)
                x = jnp.concatenate([ref[where, :] for ref in (o0, o1, o2)], axis=1)
                if k:
                    x = pltpu.roll(x, 8 * k, axis=1)
                first = x[:, :128]
                if carry is not None:
                    first = first + carry
                flat[pl.ds(start + 2 * k, PCH, stride=33), :] = first
                flat[pl.ds(start + 2 * k + 1, PCH, stride=33), :] = x[:, 128:256]
                carry = x[:, 256:]
            flat[pl.ds(start + 32, PCH, stride=33), :] = carry

        even = sc[2] == 0
        quarter = sizes.quarter
        rest = sizes.piece - quarter
        for dl in range(sizes.dl_num):
            for q in range(2):
                start = sizes.top + sizes.rows * dl + q * quarter
                v0 = flat[start : start + quarter, :]
                v1 = flat[start + sizes.second : start + sizes.second + quarter, :]
                rel = jnp.bitwise_xor(sc[1], dl)
                part = jnp.bitwise_xor(sc[3], q)
                keep_ref[rel, part, 0:quarter] = jnp.where(even, v0, v1).astype(BF16)
                send_ref[rel, part, 0:quarter] = jnp.where(even, v1, v0).astype(BF16)
                if dl == sizes.dl_num - 1 and q == 1:
                    ext = jnp.concatenate([flat[: sizes.top, :], jnp.zeros((rest - sizes.top, 128), F32)], axis=0) \
                        if rest > sizes.top else flat[: sizes.top, :]
                    keep_ref[rel, part, quarter:] = jnp.where(even, 0.0, ext).astype(BF16)
                    send_ref[rel, part, quarter:] = jnp.where(even, ext, 0.0).astype(BF16)
                else:
                    keep_ref[rel, part, quarter:] = jnp.zeros((rest, 128), BF16)
                    send_ref[rel, part, quarter:] = jnp.zeros((rest, 128), BF16)


def backward(sizes, sc, hidden, x3, cot, w, gate):
    pieces = jax.ShapeDtypeStruct((sizes.dl_num, 2, sizes.piece, 128), BF16)
    return pl.pallas_call(
        functools.partial(backward_body, sizes),
        grid=(3,),
        out_shape=(
            pieces,
            pieces,
            jax.ShapeDtypeStruct((4, 64, HALF), F32),
            jax.ShapeDtypeStruct((4, 40, HALF), BF16),
        ),
        in_specs=[
            SMEM,
            pl.BlockSpec((1, 256, CG), lambda g: (g, 0, 0)),
            pl.BlockSpec((1, 3, 10, 32, CG), lambda g: (g, 0, 0, 0, 0)),
            pl.BlockSpec((1, 256, CG), lambda g: (g, 0, 0)),
            pl.BlockSpec((1, 9, CG, CG), lambda g: (g, 0, 0, 0)),
            pl.BlockSpec((1, 8, CG), lambda g: (g, 0, 0)),
        ],
        out_specs=(VMEM, VMEM, VMEM, VMEM),
        scratch_shapes=[
            pltpu.VMEM((OROWS, 128), F32),
            pltpu.VMEM((OROWS, 128), F32),
            pltpu.VMEM((OROWS, 128), F32),
            pltpu.VMEM((sizes.flat, 128), F32),
            pltpu.VMEM((10, 4, 16, HALF), F32),
            pltpu.VMEM((10, 32, CG), F32),
        ],
        compiler_params=params(),
        name="backward_conv",
    )(sc, hidden, x3, cot, w, gate)


def rims_body(sc, ids, own_ref, other_ref, inner_ref, r0, r1, r2, r3, out0_ref, out1_ref, edges, corners):
    edges[...] = jnp.zeros_like(edges)
    corners[...] = jnp.zeros_like(corners)
    for rel, ref in enumerate((r0, r1, r2, r3)):
        dev = jnp.bitwise_xor(sc[5], rel)
        for slide in range(2):
            for slot in range(2):
                t = 2 * slide + slot
                rim = ref[t].astype(F32)
                for mine in range(2):
                    own = 2 * sc[5] + mine
                    n = 2 * slide + mine

                    def hit(offset):
                        return jnp.where(ids[dev, t, offset] == own, 1.0, 0.0)

                    for member, offset in enumerate((1, 3, 4, 6)):
                        edges[n, member] += hit(offset) * rim[8 * member : 8 * member + 8]
                    for member, offset in enumerate((0, 2, 5, 7)):
                        row = 32 + member
                        corners[n, member : member + 1] += hit(offset) * rim[row : row + 1]
    for n in range(4):
        cot = (own_ref if n < 2 else other_ref)[n % 2].astype(F32)
        inner_ref_n = inner_ref[n] + cot
        last_col = edges[n, 1]
        first_col = edges[n, 2]
        rows = []
        for i in range(8):
            row = inner_ref_n[8 * i : 8 * i + 8]
            lo = first_col[i : i + 1]
            hi = last_col[i : i + 1]
            if i == 0:
                row = row + edges[n, 3]
                hi = hi + corners[n, 2:3]
                lo = lo + corners[n, 3:4]
            if i == 7:
                row = row + edges[n, 0]
                hi = hi + corners[n, 0:1]
                lo = lo + corners[n, 1:2]
            pos = lax.broadcasted_iota(jnp.int32, (8, HALF), 0)
            row = row + jnp.where(pos == 0, lo, 0.0) + jnp.where(pos == 7, hi, 0.0)
            rows.append(row)
        (out0_ref if n < 2 else out1_ref)[n % 2] = jnp.concatenate(rows, axis=0).astype(BF16)


def add_rims(sc, ids, own, other, inner, rims):
    shape = jax.ShapeDtypeStruct((2, 64, HALF), BF16)
    return pl.pallas_call(
        rims_body,
        out_shape=(shape, shape),
        in_specs=[SMEM, SMEM] + [VMEM] * 7,
        out_specs=(VMEM, VMEM),
        scratch_shapes=[
            pltpu.VMEM((4, 4, 8, HALF), F32),
            pltpu.VMEM((4, 8, HALF), F32),
        ],
        compiler_params=params(),
        name="add_rims",
    )(sc, ids, own, other, inner, *rims)


def rows_body(sizes, sc, p0, p1, p2, p3, out_ref, land):
    for rel, ref in enumerate((p0, p1, p2, p3)):
        c = jnp.bitwise_xor(sc[2], rel & 1)
        q = jnp.bitwise_xor(sc[3], rel >> 1)
        land[c, q] = ref[...]
    for c in range(2):
        for q in range(2):
            start = c * sizes.second + q * sizes.quarter
            out_ref[start : start + sizes.quarter, :] = land[c, q].astype(F32)


def place_rows(sizes, sc, parts):
    return pl.pallas_call(
        functools.partial(rows_body, sizes),
        out_shape=jax.ShapeDtypeStruct((sizes.rows, 128), F32),
        in_specs=[SMEM] + [VMEM] * 4,
        out_specs=VMEM,
        scratch_shapes=[pltpu.VMEM((2, 2, sizes.quarter, 128), BF16)],
        compiler_params=params(),
        name="place_rows",
    )(sc, *parts)


def tile_ring(value):
    near = swap(value, "t1")
    far = swap(value, "t0")
    return value, near, far, swap(far, "t1")


def reduce_chunk(value, axes, order):
    current = value.astype(F32)
    names = list(axes)
    for name in order:
        pos = names.index(name)
        send = lax.index_in_dim(current, 1, pos, keepdims=False).astype(BF16)
        stay = lax.index_in_dim(current, 0, pos, keepdims=False)
        current = stay + swap(send, name).astype(F32)
        names.pop(pos)
    return current


def shards(dbits, features, cotangent, conv_weight, squeeze_weight, excite_weight, live_count, neighbours):
    lows = tuple(f"d{i}" for i in range(1, dbits))
    dl_num = 2 ** (dbits - 1)
    sizes = Sizes(conv_weight.shape[0], dl_num)
    dh = lax.axis_index("d0")
    dl = lax.axis_index(lows)
    y = lax.axis_index("t0")
    c = lax.axis_index("t1")
    count = live_count[0, 0]
    sc = jnp.stack([dh, dl, c, y, count, 2 * y + c, count, count]).astype(jnp.int32)

    feat_own, feat_send = split_halves(sc, features.reshape(128, CH))
    feat_other = swap(feat_send, "d0")
    half0 = conv_weight[: sizes.half]
    half1 = conv_weight[sizes.second :]
    bnd = swap(conv_weight[sizes.rows - sizes.top :], "d0")
    if len(lows) == 2:
        mine = jnp.where(c == 0, half0, half1)
        a1 = swap(mine, "d1")
        a2 = swap(mine, "d2")
        b12 = swap(a1[: sizes.quarter], "d2")
        b21 = swap(a2[sizes.quarter :], "d1")
        e1, e2 = swap(a1, "t1"), swap(a2, "t1")
        e12, e21 = swap(b12, "t1"), swap(b21, "t1")
        arrays = [half0, half1, a1, a2, b12, b21, e1, e2, e12, e21]
        plan = [(0, 0), (0, 1), (2, (None, 0)), (1, (None, 0)), (3, (0, 0)), (3, (1, 0)),
                (2, (None, 1)), (1, (None, 1)), (3, (0, 1)), (3, (1, 1))]
        bit1, bit2 = lax.axis_index("d1"), lax.axis_index("d2")
        bnd = jnp.where(bit2 == 1, bnd, swap(bnd, "d2"))
        bnd = jnp.where(bit1 == 1, bnd, swap(bnd, "d1"))
    else:
        arrays = [lax.all_gather(half0, lows), lax.all_gather(half1, lows)]
        plan = [(None, 0), (None, 1)]
        bnd = lax.all_gather(bnd, lows)[-1]

    ids_own = neighbours[0]
    ids4 = jnp.concatenate([ids_own, swap(ids_own, "d0")], axis=0)
    ids_all = lax.all_gather(ids4, ("t0", "t1"))
    cot_own, cot_send = split_halves(sc, cotangent.reshape(128, CH))
    cot_other = swap(cot_send, "d0")
    strips = tile_ring(make_strips(feat_own, feat_other))
    x3 = pad_tiles(sc, ids4, feat_own, feat_other, strips)
    cot = regroup(cot_own, cot_other)
    w = unpack_weight(sizes, sc, plan, arrays, bnd)
    hidden, sums = forward(sc, x3, cot, w)
    sums = sums + swap(sums, "t1")
    sums = sums + swap(sums, "t0")
    gate, fin = gate_stage(sc, sums, swap(sums, "d0"), squeeze_weight, excite_weight)

    keep, send, inner, rims = backward(sizes, sc, hidden, x3, cot, w, gate)

    total = keep.astype(F32) + swap(send, "t1").astype(F32)
    axes = lows + ("t0",)
    total = total.reshape((2,) * len(axes) + (sizes.piece, 128))
    chunk = sizes.piece // 3
    done = []
    for part in range(3):
        turn = (len(axes) - 1 + part) % len(axes)
        order = axes[turn:] + axes[:turn]
        done.append(reduce_chunk(total[..., part * chunk : (part + 1) * chunk, :], axes, order))
    summed = jnp.concatenate(done, axis=0)
    ext = summed[sizes.quarter : sizes.quarter + sizes.top].astype(BF16)
    ext = jnp.where(dh == 0, swap(ext, "d0").astype(F32), 0.0)
    body = summed[: sizes.quarter]
    body = body.at[sizes.quarter - sizes.top :].add(ext).astype(BF16)
    grad_conv = place_rows(sizes, sc, tile_ring(body))

    back_own, back_send = add_rims(sc, ids_all, cot_own, cot_other, inner, tile_ring(rims))
    grad_in = join_halves(sc, back_own, swap(back_send, "d0"))

    out_own, out_send = output_stage(hidden, x3, gate)
    output = join_halves(sc, out_own, swap(out_send, "d0"))

    for name in reversed(lows):
        got = swap(fin, name)
        first = lax.axis_index(name) == 0
        fin = jnp.concatenate([jnp.where(first, fin, got), jnp.where(first, got, fin)], axis=0)
    grad_squeeze, grad_excite = outer_stage(fin, squeeze_weight.shape[1])
    shape = features.shape
    return (output.reshape(shape), grad_in.reshape(shape), grad_conv, grad_squeeze, grad_excite)


def solution(mesh):
    dbits = mesh.shape["dp"].bit_length() - 1
    dnames = tuple(f"d{i}" for i in range(dbits))
    tnames = ("t0", "t1")
    fine = Mesh(mesh.devices.reshape((2,) * (dbits + 2)), dnames + tnames)
    return jax.shard_map(
        functools.partial(shards, dbits),
        mesh=fine,
        in_specs=(
            P(dnames, tnames, None, None, None),
            P(dnames, tnames, None, None, None),
            P(dnames, None),
            P(),
            P(),
            P(dnames, tnames),
            P(dnames, tnames, None),
        ),
        out_specs=(
            P(dnames, tnames, None, None, None),
            P(dnames, tnames, None, None, None),
            P(dnames, None),
            P(),
            P(),
        ),
        check_vma=False,
    )
```

time: 811 us -> 196 us (0.24)
  blocking collectives: 335 us -> 5.38 us
  local copies, waits for them, and re-layouts: 244 us -> 13.7 us
  Pallas kernels: 0 us -> 70.6 us
  waiting for transfers between devices: 115 us -> 64.4 us
  matrix products: 46.9 us -> 0 us
  other arithmetic: 43.1 us -> 7.62 us
  starting transfers between devices: 1.86 us -> 32.2 us
  between operations: 18.2 us -> 1.74 us
    unnamed x1 -> x0, blocking collectives: 294 us -> none
    pallas_call x0 -> x15, Pallas kernels: none -> 70.6 us  [the longest x1 18.7 us: backward(): pl.pallas_call(functools.partial(backward_body, sizes), grid=(3,), out_sh...]
    unnamed x5 -> x0, waiting for transfers between devices: 68.3 us -> none
    ppermute x0 -> x41, waiting for transfers between devices: none -> 64.4 us  [swap(): return lax.ppermute(value, axis, SWAP)]
    reshape x5 -> x0, local copies, waits for them, and re-layouts: 59.5 us -> none  [the longest x1 22.8 us: shards(): flat_grad = grad_w.reshape(-1)]
    scatter-add x14 -> x0, local copies, waits for them, and re-layouts: 57.8 us -> none  [the longest x7 48.9 us: fold_back(): grad_pad.at[:, row_off:row_off + edge_len, col_off:col_off + edge_len]]
    another operation x26 -> x1, local copies, waits for them, and re-layouts: 48.6 us -> 0.63 us  [shards(): jnp.stack([dh, dl, c, y, count, 2 * y + c, count, count]).astype(jnp.int32)]
    dot_general x17 -> x0, matrix products: 46.9 us -> none  [the longest x1 13.3 us: conv_backward(): jnp.einsum('rkgi,rgo->gkio', patches.reshape(patches.shape[0], 9, GROUPS,...]
  transfers between devices with their start and end apart: 4 -> 41, of which waited for: 3 -> 16; matrix products, arithmetic and copies ran while one was open for 14% -> 6% of each run, Pallas kernels for 0% -> 13%
where the time goes in v1:
time: 196 us
  Pallas kernels  70.6 us (36%)
  waiting for transfers between devices  64.4 us (33%)
  starting transfers between devices  32.2 us (16%)
  local copies, waits for them, and re-layouts  13.7 us (7%)
  other arithmetic  7.62 us (4%)
  blocking collectives  5.38 us (3%)
    ppermute x41, waiting for transfers between devices, swap(): return lax.ppermute(value, axis, SWAP)  64.4 us
    ppermute x41, starting transfers between devices, swap(): return lax.ppermute(value, axis, SWAP)  32.2 us
    pallas_call x1, Pallas kernels, backward(): pl.pallas_call(functools.partial(backward_body, sizes), grid=(3,), out_sh...  18.7 us
    unnamed x60, local copies, waits for them, and re-layouts  12.1 us
    pallas_call x1, Pallas kernels, unpack_weight(): pl.pallas_call(functools.partial(weight_body, sizes, plan), out_shape=jax...  11.6 us
    pallas_call x1, Pallas kernels, forward(): pl.pallas_call(forward_body, grid=(3,), out_shape=(jax.ShapeDtypeStruct((...  7.23 us
    all_gather x1, blocking collectives, shards(): ids_all = lax.all_gather(ids4, ('t0', 't1'))  5.38 us
    pallas_call x2, Pallas kernels, split_halves(): pl.pallas_call(split_body, out_shape=(shape, shape), in_specs=[SMEM, VMEM...  4.14 us
  transfers between devices with their start and end apart: 41, of which 16 were waited for; matrix products, arithmetic and copies ran while one was open for 6% of the time, Pallas kernels for 13%

profile of v1, /device:TPU:0, one launch (start us, length us, event | category | flops | bytes accessed | tf_op | source)
XLA Modules:
  0.0 195.6 jit_solution(15251101527333528479)
XLA Ops:
  2.8 2.9 %collective-permute-start.7 = (bf16[1856,128]{1,0:T(8,128)(2,1)S(1)}, bf16[1856,128]{1,0:T(8,128)(2,1)S(1)}, u32[]{:S(2)}, u32[]{:S(2)}) collective-permute-start(bf16[1856,128]{1,0:T(8,128)(2,1)S(1)} %get-tuple-element.71), channel_id=1, source_target_pairs={{0,4},{4,0},{1,5},{5,1},{2,6},{6,2},{3,7},{7,3},{8,12},{12,8},{9,1... | collective-permute-start | bytes 1425416 | tf_op jit(solution)/shard_map/ppermute | solution.py:31
  14.3 8.0 %collective-permute-done.14 = bf16[32,128]{1,0:T(8,128)(2,1)S(1)} collective-permute-done((bf16[32,128]{1,0:T(8,128)(2,1)S(1)}, bf16[32,128]{1,0:T(8,128)(2,1)S(1)}, u32[]{:S(2)}, u32[]{:S(2)}) %collective-permute-start.14) | collective-permute-done | bytes 8224 | tf_op jit(solution)/shard_map/ppermute | solution.py:31
  22.8 3.4 %collective-permute-start = (s32[2,8]{1,0:T(2,128)S(1)}, s32[2,8]{1,0:T(2,128)S(1)}, u32[]{:S(2)}, u32[]{:S(2)}) collective-permute-start(s32[2,8]{1,0:T(2,128)S(1)} %bitcast.83), channel_id=1, source_target_pairs={{0,16},{16,0},{1,17},{17,1},{2,18},{18,2},{3,19},{19,3},{4,20},{20... | collective-permute-start | bytes 200 | tf_op jit(solution)/shard_map/ppermute | solution.py:31
  36.6 6.7 %collective-permute-done.16 = bf16[32,128]{1,0:T(8,128)(2,1)S(1)} collective-permute-done((bf16[32,128]{1,0:T(8,128)(2,1)S(1)}, bf16[32,128]{1,0:T(8,128)(2,1)S(1)}, u32[]{:S(2)}, u32[]{:S(2)}) %collective-permute-start.16) | collective-permute-done | bytes 8224 | tf_op jit(solution)/shard_map/ppermute | solution.py:31
  49.7 3.8 %pad_tiles.1.x3_ref = bf16[3,3,10,32,264]{4,3,2,1,0:T(8,128)(2,1)} custom-call(s32[8]{0:T(128)} %stack.23.sc, s32[4,8]{1,0:T(4,128)} %get-tuple-element.79.ids, bf16[2,64,792]{2,1,0:T(8,128)(2,1)} %get-tuple-element.35.own_ref, bf16[2,64,792]{2,1,0:T(8,128)(2,1)} %copy-done.5, bf16[4,32,792]{2,1,0:T(8,128)(2,1)} %make_strips.1.s0, ...), custom_call_target="tpu_custom_call" | custom-call | tf_op jit(solution)/shard_map/pad_tiles/pallas_call | solution.py:150
  54.7 11.6 %unpack_weight.1.w_ref = bf16[3,9,264,264]{3,2,1,0:T(8,128)(2,1)} custom-call(s32[8]{0:T(128)} %stack.23.sc, bf16[1856,128]{1,0:T(8,128)(2,1)} %get-tuple-element.72.refs_0_, bf16[1856,128]{1,0:T(8,128)(2,1)} %get-tuple-element.73.refs_1_, bf16[1856,128]{1,0:T(8,128)(2,1)} %copy-done.3, bf16[1856,128]{1,0:T(8,128)(2,1)} %copy-done.2, ...), custom_call_target="tpu_custom_call" | custom-call | tf_op jit(solution)/shard_map/unpack_weight/pallas_call | solution.py:230
  66.3 7.2 %forward_conv.1 = (f32[3,256,264]{2,1,0:T(8,128)}, f32[3,8,264]{2,1,0:T(8,128)}) custom-call(s32[8]{0:T(128)} %stack.23.sc, bf16[3,3,10,32,264]{4,3,2,1,0:T(8,128)(2,1)} %pad_tiles.1.x3_ref, bf16[3,256,264]{2,1,0:T(8,128)(2,1)} %regroup.1.cot_ref, bf16[3,9,264,264]{3,2,1,0:T(8,128)(2,1)} %unpack_weight.1.w_ref), custom_call_target="tpu_custom_call" | custom-call | tf_op jit(solution)/shard_map/forward_conv/pallas_call | solution.py:266
  76.3 3.4 %collective-permute-done.18 = f32[3,8,264]{2,1,0:T(8,128)S(1)} collective-permute-done((f32[3,8,264]{2,1,0:T(8,128)S(1)}, f32[3,8,264]{2,1,0:T(8,128)S(1)}, u32[]{:S(2)}, u32[]{:S(2)}) %collective-permute-start.18) | collective-permute-done | bytes 25376 | tf_op jit(solution)/shard_map/ppermute | solution.py:31
  85.3 4.1 %gate_stage.1 = (f32[3,8,264]{2,1,0:T(8,128)}, f32[2,4096]{1,0:T(2,128)}) custom-call(s32[8]{0:T(128)} %stack.23.sc, f32[3,8,264]{2,1,0:T(8,128)} %copy-done.24, f32[3,8,264]{2,1,0:T(8,128)} %copy-done.25, bf16[1584,363]{1,0:T(8,128)(2,1)} %sq_ref.1, bf16[363,1584]{1,0:T(8,128)(2,1)} %copy.23.ex_ref), custom_call_target="tpu_custom_call" | custom-call | tf_op jit(solution)/shard_map/gate_stage/pallas_call | solution.py:342
  89.4 18.7 %backward_conv.1 = (bf16[4,2,960,128]{3,2,1,0:T(8,128)(2,1)}, bf16[4,2,960,128]{3,2,1,0:T(8,128)(2,1)}, f32[4,64,792]{2,1,0:T(8,128)}, bf16[4,40,792]{2,1,0:T(8,128)(2,1)}) custom-call(s32[8]{0:T(128)} %stack.23.sc, f32[3,256,264]{2,1,0:T(8,128)} %get-tuple-element.39.hid_ref, bf16[3,3,10,32,264]{4,3,2,1,0:T(8,128)(2,1)} %pad_tiles.1.x3_ref, ...), custom_call_target="tpu_custom_call" | custom-call | tf_op jit(solution)/shard_map/backward_conv/pallas_call | solution.py:514
  109.7 5.4 %all-gather.1.ids = s32[4,4,8]{2,1,0:T(4,128)} all-gather(s32[1,4,8]{2,1,0:T(4,128)S(1)} %get-tuple-element.78), channel_id=2, replica_groups=mesh['d0'=2,'d1'=2,'d2'=2,'t0'=2,'t1'=2] {'t0','t1'}, dimensions={0}, use_global_device_ids=true | all-gather | bytes 640 | tf_op jit(solution)/shard_map/all_gather | solution.py:684
  115.1 3.1 %output_stage.1 = (bf16[2,64,792]{2,1,0:T(8,128)(2,1)}, bf16[2,64,792]{2,1,0:T(8,128)(2,1)}) custom-call(f32[3,256,264]{2,1,0:T(8,128)} %get-tuple-element.39.hid_ref, bf16[3,3,10,32,264]{4,3,2,1,0:T(8,128)(2,1)} %pad_tiles.1.x3_ref, f32[3,8,264]{2,1,0:T(8,128)} %get-tuple-element.41.gate_ref), custom_call_target="tpu_custom_call" | custom-call | tf_op jit(solution)/shard_map/output_stage/pallas_call | solution.py:405
  123.3 4.5 %collective-permute-done.22.r2 = bf16[4,40,792]{2,1,0:T(8,128)(2,1)S(1)} collective-permute-done((bf16[4,40,792]{2,1,0:T(8,128)(2,1)S(1)}, bf16[4,40,792]{2,1,0:T(8,128)(2,1)S(1)}, u32[]{:S(2)}, u32[]{:S(2)}) %collective-permute-start.22) | collective-permute-done | bytes 253472 | tf_op jit(solution)/shard_map/ppermute | solution.py:31
  128.2 6.1 %collective-permute-done.26 = bf16[2,2,320,128]{3,2,1,0:T(8,128)(2,1)S(1)} collective-permute-done((bf16[2,2,320,128]{3,2,1,0:T(8,128)(2,1)S(1)}, bf16[2,2,320,128]{3,2,1,0:T(8,128)(2,1)S(1)}, u32[]{:S(2)}, u32[]{:S(2)}) %collective-permute-start.26) | collective-permute-done | bytes 327712 | tf_op jit(solution)/shard_map/ppermute | solution.py:31
  136.3 6.1 %collective-permute-done.30 = bf16[2,320,128]{2,1,0:T(8,128)(2,1)S(1)} collective-permute-done((bf16[2,320,128]{2,1,0:T(8,128)(2,1)S(1)}, bf16[2,320,128]{2,1,0:T(8,128)(2,1)S(1)}, u32[]{:S(2)}, u32[]{:S(2)}) %collective-permute-start.30) | collective-permute-done | bytes 163872 | tf_op jit(solution)/shard_map/ppermute | solution.py:31
  142.9 5.3 %collective-permute-done.33 = bf16[2,320,128]{2,1,0:T(8,128)(2,1)S(1)} collective-permute-done((bf16[2,320,128]{2,1,0:T(8,128)(2,1)S(1)}, bf16[2,320,128]{2,1,0:T(8,128)(2,1)S(1)}, u32[]{:S(2)}, u32[]{:S(2)}) %collective-permute-start.33) | collective-permute-done | bytes 163872 | tf_op jit(solution)/shard_map/ppermute | solution.py:31
  149.2 4.3 %collective-permute-done.27 = bf16[2,320,128]{2,1,0:T(8,128)(2,1)S(1)} collective-permute-done((bf16[2,320,128]{2,1,0:T(8,128)(2,1)S(1)}, bf16[2,320,128]{2,1,0:T(8,128)(2,1)S(1)}, u32[]{:S(2)}, u32[]{:S(2)}) %collective-permute-start.27) | collective-permute-done | bytes 163872 | tf_op jit(solution)/shard_map/ppermute | solution.py:31
  154.5 3.5 %collective-permute-done.34 = bf16[320,128]{1,0:T(8,128)(2,1)S(1)} collective-permute-done((bf16[320,128]{1,0:T(8,128)(2,1)S(1)}, bf16[320,128]{1,0:T(8,128)(2,1)S(1)}, u32[]{:S(2)}, u32[]{:S(2)}) %collective-permute-start.34) | collective-permute-done | bytes 81952 | tf_op jit(solution)/shard_map/ppermute | solution.py:31
  158.5 3.9 %collective-permute-done.31 = bf16[320,128]{1,0:T(8,128)(2,1)S(1)} collective-permute-done((bf16[320,128]{1,0:T(8,128)(2,1)S(1)}, bf16[320,128]{1,0:T(8,128)(2,1)S(1)}, u32[]{:S(2)}, u32[]{:S(2)}) %collective-permute-start.31) | collective-permute-done | bytes 81952 | tf_op jit(solution)/shard_map/ppermute | solution.py:31
  162.9 3.9 %collective-permute-done.28 = bf16[320,128]{1,0:T(8,128)(2,1)S(1)} collective-permute-done((bf16[320,128]{1,0:T(8,128)(2,1)S(1)}, bf16[320,128]{1,0:T(8,128)(2,1)S(1)}, u32[]{:S(2)}, u32[]{:S(2)}) %collective-permute-start.28) | collective-permute-done | bytes 81952 | tf_op jit(solution)/shard_map/ppermute | solution.py:31
  168.5 2.9 %collective-permute-done.35 = bf16[32,128]{1,0:T(8,128)(2,1)S(1)} collective-permute-done((bf16[32,128]{1,0:T(8,128)(2,1)S(1)}, bf16[32,128]{1,0:T(8,128)(2,1)S(1)}, u32[]{:S(2)}, u32[]{:S(2)}) %collective-permute-start.35) | collective-permute-done | bytes 8224 | tf_op jit(solution)/shard_map/ppermute | solution.py:31
  172.8 3.4 %add_rims.1 = (bf16[2,64,792]{2,1,0:T(8,128)(2,1)}, bf16[2,64,792]{2,1,0:T(8,128)(2,1)}) custom-call(s32[8]{0:T(128)} %stack.23.sc, s32[4,4,8]{2,1,0:T(4,128)} %all-gather.1.ids, bf16[2,64,792]{2,1,0:T(8,128)(2,1)} %get-tuple-element.37.own_ref, bf16[2,64,792]{2,1,0:T(8,128)(2,1)} %copy-done.6, f32[4,64,792]{2,1,0:T(8,128)} %get-tuple-element.44.inner_ref, ...), custom_call_target="tpu_custom_call" | custom-call | tf_op jit(solution)/shard_map/add_rims/pallas_call | solution.py:592
  179.1 3.8 %outer_stage.1 = (f32[1584,363]{1,0:T(8,128)}, f32[363,1584]{1,0:T(8,128)}) custom-call(f32[8,4096]{1,0:T(8,128)} %pad_maximum_fusion.2.fin_ref), custom_call_target="tpu_custom_call" | custom-call | tf_op jit(solution)/shard_map/outer_stage/pallas_call | solution.py:374
  182.8 3.2 %copy.27 = f32[363,1584]{0,1:T(8,128)} copy(f32[363,1584]{1,0:T(8,128)} %get-tuple-element.67) | data formatting | bytes 4599936
  (169 shorter events, 64.6 us)
Async XLA Ops:
  2.8 28.1 %collective-permute-start.7 = (bf16[1856,128]{1,0:T(8,128)(2,1)S(1)}, bf16[1856,128]{1,0:T(8,128)(2,1)S(1)}, u32[]{:S(2)}, u32[]{:S(2)}) collective-permute-start(bf16[1856,128]{1,0:T(8,128)(2,1)S(1)} %get-tuple-element.71), channel_id=1, source_target_pairs={{0,4},{4,0},{1,5},{5,1},{2,6},{6,2},{3,7},{7,3},{8,12},{12,8},{9,1... | collective-permute-start | bytes 1425416 | tf_op jit(solution)/shard_map/ppermute | solution.py:31
  5.8 26.7 %collective-permute-start.6 = (bf16[1856,128]{1,0:T(8,128)(2,1)S(1)}, bf16[1856,128]{1,0:T(8,128)(2,1)S(1)}, u32[]{:S(2)}, u32[]{:S(2)}) collective-permute-start(bf16[1856,128]{1,0:T(8,128)(2,1)S(1)} %get-tuple-element.71), channel_id=1, source_target_pairs={{0,8},{8,0},{1,9},{9,1},{2,10},{10,2},{3,11},{11,3},{4,12},{12,4},... | collective-permute-start | bytes 1425416 | tf_op jit(solution)/shard_map/ppermute | solution.py:31
  10.7 17.6 %collective-permute-start.1 = (bf16[2,64,792]{2,1,0:T(8,128)(2,1)}, bf16[2,64,792]{2,1,0:T(8,128)(2,1)S(1)}, u32[]{:S(2)}, u32[]{:S(2)}) collective-permute-start(bf16[2,64,792]{2,1,0:T(8,128)(2,1)} %get-tuple-element.36), channel_id=1, source_target_pairs={{0,16},{16,0},{1,17},{17,1},{2,18},{18,2},{3,19},{19,3},{4,20},{20... | collective-permute-start | bytes 608264 | tf_op jit(solution)/shard_map/ppermute | solution.py:31
  22.3 12.6 %collective-permute-start.15 = (bf16[32,128]{1,0:T(8,128)(2,1)S(1)}, bf16[32,128]{1,0:T(8,128)(2,1)S(1)}, u32[]{:S(2)}, u32[]{:S(2)}) collective-permute-start(bf16[32,128]{1,0:T(8,128)(2,1)S(1)} %collective-permute-done.14), channel_id=1, source_target_pairs={{0,4},{4,0},{1,5},{5,1},{2,6},{6,2},{3,7},{7,3},{8,12},{12,8},{9,1... | collective-permute-start | bytes 24584 | tf_op jit(solution)/shard_map/ppermute | solution.py:31
  22.8 13.7 %collective-permute-start = (s32[2,8]{1,0:T(2,128)S(1)}, s32[2,8]{1,0:T(2,128)S(1)}, u32[]{:S(2)}, u32[]{:S(2)}) collective-permute-start(s32[2,8]{1,0:T(2,128)S(1)} %bitcast.83), channel_id=1, source_target_pairs={{0,16},{16,0},{1,17},{17,1},{2,18},{18,2},{3,19},{19,3},{4,20},{20... | collective-permute-start | bytes 200 | tf_op jit(solution)/shard_map/ppermute | solution.py:31
  28.3 15.1 %collective-permute-start.5 = (bf16[2,64,792]{2,1,0:T(8,128)(2,1)}, bf16[2,64,792]{2,1,0:T(8,128)(2,1)S(1)}, u32[]{:S(2)}, u32[]{:S(2)}) collective-permute-start(bf16[2,64,792]{2,1,0:T(8,128)(2,1)} %get-tuple-element.38), channel_id=1, source_target_pairs={{0,16},{16,0},{1,17},{17,1},{2,18},{18,2},{3,19},{19,3},{4,20},{20... | collective-permute-start | bytes 608264 | tf_op jit(solution)/shard_map/ppermute | solution.py:31
  30.9 12.9 %collective-permute-start.3 = (bf16[4,32,792]{2,1,0:T(8,128)(2,1)}, bf16[4,32,792]{2,1,0:T(8,128)(2,1)S(1)}, u32[]{:S(2)}, u32[]{:S(2)}) collective-permute-start(bf16[4,32,792]{2,1,0:T(8,128)(2,1)} %make_strips.1.s0), channel_id=1, source_target_pairs={{0,2},{2,0},{1,3},{3,1},{4,6},{6,4},{5,7},{7,5},{8,10},{10,8},{9,1... | collective-permute-start | bytes 608264 | tf_op jit(solution)/shard_map/ppermute | solution.py:31
  32.5 11.5 %collective-permute-start.9 = (bf16[928,128]{1,0:T(8,128)(2,1)S(1)}, bf16[928,128]{1,0:T(8,128)(2,1)S(1)}, u32[]{:S(2)}, u32[]{:S(2)}) collective-permute-start(bf16[928,128]{1,0:T(8,128)(2,1)S(1)} %slice.142), channel_id=1, source_target_pairs={{0,8},{8,0},{1,9},{9,1},{2,10},{10,2},{3,11},{11,3},{4,12},{12,4},... | collective-permute-start | bytes 712712 | tf_op jit(solution)/shard_map/ppermute | solution.py:31
  43.3 10.2 %collective-permute-start.11 = (bf16[1856,128]{1,0:T(8,128)(2,1)S(1)}, bf16[1856,128]{1,0:T(8,128)(2,1)S(1)}, u32[]{:S(2)}, u32[]{:S(2)}) collective-permute-start(bf16[1856,128]{1,0:T(8,128)(2,1)S(1)} %collective-permute-done.7.refs_3_), channel_id=1, source_target_pairs={{0,1},{1,0},{2,3},{3,2},{4,5},{5,4},{6,7},{7,6},{8,9},{9,8},{10,11... | collective-permute-start | bytes 1425416 | tf_op jit(solution)/shard_map/ppermute | solution.py:31
  43.4 10.2 %collective-permute-start.10 = (bf16[1856,128]{1,0:T(8,128)(2,1)S(1)}, bf16[1856,128]{1,0:T(8,128)(2,1)S(1)}, u32[]{:S(2)}, u32[]{:S(2)}) collective-permute-start(bf16[1856,128]{1,0:T(8,128)(2,1)S(1)} %collective-permute-done.6.refs_2_), channel_id=1, source_target_pairs={{0,1},{1,0},{2,3},{3,2},{4,5},{5,4},{6,7},{7,6},{8,9},{9,8},{10,11... | collective-permute-start | bytes 1425416 | tf_op jit(solution)/shard_map/ppermute | solution.py:31
  44.0 9.6 %collective-permute-start.13 = (bf16[928,128]{1,0:T(8,128)(2,1)S(1)}, bf16[928,128]{1,0:T(8,128)(2,1)S(1)}, u32[]{:S(2)}, u32[]{:S(2)}) collective-permute-start(bf16[928,128]{1,0:T(8,128)(2,1)S(1)} %collective-permute-done.9.refs_5_), channel_id=1, source_target_pairs={{0,1},{1,0},{2,3},{3,2},{4,5},{5,4},{6,7},{7,6},{8,9},{9,8},{10,11... | collective-permute-start | bytes 712712 | tf_op jit(solution)/shard_map/ppermute | solution.py:31
  108.1 10.7 %collective-permute-start.25 = (bf16[4,2,960,128]{3,2,1,0:T(8,128)(2,1)}, bf16[4,2,960,128]{3,2,1,0:T(8,128)(2,1)}, u32[]{:S(2)}, u32[]{:S(2)}) collective-permute-start(bf16[4,2,960,128]{3,2,1,0:T(8,128)(2,1)} %get-tuple-element.49), channel_id=1, source_target_pairs={{0,1},{1,0},{2,3},{3,2},{4,5},{5,4},{6,7},{7,6},{8,9},{9,8},{10,11... | collective-permute-start | bytes 5898248 | tf_op jit(solution)/shard_map/ppermute | solution.py:31
  108.2 10.6 %collective-permute-start.39 = (f32[2,4096]{1,0:T(2,128)S(1)}, f32[2,4096]{1,0:T(2,128)S(1)}, u32[]{:S(2)}, u32[]{:S(2)}) collective-permute-start(f32[2,4096]{1,0:T(2,128)S(1)} %copy-done.26), channel_id=1, source_target_pairs={{0,4},{4,0},{1,5},{5,1},{2,6},{6,2},{3,7},{7,3},{8,12},{12,8},{9,1... | collective-permute-start | bytes 98312 | tf_op jit(solution)/shard_map/ppermute | solution.py:31
  118.2 9.7 %collective-permute-start.22 = (bf16[4,40,792]{2,1,0:T(8,128)(2,1)S(1)}, bf16[4,40,792]{2,1,0:T(8,128)(2,1)S(1)}, u32[]{:S(2)}, u32[]{:S(2)}) collective-permute-start(bf16[4,40,792]{2,1,0:T(8,128)(2,1)S(1)} %copy-done.9), channel_id=1, source_target_pairs={{0,2},{2,0},{1,3},{3,1},{4,6},{6,4},{5,7},{7,5},{8,10},{10,8},{9,1... | collective-permute-start | bytes 760328 | tf_op jit(solution)/shard_map/ppermute | solution.py:31
  118.8 53.3 %collective-permute-start.21 = (bf16[4,40,792]{2,1,0:T(8,128)(2,1)S(1)}, bf16[4,40,792]{2,1,0:T(8,128)(2,1)S(1)}, u32[]{:S(2)}, u32[]{:S(2)}) collective-permute-start(bf16[4,40,792]{2,1,0:T(8,128)(2,1)S(1)} %copy-done.9), channel_id=1, source_target_pairs={{0,1},{1,0},{2,3},{3,2},{4,5},{5,4},{6,7},{7,6},{8,9},{9,8},{10,11... | collective-permute-start | bytes 760328 | tf_op jit(solution)/shard_map/ppermute | solution.py:31
  121.2 13.1 %collective-permute-start.26 = (bf16[2,2,320,128]{3,2,1,0:T(8,128)(2,1)S(1)}, bf16[2,2,320,128]{3,2,1,0:T(8,128)(2,1)S(1)}, u32[]{:S(2)}, u32[]{:S(2)}) collective-permute-start(bf16[2,2,320,128]{3,2,1,0:T(8,128)(2,1)S(1)} %slice_bitcast_fusion.8), channel_id=1, source_target_pairs={{0,2},{2,0},{1,3},{3,1},{4,6},{6,4},{5,7},{7,5},{8,10},{10,8},{9,1... | collective-permute-start | bytes 983048 | tf_op jit(solution)/shard_map/ppermute | solution.py:31
  122.7 12.7 %collective-permute-start.29 = (bf16[2,2,320,128]{3,2,1,0:T(8,128)(2,1)S(1)}, bf16[2,2,320,128]{3,2,1,0:T(8,128)(2,1)S(1)}, u32[]{:S(2)}, u32[]{:S(2)}) collective-permute-start(bf16[2,2,320,128]{3,2,1,0:T(8,128)(2,1)S(1)} %slice_bitcast_fusion.6), channel_id=1, source_target_pairs={{0,8},{8,0},{1,9},{9,1},{2,10},{10,2},{3,11},{11,3},{4,12},{12,4},... | collective-permute-start | bytes 983048 | tf_op jit(solution)/shard_map/ppermute | solution.py:31
  122.8 12.6 %collective-permute-start.32 = (bf16[2,2,320,128]{3,2,1,0:T(8,128)(2,1)S(1)}, bf16[2,2,320,128]{3,2,1,0:T(8,128)(2,1)S(1)}, u32[]{:S(2)}, u32[]{:S(2)}) collective-permute-start(bf16[2,2,320,128]{3,2,1,0:T(8,128)(2,1)S(1)} %slice_bitcast_fusion.4), channel_id=1, source_target_pairs={{0,4},{4,0},{1,5},{5,1},{2,6},{6,2},{3,7},{7,3},{8,12},{12,8},{9,1... | collective-permute-start | bytes 983048 | tf_op jit(solution)/shard_map/ppermute | solution.py:31
  127.9 58.1 %collective-permute-start.20 = (bf16[2,64,792]{2,1,0:T(8,128)(2,1)S(1)}, bf16[2,64,792]{2,1,0:T(8,128)(2,1)S(1)}, u32[]{:S(2)}, u32[]{:S(2)}) collective-permute-start(bf16[2,64,792]{2,1,0:T(8,128)(2,1)S(1)} %copy-done.28), channel_id=1, source_target_pairs={{0,16},{16,0},{1,17},{17,1},{2,18},{18,2},{3,19},{19,3},{4,20},{20... | collective-permute-start | bytes 608264 | tf_op jit(solution)/shard_map/ppermute | solution.py:31
  134.3 37.7 %collective-permute-start.40 = (f32[4,4096]{1,0:T(4,128)S(1)}, f32[4,4096]{1,0:T(4,128)S(1)}, u32[]{:S(2)}, u32[]{:S(2)}) collective-permute-start(f32[4,4096]{1,0:T(4,128)S(1)} %pad_maximum_fusion.3), channel_id=1, source_target_pairs={{0,8},{8,0},{1,9},{9,1},{2,10},{10,2},{3,11},{11,3},{4,12},{12,4},... | collective-permute-start | bytes 196616 | tf_op jit(solution)/shard_map/ppermute | solution.py:31
  135.4 36.7 %collective-permute-start.23 = (bf16[4,40,792]{2,1,0:T(8,128)(2,1)S(1)}, bf16[4,40,792]{2,1,0:T(8,128)(2,1)S(1)}, u32[]{:S(2)}, u32[]{:S(2)}) collective-permute-start(bf16[4,40,792]{2,1,0:T(8,128)(2,1)S(1)} %collective-permute-done.22.r2), channel_id=1, source_target_pairs={{0,1},{1,0},{2,3},{3,2},{4,5},{5,4},{6,7},{7,6},{8,9},{9,8},{10,11... | collective-permute-start | bytes 760328 | tf_op jit(solution)/shard_map/ppermute | solution.py:31
  176.3 12.5 %collective-permute-start.24 = (bf16[2,64,792]{2,1,0:T(8,128)(2,1)}, bf16[2,64,792]{2,1,0:T(8,128)(2,1)S(1)}, u32[]{:S(2)}, u32[]{:S(2)}) collective-permute-start(bf16[2,64,792]{2,1,0:T(8,128)(2,1)} %get-tuple-element.47), channel_id=1, source_target_pairs={{0,16},{16,0},{1,17},{17,1},{2,18},{18,2},{3,19},{19,3},{4,20},{20... | collective-permute-start | bytes 608264 | tf_op jit(solution)/shard_map/ppermute | solution.py:31
  177.9 13.6 %collective-permute-start.36 = (bf16[928,128]{1,0:T(8,128)(2,1)S(1)}, bf16[928,128]{1,0:T(8,128)(2,1)S(1)}, u32[]{:S(2)}, u32[]{:S(2)}) collective-permute-start(bf16[928,128]{1,0:T(8,128)(2,1)S(1)} %fusion.15.p0), channel_id=1, source_target_pairs={{0,1},{1,0},{2,3},{3,2},{4,5},{5,4},{6,7},{7,6},{8,9},{9,8},{10,11... | collective-permute-start | bytes 712712 | tf_op jit(solution)/shard_map/ppermute | solution.py:31
  177.9 13.6 %collective-permute-start.38 = (bf16[928,128]{1,0:T(8,128)(2,1)S(1)}, bf16[928,128]{1,0:T(8,128)(2,1)S(1)}, u32[]{:S(2)}, u32[]{:S(2)}) collective-permute-start(bf16[928,128]{1,0:T(8,128)(2,1)S(1)} %collective-permute-done.37.p2), channel_id=1, source_target_pairs={{0,1},{1,0},{2,3},{3,2},{4,5},{5,4},{6,7},{7,6},{8,9},{9,8},{10,11... | collective-permute-start | bytes 712712 | tf_op jit(solution)/shard_map/ppermute | solution.py:31
  (46 other events, 290.1 us)

commit v2 on v1

v2 whole, which is shorter than its diff:
```python
import functools

import jax
import jax.numpy as jnp
from jax import lax
from jax.experimental import pallas as pl
from jax.experimental.pallas import tpu as pltpu
from jax.sharding import Mesh, PartitionSpec as P

CG = 264
HALF = 3 * CG
TAPROWS = 27 * CG
LEAD = 33 * (TAPROWS // 16)
CH = 2 * HALF
F32 = jnp.float32
BF16 = jnp.bfloat16
SWAP = [(0, 1), (1, 0)]
PCH = 64
NCH = 7
OROWS = 16 * PCH * NCH + 8
VMEM = pl.BlockSpec(memory_space=pltpu.VMEM)
SMEM = pl.BlockSpec(memory_space=pltpu.SMEM)
HBM = pl.BlockSpec(memory_space=pltpu.HBM)


def params(mebibytes):
    return pltpu.CompilerParams(vmem_limit_bytes=mebibytes * 1024 * 1024)


def cost(microseconds):
    return pl.CostEstimate(flops=0, bytes_accessed=int(microseconds * 0.05 * 3.6e6), transcendentals=0)


def swap(value, axis):
    return lax.ppermute(value, axis, SWAP)


class Sizes:
    def __init__(self, rows, dl_num):
        self.rows = rows
        self.dl_num = dl_num
        self.bound = rows * dl_num - LEAD
        self.top = -(-self.bound // 16) * 16
        self.half = -(-rows // 64) * 32
        self.second = rows - self.half
        self.quarter = self.half // 2
        self.flat = self.top + 33 * PCH * NCH + 8


def split_body(sc, x_ref, mine_ref, send_ref):
    low = sc[0] == 0
    for slot in range(2):
        x = x_ref[64 * slot : 64 * slot + 64, :]
        x = jnp.where(slot < sc[4], x, jnp.zeros_like(x))
        first, second = x[:, :HALF], x[:, HALF:]
        mine_ref[slot] = jnp.where(low, first, second)
        send_ref[slot] = jnp.where(low, second, first)


def split_halves(sc, x):
    shape = jax.ShapeDtypeStruct((2, 64, HALF), BF16)
    return pl.pallas_call(
        split_body,
        out_shape=(shape, shape),
        in_specs=[SMEM, VMEM],
        out_specs=(VMEM, VMEM),
        compiler_params=params(10),
        cost_estimate=cost(2),
        name="split_halves",
    )(sc, x)


def join_body(sc, a_ref, b_ref, out_ref, wide):
    low = sc[0] == 0
    for slot in range(2):
        a = a_ref[slot].astype(F32)
        b = b_ref[slot].astype(F32)
        live = slot < sc[4]
        first = jnp.where(low, a, b)
        second = jnp.where(low, b, a)
        wide[:, :HALF] = jnp.where(live, first, 0.0)
        wide[:, HALF:] = jnp.where(live, second, 0.0)
        out_ref[64 * slot : 64 * slot + 64, :] = wide[...].astype(BF16)


def join_halves(sc, a, b):
    return pl.pallas_call(
        join_body,
        out_shape=jax.ShapeDtypeStruct((128, CH), BF16),
        in_specs=[SMEM, VMEM, VMEM],
        out_specs=VMEM,
        scratch_shapes=[pltpu.VMEM((64, CH), F32)],
        compiler_params=params(10),
        cost_estimate=cost(2),
        name="join_halves",
    )(sc, a, b)


def strips_body(own_ref, other_ref, out_ref):
    for t in range(4):
        ref = own_ref if t < 2 else other_ref
        x = ref[t % 2].astype(F32)
        cube = x.reshape(8, 8, HALF)
        out = jnp.concatenate([x[:8], x[56:], cube[:, 0, :], cube[:, 7, :]], axis=0)
        out_ref[t] = out.astype(BF16)


def make_strips(own, other):
    return pl.pallas_call(
        strips_body,
        out_shape=jax.ShapeDtypeStruct((4, 32, HALF), BF16),
        in_specs=[VMEM, VMEM],
        out_specs=VMEM,
        compiler_params=params(10),
        cost_estimate=cost(1.9),
        name="make_strips",
    )(own, other)


def pad_body(sc, ids, own_ref, other_ref, s0, s1, s2, s3, x3_ref, strips, pad):
    for rel, ref in enumerate((s0, s1, s2, s3)):
        strips[rel] = ref[...]
    for t in range(4):
        ref = own_ref if t < 2 else other_ref
        x = ref[t % 2].astype(F32)
        for i in range(8):
            pad[1 + i, t, 1:9, :] = x[8 * i : 8 * i + 8]

        def piece(offset, member):
            n = ids[t, offset]
            safe = jnp.maximum(n, 0)
            rel = jnp.bitwise_xor(lax.shift_right_logical(safe, 1), sc[5])
            other = 2 * (t // 2) + jnp.bitwise_and(safe, 1)
            got = strips[rel, other].astype(F32)[8 * member : 8 * member + 8]
            return jnp.where(n >= 0, got, 0.0)

        pad[0, t, 0:1, :] = piece(0, 1)[7:8]
        pad[0, t, 1:9, :] = piece(1, 1)
        pad[0, t, 9:10, :] = piece(2, 1)[0:1]
        left = piece(3, 3)
        right = piece(4, 2)
        for i in range(8):
            pad[1 + i, t, 0:1, :] = left[i : i + 1]
            pad[1 + i, t, 9:10, :] = right[i : i + 1]
        pad[9, t, 0:1, :] = piece(5, 0)[7:8]
        pad[9, t, 1:9, :] = piece(6, 0)
        pad[9, t, 9:10, :] = piece(7, 0)[0:1]
    for i in range(10):
        for dx in range(3):
            row = pad[i, :, dx : dx + 8, :].reshape(32, HALF)
            for g in range(3):
                x3_ref[g, dx, i] = row[:, CG * g : CG * g + CG].astype(BF16)


def pad_tiles(sc, ids, own, other, strips):
    return pl.pallas_call(
        pad_body,
        out_shape=jax.ShapeDtypeStruct((3, 3, 10, 32, CG), BF16),
        in_specs=[SMEM, SMEM] + [VMEM] * 6,
        out_specs=VMEM,
        scratch_shapes=[
            pltpu.VMEM((4, 4, 32, HALF), BF16),
            pltpu.VMEM((10, 4, 16, HALF), F32),
        ],
        compiler_params=params(20),
        cost_estimate=cost(3.8),
        name="pad_tiles",
    )(sc, ids, own, other, *strips)


def weight_body(sizes, plan, sc, *refs):
    count = len(plan)
    srcs = refs[:count]
    x3_hbm, w_ref, hid_ref, sums_ref, land, tails, flat, o0, o1, o2, built, x3, sems, more = refs[count:]
    load = pltpu.make_async_copy(x3_hbm, x3, more.at[3])
    copies = []
    for pos, (kind, rel, half, quarter) in enumerate(plan):
        src = srcs[pos]
        pairs = []
        if kind == "all":
            pairs.append((src, land.at[:, half]))
        elif kind == "tail":
            pairs.append((src, tails.at[rel]))
        else:
            dl = jnp.bitwise_xor(sc[1], rel)
            if kind == "own":
                pairs.append((src, land.at[dl, half]))
            elif kind == "half":
                pairs.append((src, land.at[dl, jnp.bitwise_xor(sc[2], half)]))
            else:
                start = pl.multiple_of(jnp.bitwise_xor(sc[3], quarter) * sizes.quarter, 16)
                slot = land.at[dl, jnp.bitwise_xor(sc[2], half), pl.ds(start, sizes.quarter)]
                pairs.append((src.at[pl.ds(0, sizes.quarter)], slot))
                if rel == 2:
                    pairs.append((src.at[pl.ds(sizes.quarter, sizes.top)], tails.at[2 * quarter + half]))
        for src, dst in pairs:
            copies.append(pltpu.make_async_copy(src, dst, sems.at[len(copies)]))
            copies[-1].start()
    load.start()
    for copy in copies:
        copy.wait()
    last = 0 if plan[0][0] == "all" else jnp.bitwise_xor(sc[1], sc[5])
    flat[: sizes.top, :] = tails[last].astype(F32)
    for dl in range(sizes.dl_num):
        start = sizes.top + sizes.rows * dl
        flat[start : start + sizes.half, :] = land[dl, 0].astype(F32)
        start += sizes.second
        flat[start : start + sizes.half, :] = land[dl, 1].astype(F32)
    base = jnp.where(sc[0] == 0, sizes.top, sizes.top - sizes.bound)

    @pl.loop(0, NCH)
    def _(ch):
        start = base + ch * (33 * PCH)
        for k in range(16):
            rows = [flat[pl.ds(start + 2 * k + j, PCH, stride=33), :] for j in range(3)]
            x = jnp.concatenate(rows, axis=1)
            if k:
                x = pltpu.roll(x, 384 - 8 * k, axis=1)
            for col, ref in enumerate((o0, o1, o2)):
                ref[pl.ds(ch * (16 * PCH) + k, PCH, stride=16), :] = x[:, 128 * col : 128 * col + 128]

    off = jnp.where(sc[0] == 0, 0, 8)
    stores = []
    for g in range(3):
        for tap in range(9):
            here = pl.ds(pl.multiple_of(off + CG * (9 * g + tap), 8), CG)
            built[g, tap, :, :128] = o0[here, :].astype(BF16)
            built[g, tap, :, 128:256] = o1[here, :].astype(BF16)
            built[g, tap, :, 256:] = o2[here, :8].astype(BF16)
        stores.append(pltpu.make_async_copy(built.at[g], w_ref.at[g], more.at[g]))
        stores[g].start()
        if g == 0:
            load.wait()
        forward_group(sc, g, x3, built, hid_ref, sums_ref)
    for copy in stores:
        copy.wait()


def forward_group(sc, g, x3, w, hid_ref, sums_ref):
    acc = jnp.zeros((256, CG), F32)
    for dx in range(3):
        for dy in range(3):
            x = x3[g, dx, dy : dy + 8].reshape(256, CG)
            acc += jnp.dot(x, w[g, 3 * dy + dx], preferred_element_type=F32)
    hid_ref[g] = acc
    active = (acc * jax.nn.sigmoid(acc)).astype(BF16).astype(F32)
    sums_ref[g] = jnp.full((8, CG), sc[4].astype(F32), F32)
    slide_sums(active, sums_ref, g, 0)


def slide_sums(value, sums_ref, g, row):
    value = value.reshape(8, 4, 8, CG)
    for slide in range(2):
        part = value[:, 2 * slide] + value[:, 2 * slide + 1]
        sums_ref[g, row + slide : row + slide + 1, :] = jnp.sum(jnp.sum(part, axis=0), axis=0, keepdims=True)


def weight_forward(sizes, sc, plan, arrays, x3):
    return pl.pallas_call(
        functools.partial(weight_body, sizes, plan),
        out_shape=(
            jax.ShapeDtypeStruct((3, 9, CG, CG), BF16),
            jax.ShapeDtypeStruct((3, 256, CG), F32),
            jax.ShapeDtypeStruct((3, 8, CG), F32),
        ),
        in_specs=[SMEM] + [HBM] * (len(plan) + 1),
        out_specs=(HBM, VMEM, VMEM),
        scratch_shapes=[
            pltpu.VMEM((sizes.dl_num, 2, sizes.half, 128), BF16),
            pltpu.VMEM((4, sizes.top, 128), BF16),
            pltpu.VMEM((sizes.flat, 128), F32),
            pltpu.VMEM((OROWS, 128), F32),
            pltpu.VMEM((OROWS, 128), F32),
            pltpu.VMEM((OROWS, 128), F32),
            pltpu.VMEM((3, 9, CG, CG), BF16),
            pltpu.VMEM((3, 3, 10, 32, CG), BF16),
            pltpu.SemaphoreType.DMA((len(plan) + 4,)),
            pltpu.SemaphoreType.DMA((4,)),
        ],
        compiler_params=params(48),
        cost_estimate=cost(18),
        name="weight_forward",
    )(sc, *arrays, x3)


def regroup_body(own_ref, other_ref, hid_ref, half_ref, out_ref, sums_ref, cot):
    x = [(own_ref if t < 2 else other_ref)[t % 2].astype(F32) for t in range(4)]
    for i in range(8):
        row = jnp.concatenate([x[t][8 * i : 8 * i + 8] for t in range(4)], axis=0)
        for g in range(3):
            part = row[:, CG * g : CG * g + CG]
            out_ref[g, 32 * i : 32 * i + 32, :] = part.astype(BF16)
            cot[g, 32 * i : 32 * i + 32, :] = part
    for g in range(3):
        hidden = hid_ref[g]
        active = (hidden * jax.nn.sigmoid(hidden)).astype(BF16).astype(F32)
        sums_ref[g] = half_ref[g]
        slide_sums(active * cot[g], sums_ref, g, 2)


def regroup(own, other, hidden, sums):
    return pl.pallas_call(
        regroup_body,
        out_shape=(
            jax.ShapeDtypeStruct((3, 256, CG), BF16),
            jax.ShapeDtypeStruct((3, 8, CG), F32),
        ),
        in_specs=[VMEM] * 4,
        out_specs=(VMEM, VMEM),
        scratch_shapes=[pltpu.VMEM((3, 256, CG), F32)],
        compiler_params=params(12),
        cost_estimate=cost(3.3),
        name="regroup",
    )(own, other, hidden, sums)


def thirds(x):
    hi = x.astype(BF16).astype(F32)
    mid = (x - hi).astype(BF16).astype(F32)
    low = (x - hi - mid).astype(BF16).astype(F32)
    return hi, mid, low


def exact_dot(x, w, contract):
    parts = jnp.concatenate([*thirds(x), jnp.zeros((10, x.shape[1]), F32)], axis=0).astype(BF16)
    out = lax.dot_general(parts, w, (((1,), (contract,)), ((), ())), preferred_element_type=F32)
    return out[0:2] + out[2:4] + out[4:6]


def gate_body(sc, mine_ref, mine_far_ref, other_ref, other_far_ref, sq_ref, ex_ref, gate_ref, fin_ref, wide):
    low = sc[0] == 0
    for g in range(3):
        a = mine_ref[g] + mine_far_ref[g]
        b = other_ref[g] + other_far_ref[g]
        if g == 0:
            counts = jnp.concatenate([a[4:5, 0:1], b[4:5, 0:1]], axis=0)
        a = a[0:4]
        b = jnp.concatenate([b[1:2], b[0:1], b[3:4], b[2:3]], axis=0)
        wide[0:4, CG * g : CG * g + CG] = jnp.where(low, a, b)
        wide[0:4, HALF + CG * g : HALF + CG * g + CG] = jnp.where(low, b, a)
    total = counts * 64.0
    pooled = wide[0:2, :] / total
    gate = wide[2:4, :]
    w_squeeze = sq_ref[...]
    w_excite = ex_ref[...]
    pre = exact_dot(pooled, w_squeeze, 0)
    sig = jax.nn.sigmoid(pre)
    squeezed = pre * sig
    excite = jax.nn.sigmoid(exact_dot(squeezed, w_excite, 1))
    excite_grad = gate * excite * (1.0 - excite)
    slope = sig * (1.0 + pre * (1.0 - sig))
    squeeze_grad = exact_dot(excite_grad, w_excite, 0) * slope
    pool = exact_dot(squeeze_grad, w_squeeze, 1) / total
    half_e = jnp.where(low, excite[:, :HALF], excite[:, HALF:])
    half_p = jnp.where(low, pool[:, :HALF], pool[:, HALF:])
    for g in range(3):
        gate_ref[g, 0:2, :] = half_e[:, CG * g : CG * g + CG]
        gate_ref[g, 2:4, :] = half_p[:, CG * g : CG * g + CG]

    def ordered(x):
        return jnp.where(low, x, jnp.concatenate([x[1:2], x[0:1]], axis=0))

    fin_ref[...] = jnp.zeros_like(fin_ref)
    fin_ref[:, 0:CH] = ordered(pooled)
    fin_ref[:, 1664 : 1664 + CH] = ordered(excite_grad)
    width = squeezed.shape[1]
    fin_ref[:, 3328 : 3328 + width] = ordered(squeezed)
    fin_ref[:, 3712 : 3712 + width] = ordered(squeeze_grad)


def gate_stage(sc, sums, w_squeeze, w_excite):
    return pl.pallas_call(
        gate_body,
        out_shape=(
            jax.ShapeDtypeStruct((3, 8, CG), F32),
            jax.ShapeDtypeStruct((2, 4096), F32),
        ),
        in_specs=[SMEM] + [VMEM] * 6,
        out_specs=(VMEM, VMEM),
        scratch_shapes=[pltpu.VMEM((8, CH), F32)],
        compiler_params=params(16),
        cost_estimate=cost(3.9),
        name="gate_stage",
    )(sc, *sums, w_squeeze, w_excite)


def outer_dot(a, b):
    ah, am, al = thirds(a)
    bh, bm, bl = thirds(b)
    left = jnp.concatenate([ah, ah, ah, am, am, al], axis=0).astype(BF16)
    right = jnp.concatenate([bh, bm, bl, bh, bm, bh], axis=0).astype(BF16)
    return lax.dot_general(left, right, (((0,), (0,)), ((), ())), preferred_element_type=F32)


def outer_body(width, fin_ref, sq_ref, ex_ref):
    pooled = fin_ref[:, 0:CH]
    excite_grad = fin_ref[:, 1664 : 1664 + CH]
    squeezed = fin_ref[:, 3328 : 3328 + width]
    squeeze_grad = fin_ref[:, 3712 : 3712 + width]
    sq_ref[...] = outer_dot(pooled, squeeze_grad)
    ex_ref[...] = outer_dot(excite_grad, squeezed)


def outer_stage(fin, width):
    return pl.pallas_call(
        functools.partial(outer_body, width),
        out_shape=(
            jax.ShapeDtypeStruct((CH, width), F32),
            jax.ShapeDtypeStruct((CH, width), F32),
        ),
        in_specs=[VMEM],
        out_specs=(VMEM, VMEM),
        compiler_params=params(20),
        cost_estimate=cost(3.7),
        name="outer_stage",
    )(fin)


def output_body(hid_ref, x3_ref, gate_ref, own_ref, other_ref, wide):
    for g in range(3):
        gate = gate_ref[g]
        by_slide = jnp.concatenate(
            [jnp.broadcast_to(gate[s : s + 1], (16, CG)) for s in range(2)], axis=0
        )
        for i in range(8):
            hidden = hid_ref[g, 32 * i : 32 * i + 32, :]
            active = (hidden * jax.nn.sigmoid(hidden)).astype(BF16).astype(F32)
            value = x3_ref[g, 1, 1 + i].astype(F32) + active * by_slide
            for t in range(4):
                wide[t, 8 * i : 8 * i + 8, CG * g : CG * g + CG] = value[8 * t : 8 * t + 8]
    for t in range(4):
        (own_ref if t < 2 else other_ref)[t % 2] = wide[t].astype(BF16)


def output_stage(hidden, x3, gate):
    shape = jax.ShapeDtypeStruct((2, 64, HALF), BF16)
    return pl.pallas_call(
        output_body,
        out_shape=(shape, shape),
        in_specs=[VMEM] * 3,
        out_specs=(VMEM, VMEM),
        scratch_shapes=[pltpu.VMEM((4, 64, HALF), F32)],
        compiler_params=params(16),
        cost_estimate=cost(3.1),
        name="output_stage",
    )(hidden, x3, gate)


def hidden_slope(hid_ref, cot_ref, gate_ref):
    hidden = hid_ref[0]
    gate = gate_ref[0]

    def spread(row):
        pair = [jnp.broadcast_to(gate[row + s : row + s + 1], (16, CG)) for s in range(2)]
        both = jnp.concatenate(pair, axis=0)
        return jnp.broadcast_to(both[None], (8, 32, CG)).reshape(256, CG)

    sig = jax.nn.sigmoid(hidden)
    slope = sig * (1.0 + hidden * (1.0 - sig))
    return ((cot_ref[0].astype(F32) * spread(0) + spread(2)) * slope).astype(BF16)


def weight_grad_body(sizes, sc, grad_ref, x3_ref, keep_ref, send_ref, ext_ref, flat, carry):
    g = pl.program_id(0)

    @pl.when(g == 0)
    def _():
        end = sizes.top + sizes.rows * sizes.dl_num
        flat[: sizes.top, :] = jnp.zeros((sizes.top, 128), F32)
        flat[end - 16 : end, :] = jnp.zeros((16, 128), F32)
        carry[...] = jnp.zeros_like(carry)

    grad = grad_ref[0]
    base = jnp.where(sc[0] == 0, sizes.top, sizes.top - sizes.bound)
    first = jnp.where(sc[0] == 0, 0, 1) + g * (9 * 33)
    row = lax.broadcasted_iota(jnp.int32, (8, 128), 0)
    lane = lax.broadcasted_iota(jnp.int32, (8, 128), 1)
    edge = lane - 8 * row
    zeros = jnp.zeros((CG, 120), F32)

    def taps(odd):
        held = carry[...]
        for tap in range(9):
            dy, dx = divmod(tap, 3)
            x = x3_ref[0, dx, dy : dy + 8].reshape(256, CG)
            res = lax.dot_general(x, grad, (((0,), (0,)), ((), ())), preferred_element_type=F32)
            res = jnp.concatenate([res, zeros], axis=1)
            for i in range(33):
                h = (odd + tap + i) % 2
                place = first + 33 * tap + i
                start = base + 33 * lax.shift_right_logical(place, 1) + 16 * h
                turned = [
                    pltpu.roll(
                        res[8 * i : 8 * i + 8, 128 * col : 128 * col + 128], 64 * h, axis=1, stride=8, stride_axis=0
                    )
                    for col in range(3)
                ]
                own = edge >= 64 * h
                third = jnp.where(own, turned[2], turned[1])
                shifted = pltpu.roll(third, 1, axis=0)
                before = jnp.where(row == 0, held, shifted)
                flat[pl.ds(start, 8, stride=2), :] = jnp.where(own, turned[0], before)
                flat[pl.ds(start + 1, 8, stride=2), :] = jnp.where(own, turned[1], turned[0])
                flat[pl.ds(start + 16, 1), :] = third[7:8]
                held = shifted
        carry[...] = held

    parity = jnp.bitwise_and(first, 1)
    for odd in range(2):
        @pl.when(parity == odd)
        def _():
            taps(odd)

    @pl.when(g == 2)
    def _():
        even = sc[2] == 0
        quarter = sizes.quarter
        ext_ref[...] = flat[: sizes.top, :]
        for dl in range(sizes.dl_num):
            for q in range(2):
                start = sizes.top + sizes.rows * dl + q * quarter
                v0 = flat[start : start + quarter, :]
                v1 = flat[start + sizes.second : start + sizes.second + quarter, :]
                rel = jnp.bitwise_xor(sc[1], dl)
                part = jnp.bitwise_xor(sc[3], q)
                keep_ref[rel, part] = jnp.where(even, v0, v1).astype(BF16)
                send_ref[rel, part] = jnp.where(even, v1, v0).astype(BF16)


def weight_grad(sizes, sc, grad, x3):
    pieces = jax.ShapeDtypeStruct((sizes.dl_num, 2, sizes.quarter, 128), BF16)
    return pl.pallas_call(
        functools.partial(weight_grad_body, sizes),
        grid=(3,),
        out_shape=(
            pieces,
            pieces,
            jax.ShapeDtypeStruct((sizes.top, 128), F32),
        ),
        in_specs=[
            SMEM,
            pl.BlockSpec((1, 256, CG), lambda g: (g, 0, 0)),
            pl.BlockSpec((1, 3, 10, 32, CG), lambda g: (g, 0, 0, 0, 0)),
        ],
        out_specs=(VMEM, VMEM, VMEM),
        scratch_shapes=[
            pltpu.VMEM((sizes.flat, 128), F32),
            pltpu.VMEM((8, 128), F32),
        ],
        compiler_params=params(32),
        cost_estimate=cost(11.9),
        name="weight_grad",
    )(sc, grad, x3)


def input_grad_body(ids, hid_ref, cot_ref, gate_ref, w_ref, inner_ref, rim_ref, grad_ref, pads, part, cols):
    g = pl.program_id(0)

    part[...] = jnp.zeros_like(part)
    grad = hidden_slope(hid_ref, cot_ref, gate_ref)
    grad_ref[0] = grad
    for dx in range(3):
        cols[...] = jnp.zeros_like(cols)
        for dy in range(3):
            d = lax.dot_general(grad, w_ref[0, 3 * dy + dx], (((1,), (1,)), ((), ())), preferred_element_type=F32)
            cols[dy : dy + 8] += d.reshape(8, 32, CG)
        part[:, :, dx : dx + 8, :] += cols[...].reshape(10, 4, 8, CG)
    for value in range(3):
        @pl.when(g == value)
        def _():
            pads[:, :, :, CG * value : CG * value + CG] = part[...]

    @pl.when(g == 2)
    def _():
        for t in range(4):
            for i in range(8):
                inner_ref[t, 8 * i : 8 * i + 8, :] = pads[1 + i, t, 1:9, :]
            left = jnp.concatenate([pads[1 + i, t, 0:1, :] for i in range(8)], axis=0)
            right = jnp.concatenate([pads[1 + i, t, 9:10, :] for i in range(8)], axis=0)
            corners = [pads[0, t, 0:1, :], pads[0, t, 9:10, :], pads[9, t, 0:1, :], pads[9, t, 9:10, :]]
            lane = lax.broadcasted_iota(jnp.int32, (4, HALF), 1)
            listed = jnp.full((4, HALF), -1.0, F32)
            for k in range(8):
                listed = jnp.where(lane == k, ids[t, k].astype(F32), listed)
            parts = [pads[0, t, 1:9, :], left, right, pads[9, t, 1:9, :], *corners, listed]
            rim_ref[t] = jnp.concatenate(parts, axis=0).astype(BF16)


def input_grad(ids, hidden, cot, gate, w):
    return pl.pallas_call(
        input_grad_body,
        grid=(3,),
        out_shape=(
            jax.ShapeDtypeStruct((4, 64, HALF), F32),
            jax.ShapeDtypeStruct((4, 40, HALF), BF16),
            jax.ShapeDtypeStruct((3, 256, CG), BF16),
        ),
        in_specs=[
            SMEM,
            pl.BlockSpec((1, 256, CG), lambda g: (g, 0, 0)),
            pl.BlockSpec((1, 256, CG), lambda g: (g, 0, 0)),
            pl.BlockSpec((1, 8, CG), lambda g: (g, 0, 0)),
            pl.BlockSpec((1, 9, CG, CG), lambda g: (g, 0, 0, 0)),
        ],
        out_specs=(VMEM, VMEM, pl.BlockSpec((1, 256, CG), lambda g: (g, 0, 0))),
        scratch_shapes=[
            pltpu.VMEM((10, 4, 16, HALF), F32),
            pltpu.VMEM((10, 4, 16, CG), F32),
            pltpu.VMEM((10, 32, CG), F32),
        ],
        compiler_params=params(28),
        cost_estimate=cost(9.5),
        name="input_grad",
    )(ids, hidden, cot, gate, w)


def rims_body(sc, own_ref, other_ref, inner_ref, r0, r1, r2, r3, out0_ref, out1_ref, edges, corners):
    edges[...] = jnp.zeros_like(edges)
    corners[...] = jnp.zeros_like(corners)
    for ref in (r0, r1, r2, r3):
        for slide in range(2):
            for slot in range(2):
                t = 2 * slide + slot
                rim = ref[t].astype(F32)
                for mine in range(2):
                    own = (2 * sc[5] + mine).astype(F32)
                    n = 2 * slide + mine

                    def hit(offset):
                        return jnp.where(rim[36:37, offset : offset + 1] == own, 1.0, 0.0)

                    for member, offset in enumerate((1, 3, 4, 6)):
                        edges[n, member] += hit(offset) * rim[8 * member : 8 * member + 8]
                    for member, offset in enumerate((0, 2, 5, 7)):
                        row = 32 + member
                        corners[n, member : member + 1] += hit(offset) * rim[row : row + 1]
    for n in range(4):
        cot = (own_ref if n < 2 else other_ref)[n % 2].astype(F32)
        inner_ref_n = inner_ref[n] + cot
        last_col = edges[n, 1]
        first_col = edges[n, 2]
        rows = []
        for i in range(8):
            row = inner_ref_n[8 * i : 8 * i + 8]
            lo = first_col[i : i + 1]
            hi = last_col[i : i + 1]
            if i == 0:
                row = row + edges[n, 3]
                hi = hi + corners[n, 2:3]
                lo = lo + corners[n, 3:4]
            if i == 7:
                row = row + edges[n, 0]
                hi = hi + corners[n, 0:1]
                lo = lo + corners[n, 1:2]
            pos = lax.broadcasted_iota(jnp.int32, (8, HALF), 0)
            row = row + jnp.where(pos == 0, lo, 0.0) + jnp.where(pos == 7, hi, 0.0)
            rows.append(row)
        (out0_ref if n < 2 else out1_ref)[n % 2] = jnp.concatenate(rows, axis=0).astype(BF16)


def add_rims(sc, own, other, inner, rims):
    shape = jax.ShapeDtypeStruct((2, 64, HALF), BF16)
    return pl.pallas_call(
        rims_body,
        out_shape=(shape, shape),
        in_specs=[SMEM] + [VMEM] * 7,
        out_specs=(VMEM, VMEM),
        scratch_shapes=[
            pltpu.VMEM((4, 4, 8, HALF), F32),
            pltpu.VMEM((4, 8, HALF), F32),
        ],
        compiler_params=params(16),
        cost_estimate=cost(3.4),
        name="add_rims",
    )(sc, own, other, inner, *rims)


def rows_body(sizes, sc, p0, p1, p2, p3, out_ref, land, sems):
    copies = []
    for rel, ref in enumerate((p0, p1, p2, p3)):
        c = jnp.bitwise_xor(sc[2], rel & 1)
        q = jnp.bitwise_xor(sc[3], rel >> 1)
        copies.append(pltpu.make_async_copy(ref, land.at[c, q], sems.at[rel]))
        copies[-1].start()
    for copy in copies:
        copy.wait()
    for c in range(2):
        for q in range(2):
            start = c * sizes.second + q * sizes.quarter
            out_ref[start : start + sizes.quarter, :] = land[c, q].astype(F32)


def place_rows(sizes, sc, parts):
    return pl.pallas_call(
        functools.partial(rows_body, sizes),
        out_shape=jax.ShapeDtypeStruct((sizes.rows, 128), F32),
        in_specs=[SMEM] + [HBM] * 4,
        out_specs=VMEM,
        scratch_shapes=[
            pltpu.VMEM((2, 2, sizes.quarter, 128), BF16),
            pltpu.SemaphoreType.DMA((4,)),
        ],
        compiler_params=params(12),
        cost_estimate=cost(3),
        name="place_rows",
    )(sc, *parts)


def tile_ring(value):
    near = swap(value, "t1")
    far = swap(value, "t0")
    return value, near, far, swap(far, "t1")


def tie(*values):
    return lax.optimization_barrier(values)


def grow(value, name):
    other = swap(value, name)
    first = lax.axis_index(name) == 0
    return jnp.concatenate([jnp.where(first, value, other), jnp.where(first, other, value)], axis=0)


def halve(current, names, name):
    pos = names.index(name)
    send = lax.index_in_dim(current, 1, pos, keepdims=False).astype(BF16)
    stay = lax.index_in_dim(current, 0, pos, keepdims=False)
    return send, stay, [n for n in names if n != name]


def shards(dbits, features, cotangent, conv_weight, squeeze_weight, excite_weight, live_count, neighbours):
    lows = tuple(f"d{i}" for i in range(1, dbits))
    dl_num = 2 ** (dbits - 1)
    sizes = Sizes(conv_weight.shape[0], dl_num)
    dh = lax.axis_index("d0")
    dl = lax.axis_index(lows)
    y = lax.axis_index("t0")
    c = lax.axis_index("t1")
    count = live_count[0, 0]
    sc = jnp.stack([dh, dl, c, y, count, 2 * y + c, count, count]).astype(jnp.int32)

    half0 = conv_weight[: sizes.half]
    half1 = conv_weight[sizes.second :]
    tail = conv_weight[sizes.rows - sizes.top :]
    ids_own = neighbours[0]
    if len(lows) == 2:
        mine = jnp.where(c == 0, half0, half1)
        part = jnp.where(y == 0, mine[: sizes.quarter], mine[sizes.quarter :])
        mine, part, features = tie(mine, part, features)
        a2 = swap(mine, "d2")
        q1 = swap(part, "d1")
        bnd = lax.ppermute(tail, ("d0",) + lows + ("t0", "t1"), [(12 + t, 16 + 5 * t) for t in range(4)])
        feat_own, feat_send = split_halves(sc, features.reshape(128, CH))
        feat_other = swap(feat_send, "d0")
        ids4 = jnp.concatenate([ids_own, swap(ids_own, "d0")], axis=0)
        s0 = make_strips(feat_own, feat_other)
        q1, feat_own = tie(q1, feat_own)
        q3 = swap(q1, "d2")
        q1 = jnp.concatenate([q1, bnd], axis=0)
        y1 = swap(q1, "t0")
        s0, y1, q3, ids4, cotangent = tie(s0, y1, q3, ids4, cotangent)
        cot_own, cot_send = split_halves(sc, cotangent.reshape(128, CH))
        s1, s2 = swap(s0, "t1"), swap(s0, "t0")
        s1, s2, q3, y1, cot_send = tie(s1, s2, q3, y1, cot_send)
        y3 = swap(q3, "t0")
        cot_other = swap(cot_send, "d0")
        strips = [s0, s1, s2, swap(s2, "t1")]
        near = [swap(p, "t1") for p in (a2, q1, q3, y1)]
        x3 = pad_tiles(sc, ids4, feat_own, feat_other, strips)
        y3, x3 = tie(y3, x3)
        arrays = [bnd, half0, half1, a2, q1, q3, y1, y3, *near, swap(y3, "t1")]
        plan = [("tail", 0, 0, 0), ("own", 0, 0, 0), ("own", 0, 1, 0)]
        for half in range(2):
            plan += [("half", 1, half, 0), ("quarter", 2, half, 0), ("quarter", 3, half, 0),
                     ("quarter", 2, half, 1), ("quarter", 3, half, 1)]
    else:
        feat_own, feat_send = split_halves(sc, features.reshape(128, CH))
        feat_other = swap(feat_send, "d0")
        cot_own, cot_send = split_halves(sc, cotangent.reshape(128, CH))
        cot_other = swap(cot_send, "d0")
        ids4 = jnp.concatenate([ids_own, swap(ids_own, "d0")], axis=0)
        strips = tile_ring(make_strips(feat_own, feat_other))
        x3 = pad_tiles(sc, ids4, feat_own, feat_other, strips)
        bnd = lax.all_gather(swap(tail, "d0"), lows)[-1]
        arrays = [lax.all_gather(half0, lows), lax.all_gather(half1, lows), bnd]
        plan = [("all", 0, 0, 0), ("all", 0, 1, 0), ("tail", 0, 0, 0)]
    w, hidden, sums = weight_forward(sizes, sc, plan, arrays, x3)
    hidden, cot_other = tie(hidden, cot_other)
    cot, sums = regroup(cot_own, cot_other, hidden, sums)
    sums = sums + swap(sums, "t1")
    cross = [(0, 3), (1, 2), (2, 1), (3, 0)]
    sums = [sums, swap(sums, "t0"), swap(sums, "d0"), lax.ppermute(sums, ("d0", "t0"), cross)]
    gate, fin = gate_stage(sc, sums, squeeze_weight, excite_weight.T)

    out_own, out_send = output_stage(hidden, x3, gate)
    out_send, gate, fin = tie(out_send, gate, fin)
    out_other = swap(out_send, "d0")
    for name in lows[:0:-1]:
        fin = grow(fin, name)
    inner, r0, grad = input_grad(ids4, hidden, cot, gate, w)
    r0, grad, out_other, fin = tie(r0, grad, out_other, fin)
    r2, r1 = swap(r0, "t0"), swap(r0, "t1")
    keep, send, ext = weight_grad(sizes, sc, grad, x3)

    send, ext, r1, r2 = tie(send, ext, r1, r2)
    got = swap(send, "t1")
    ext_near = swap(ext, "d0")
    ext_far = lax.ppermute(ext, ("d0", "t1"), cross)
    r3 = swap(r2, "t1")
    got, ext_near, ext_far, keep = tie(got, ext_near, ext_far, keep)
    ext = ext_near + ext_far
    place = jnp.logical_and(jnp.arange(dl_num)[:, None] == dl ^ (dl_num - 1), jnp.arange(2)[None] == 1 - y)
    place = jnp.logical_and(place, jnp.logical_and(dh == 0, c == 1))
    ext = jnp.where(place[:, :, None, None], ext[None, None], 0.0)
    ext = jnp.pad(ext, ((0, 0), (0, 0), (sizes.quarter - sizes.top, 0), (0, 0)))
    total = keep.astype(F32) + got.astype(F32) + ext
    axes = lows + ("t0",)
    total = total.reshape((2,) * len(axes) + (sizes.quarter, 128))
    most = sizes.quarter * 13 // 32 // 16 * 16
    cuts = [(0, most), (most, 2 * most), (2 * most, sizes.quarter)]
    far = lows[::-1]
    turns = [("t0",) + far, far[:1] + ("t0",) + far[1:], far[-1:] + far[:-1] + ("t0",)]
    state = [(total[..., lo:hi, :], list(axes)) for lo, hi in cuts]
    for step in range(len(axes)):
        halves = [halve(cur, names, turn[step]) for (cur, names), turn in zip(state, turns)]
        sends = [h[0] for h in halves]
        if step == 0:
            *sends, r3 = tie(*sends, r3)
        elif step == 1:
            *sends, back_send, fin, out_own = tie(*sends, back_send, fin, out_own)
        else:
            sends = tie(*sends)
        recv = [swap(v, turn[step]) for v, turn in zip(sends, turns)]
        if step == 0:
            back_own, back_send = add_rims(sc, cot_own, cot_other, inner, [r0, r1, r2, r3])
            *recv, back_own, back_send = tie(*recv, back_own, back_send)
        elif step == 1:
            back_other = swap(back_send, "d0")
            fin = grow(fin, lows[0])
            output = join_halves(sc, out_own, out_other)
            *recv, fin, output = tie(*recv, fin, output)
        elif step == 2:
            *recv, back_other = tie(*recv, back_other)
        else:
            recv = tie(*recv)
        state = [(h[1] + r.astype(F32), h[2]) for h, r in zip(halves, recv)]
    body = jnp.concatenate([cur for cur, _ in state], axis=0).astype(BF16)
    body, back_own, fin = tie(body, back_own, fin)
    p2, p1 = swap(body, "t0"), swap(body, "t1")
    grad_in = join_halves(sc, back_own, back_other)
    grad_squeeze, grad_excite = outer_stage(fin, squeeze_weight.shape[1])
    p2, p1, grad_in, grad_squeeze = tie(p2, p1, grad_in, grad_squeeze)
    parts = [body, p1, p2, swap(p2, "t1")]
    grad_conv = place_rows(sizes, sc, parts)
    shape = features.shape
    return (output.reshape(shape), grad_in.reshape(shape), grad_conv, grad_squeeze, grad_excite.T)


def solution(mesh):
    dbits = mesh.shape["dp"].bit_length() - 1
    dnames = tuple(f"d{i}" for i in range(dbits))
    tnames = ("t0", "t1")
    fine = Mesh(mesh.devices.reshape((2,) * (dbits + 2)), dnames + tnames)
    return jax.shard_map(
        functools.partial(shards, dbits),
        mesh=fine,
        in_specs=(
            P(dnames, tnames, None, None, None),
            P(dnames, tnames, None, None, None),
            P(dnames, None),
            P(),
            P(),
            P(dnames, tnames),
            P(dnames, tnames, None),
        ),
        out_specs=(
            P(dnames, tnames, None, None, None),
            P(dnames, tnames, None, None, None),
            P(dnames, None),
            P(),
            P(),
        ),
        check_vma=False,
    )
```

time: 196 us -> 145 us (0.74)
  waiting for transfers between devices: 64.4 us -> 37.6 us
  Pallas kernels: 70.6 us -> 45.8 us
  starting transfers between devices: 32.2 us -> 44 us
  blocking collectives: 5.38 us -> 0 us
  other arithmetic: 7.62 us -> 4.2 us
  local copies, waits for them, and re-layouts: 13.7 us -> 10.9 us
    ppermute x41 -> x40, waiting for transfers between devices: 64.4 us -> 35 us  [swap(): return lax.ppermute(value, axis, SWAP)]
    pallas_call x5, Pallas kernels: 43 us -> 30.6 us  [the longest x1 15.1 us: weight_forward(): pl.pallas_call(functools.partial(weight_body, sizes, plan), out_shape=(ja...]
    ppermute x41 -> x40, starting transfers between devices: 32.2 us -> 39.6 us  [swap(): return lax.ppermute(value, axis, SWAP)]
    all_gather x1 -> x0, blocking collectives: 5.38 us -> none  [shards(): ids_all = lax.all_gather(ids4, ('t0', 't1'))]
    ppermute x0 -> x3, starting transfers between devices: none -> 4.39 us  [the longest x1 2.55 us: shards(): lax.ppermute(sums, ('d0', 't0'), cross)]
    unnamed x60 -> x49, local copies, waits for them, and re-layouts: 12.1 us -> 9.31 us
    select_n x5 -> x4, other arithmetic: 2.86 us -> 0.15 us  [the longest x1 0.08 us: shards(): ext = jnp.where(place[:, :, None, None], ext[None, None], 0.0)]
    pallas_call x1, Pallas kernels: 3.1 us -> 0.41 us  [output_stage(): pl.pallas_call(output_body, out_shape=(shape, shape), in_specs=[VMEM] * 3...]
  transfers between devices with their start and end apart: 41 -> 43, of which waited for: 16 -> 21; matrix products, arithmetic and copies ran while one was open for 6% -> 2% of each run, Pallas kernels for 13% -> 27%
where the time goes in v2:
time: 145 us
  Pallas kernels  45.8 us (32%)
  starting transfers between devices  44 us (30%)
  waiting for transfers between devices  37.6 us (26%)
  local copies, waits for them, and re-layouts  10.9 us (8%)
  other arithmetic  4.2 us (3%)
  between operations  2.01 us (1%)
    ppermute x40, starting transfers between devices, swap(): return lax.ppermute(value, axis, SWAP)  39.6 us
    ppermute x40, waiting for transfers between devices, swap(): return lax.ppermute(value, axis, SWAP)  35 us
    pallas_call x1, Pallas kernels, weight_forward(): pl.pallas_call(functools.partial(weight_body, sizes, plan), out_shape=(ja...  15.1 us
    unnamed x49, local copies, waits for them, and re-layouts  9.31 us
    pallas_call x1, Pallas kernels, weight_grad(): pl.pallas_call(functools.partial(weight_grad_body, sizes), grid=(3,), out...  7.16 us
    pallas_call x1, Pallas kernels, input_grad(): pl.pallas_call(input_grad_body, grid=(3,), out_shape=(jax.ShapeDtypeStruc...  6.02 us
    pallas_call x1, Pallas kernels, place_rows(): pl.pallas_call(functools.partial(rows_body, sizes), out_shape=jax.ShapeDt...  3.19 us
    pallas_call x2, Pallas kernels, join_halves(): pl.pallas_call(join_body, out_shape=jax.ShapeDtypeStruct((128, CH), BF16)...  2.98 us
  transfers between devices with their start and end apart: 43, of which 21 were waited for; matrix products, arithmetic and copies ran while one was open for 2% of the time, Pallas kernels for 27%

profile of v2, /device:TPU:0, one launch (start us, length us, event | category | flops | bytes accessed | tf_op | source)
XLA Modules:
  0.0 144.6 jit_solution(1017982461689762704)
XLA Ops:
  2.1 3.1 %collective-permute-start.1 = (bf16[928,128]{1,0:T(8,128)(2,1)S(1)}, bf16[928,128]{1,0:T(8,128)(2,1)S(1)}, u32[]{:S(2)}, u32[]{:S(2)}) collective-permute-start(bf16[928,128]{1,0:T(8,128)(2,1)S(1)} %slice_select_fusion), channel_id=1, source_target_pairs={{0,8},{8,0},{1,9},{9,1},{2,10},{10,2},{3,11},{11,3},{4,12},{12,4},... | collective-permute-start | bytes 712712 | tf_op jit(solution)/shard_map/ppermute | solution.py:35
  11.0 1.7 %collective-permute-start.3 = (bf16[960,128]{1,0:T(8,128)(2,1)S(1)}, bf16[960,128]{1,0:T(8,128)(2,1)S(1)}, u32[]{:S(2)}, u32[]{:S(2)}) collective-permute-start(bf16[960,128]{1,0:T(8,128)(2,1)S(1)} %constant_dynamic-update-slice_fusion.refs_4_), channel_id=1, source_target_pairs={{0,2},{2,0},{1,3},{3,1},{4,6},{6,4},{5,7},{7,5},{8,10},{10,8},{9,1... | collective-permute-start | bytes 737288 | tf_op jit(solution)/shard_map/ppermute | solution.py:35
  14.2 2.6 %collective-permute-start = (bf16[2,64,792]{2,1,0:T(8,128)(2,1)S(1)}, bf16[2,64,792]{2,1,0:T(8,128)(2,1)S(1)}, u32[]{:S(2)}, u32[]{:S(2)}) collective-permute-start(bf16[2,64,792]{2,1,0:T(8,128)(2,1)S(1)} %get-tuple-element.98), channel_id=1, source_target_pairs={{0,16},{16,0},{1,17},{17,1},{2,18},{18,2},{3,19},{19,3},{4,20},{20... | collective-permute-start | bytes 608264 | tf_op jit(solution)/shard_map/ppermute | solution.py:35
  17.2 8.9 %collective-permute-done.5 = s32[2,8]{1,0:T(2,128)S(1)} collective-permute-done((s32[2,8]{1,0:T(2,128)S(1)}, s32[2,8]{1,0:T(2,128)S(1)}, u32[]{:S(2)}, u32[]{:S(2)}) %collective-permute-start.5) | collective-permute-done | bytes 96 | tf_op jit(solution)/shard_map/ppermute | solution.py:35
  27.7 4.8 %collective-permute-done.8.s2 = bf16[4,32,792]{2,1,0:T(8,128)(2,1)S(1)} collective-permute-done((bf16[4,32,792]{2,1,0:T(8,128)(2,1)S(1)}, bf16[4,32,792]{2,1,0:T(8,128)(2,1)S(1)}, u32[]{:S(2)}, u32[]{:S(2)}) %collective-permute-start.8) | collective-permute-done | bytes 202784 | tf_op jit(solution)/shard_map/ppermute | solution.py:35
  40.3 15.1 %weight_forward.1 = (bf16[3,9,264,264]{3,2,1,0:T(8,128)(2,1)}, f32[3,256,264]{2,1,0:T(8,128)S(1)}, f32[3,8,264]{2,1,0:T(8,128)S(1)}) custom-call(s32[8]{0:T(128)S(1)} %stack.23.sc, bf16[32,128]{1,0:T(8,128)(2,1)S(1)} %collective-permute-done.2.refs_0_, bf16[1856,128]{1,0:T(8,128)(2,1)S(1)} %get-tuple-element.191.refs_1_, ...), custom_call_target="tpu_custom_call" | custom-call | bytes 3240000 | tf_op jit(solution)/shard_map/weight_forward/pallas_call | solution.py:259
  57.3 2.5 %collective-permute-start.20 = (f32[3,8,264]{2,1,0:T(8,128)S(1)}, f32[3,8,264]{2,1,0:T(8,128)S(1)}, u32[]{:S(2)}, u32[]{:S(2)}) collective-permute-start(f32[3,8,264]{2,1,0:T(8,128)S(1)} %add.49.mine_ref), channel_id=1, source_target_pairs={{0,18},{2,16},{16,2},{18,0},{1,19},{3,17},{17,3},{19,1},{4,22},{6,... | collective-permute-start | bytes 76040 | tf_op jit(solution)/shard_map/ppermute | solution.py:793
  64.9 2.1 %gate_stage.1 = (f32[3,8,264]{2,1,0:T(8,128)S(1)}, f32[2,4096]{1,0:T(2,128)S(1)}) custom-call(s32[8]{0:T(128)S(1)} %stack.23.sc, f32[3,8,264]{2,1,0:T(8,128)S(1)} %add.49.mine_ref, f32[3,8,264]{2,1,0:T(8,128)S(1)} %collective-permute-done.18.mine_far_ref, f32[3,8,264]{2,1,0:T(8,128)S(1)} %collective-permute-done.19.other_ref, ...), custom_call_target="tpu_custom_call" | custom-call | bytes 702000 | tf_op jit(solution)/shard_map/gate_stage/pallas_call | solution.py:372
  68.8 2.0 %collective-permute-start.22 = (f32[2,4096]{1,0:T(2,128)S(1)}, f32[2,4096]{1,0:T(2,128)S(1)}, u32[]{:S(2)}, u32[]{:S(2)}) collective-permute-start(f32[2,4096]{1,0:T(2,128)S(1)} %get-tuple-element.131), channel_id=1, source_target_pairs={{0,4},{4,0},{1,5},{5,1},{2,6},{6,2},{3,7},{7,3},{8,12},{12,8},{9,1... | collective-permute-start | bytes 98312 | tf_op jit(solution)/shard_map/ppermute | solution.py:35
  72.0 2.5 %copy-done.2 = bf16[3,9,264,264]{3,2,1,0:T(8,128)(2,1)S(1)} copy-done((bf16[3,9,264,264]{3,2,1,0:T(8,128)(2,1)S(1)}, bf16[3,9,264,264]{3,2,1,0:T(8,128)(2,1)}, u32[]{:S(2)}) %copy-start.2) | copy-done | bytes 3763608
  75.7 6.0 %input_grad.1 = (f32[4,64,792]{2,1,0:T(8,128)S(1)}, bf16[4,40,792]{2,1,0:T(8,128)(2,1)S(1)}, bf16[3,256,264]{2,1,0:T(8,128)(2,1)S(1)}) custom-call(s32[4,8]{1,0:T(4,128)S(1)} %pad_add_fusion.1.ids, f32[3,256,264]{2,1,0:T(8,128)S(1)} %get-tuple-element.117.hid_ref, bf16[3,256,264]{2,1,0:T(8,128)(2,1)S(1)} %copy-done.13, ...), custom_call_target="tpu_custom_call" | custom-call | bytes 1710000 | tf_op jit(solution)/shard_map/input_grad/pallas_call | solution.py:590
  83.9 7.2 %weight_grad.1 = (bf16[4,2,928,128]{3,2,1,0:T(8,128)(2,1)S(1)}, bf16[4,2,928,128]{3,2,1,0:T(8,128)(2,1)}, f32[32,128]{1,0:T(8,128)S(1)}) custom-call(s32[8]{0:T(128)S(1)} %stack.23.sc, bf16[3,256,264]{2,1,0:T(8,128)(2,1)S(1)} %get-tuple-element.132.grad_ref, bf16[3,3,10,32,264]{4,3,2,1,0:T(8,128)(2,1)S(1)} %copy-done.1), custom_call_target="tpu_custom_call" | custom-call | bytes 2142000 | tf_op jit(solution)/shard_map/weight_grad/pallas_call | solution.py:532
  97.0 1.7 %collective-permute-done.26 = f32[32,128]{1,0:T(8,128)S(1)} collective-permute-done((f32[32,128]{1,0:T(8,128)S(1)}, f32[32,128]{1,0:T(8,128)S(1)}, u32[]{:S(2)}, u32[]{:S(2)}) %collective-permute-start.26) | collective-permute-done | bytes 16416 | tf_op jit(solution)/shard_map/ppermute | solution.py:35
  98.8 1.9 %pad_add_fusion = f32[4,2,928,128]{3,2,1,0:T(8,128)S(1)} fusion(f32[4,2,32,128]{3,2,1,0:T(8,128)S(1)} %broadcast_select_fusion.1, bf16[4,2,928,128]{3,2,1,0:T(8,128)(2,1)S(1)} %collective-permute-done.25, bf16[4,2,928,128]{3,2,1,0:T(8,128)(2,1)} %copy-done.3), kind=kLoop, calls=%fused_computation | loop fusion | flops 3801088 | bytes 7733248 | tf_op jit(solution)/shard_map/add | solution.py:817
  101.1 1.8 %collective-permute-start.29 = (bf16[2,2,368,128]{3,2,1,0:T(8,128)(2,1)S(1)}, bf16[2,2,368,128]{3,2,1,0:T(8,128)(2,1)S(1)}, u32[]{:S(2)}, u32[]{:S(2)}) collective-permute-start(bf16[2,2,368,128]{3,2,1,0:T(8,128)(2,1)S(1)} %slice_bitcast_fusion.6), channel_id=1, source_target_pairs={{0,2},{2,0},{1,3},{3,1},{4,6},{6,4},{5,7},{7,5},{8,10},{10,8},{9,1... | collective-permute-start | bytes 1130504 | tf_op jit(solution)/shard_map/ppermute | solution.py:35
  102.9 4.2 %collective-permute-start.31 = (bf16[2,2,192,128]{3,2,1,0:T(8,128)(2,1)S(1)}, bf16[2,2,192,128]{3,2,1,0:T(8,128)(2,1)S(1)}, u32[]{:S(2)}, u32[]{:S(2)}) collective-permute-start(bf16[2,2,192,128]{3,2,1,0:T(8,128)(2,1)S(1)} %slice_bitcast_fusion.8), channel_id=1, source_target_pairs={{0,8},{8,0},{1,9},{9,1},{2,10},{10,2},{3,11},{11,3},{4,12},{12,4},... | collective-permute-start | bytes 589832 | tf_op jit(solution)/shard_map/ppermute | solution.py:35
  107.2 1.9 %add_rims.1 = (bf16[2,64,792]{2,1,0:T(8,128)(2,1)S(1)}, bf16[2,64,792]{2,1,0:T(8,128)(2,1)S(1)}) custom-call(s32[8]{0:T(128)S(1)} %stack.23.sc, bf16[2,64,792]{2,1,0:T(8,128)(2,1)S(1)} %copy-done.9, bf16[2,64,792]{2,1,0:T(8,128)(2,1)S(1)} %copy-done.11, f32[4,64,792]{2,1,0:T(8,128)S(1)} %copy-done.7, bf16[4,40,792]{2,1,0:T(8,128)(2,1)S(1)} %copy-done.17, ...), custom_call_target="tpu_custom_call" | custom-call | bytes 612000 | tf_op jit(solution)/shard_map/add_rims/pallas_call | solution.py:663
  109.1 1.9 %collective-permute-done.31 = bf16[2,2,192,128]{3,2,1,0:T(8,128)(2,1)S(1)} collective-permute-done((bf16[2,2,192,128]{3,2,1,0:T(8,128)(2,1)S(1)}, bf16[2,2,192,128]{3,2,1,0:T(8,128)(2,1)S(1)}, u32[]{:S(2)}, u32[]{:S(2)}) %collective-permute-start.31) | collective-permute-done | bytes 196640 | tf_op jit(solution)/shard_map/ppermute | solution.py:35
  113.5 2.8 %collective-permute-start.35 = (f32[4,4096]{1,0:T(4,128)S(1)}, f32[4,4096]{1,0:T(4,128)S(1)}, u32[]{:S(2)}, u32[]{:S(2)}) collective-permute-start(f32[4,4096]{1,0:T(4,128)S(1)} %pad_maximum_fusion.2), channel_id=1, source_target_pairs={{0,8},{8,0},{1,9},{9,1},{2,10},{10,2},{3,11},{11,3},{4,12},{12,4},... | collective-permute-start | bytes 196616 | tf_op jit(solution)/shard_map/ppermute | solution.py:35
  124.3 1.9 %collective-permute-start.37 = (bf16[368,128]{1,0:T(8,128)(2,1)S(1)}, bf16[368,128]{1,0:T(8,128)(2,1)S(1)}, u32[]{:S(2)}, u32[]{:S(2)}) collective-permute-start(bf16[368,128]{1,0:T(8,128)(2,1)S(1)} %fusion.16), channel_id=1, source_target_pairs={{0,8},{8,0},{1,9},{9,1},{2,10},{10,2},{3,11},{11,3},{4,12},{12,4},... | collective-permute-start | bytes 282632 | tf_op jit(solution)/shard_map/ppermute | solution.py:35
  127.0 2.4 %collective-permute-done.39.b_ref = bf16[2,64,792]{2,1,0:T(8,128)(2,1)S(1)} collective-permute-done((bf16[2,64,792]{2,1,0:T(8,128)(2,1)S(1)}, bf16[2,64,792]{2,1,0:T(8,128)(2,1)S(1)}, u32[]{:S(2)}, u32[]{:S(2)}) %collective-permute-start.39) | collective-permute-done | bytes 202784 | tf_op jit(solution)/shard_map/ppermute | solution.py:35
  132.6 3.0 %outer_stage.1 = (f32[1584,363]{1,0:T(8,128)}, f32[1584,363]{1,0:T(8,128)}) custom-call(f32[8,4096]{1,0:T(8,128)S(1)} %pad_maximum_fusion.1.fin_ref), custom_call_target="tpu_custom_call" | custom-call | bytes 666000 | tf_op jit(solution)/shard_map/outer_stage/pallas_call | solution.py:405
  137.1 2.6 %collective-permute-done.40.p2 = bf16[928,128]{1,0:T(8,128)(2,1)S(1)} collective-permute-done((bf16[928,128]{1,0:T(8,128)(2,1)S(1)}, bf16[928,128]{1,0:T(8,128)(2,1)S(1)}, u32[]{:S(2)}, u32[]{:S(2)}) %collective-permute-start.40) | collective-permute-done | bytes 237600 | tf_op jit(solution)/shard_map/ppermute | solution.py:35
  141.2 3.2 %place_rows.1 = f32[3676,128]{1,0:T(8,128)} custom-call(s32[8]{0:T(128)S(1)} %stack.23.sc, bf16[928,128]{1,0:T(8,128)(2,1)S(1)} %pad_maximum_fusion.p0, bf16[928,128]{1,0:T(8,128)(2,1)S(1)} %collective-permute-done.41.p1, bf16[928,128]{1,0:T(8,128)(2,1)S(1)} %collective-permute-done.40.p2, bf16[928,128]{1,0:T(8,128)(2,1)S(1)} %collective-permute-done.42.p3), custom_call_target="tpu_custom_call" | custom-call | bytes 540000 | tf_op jit(solution)/shard_map/place_rows/pallas_call | solution.py:694
  (161 shorter events, 54.7 us)
Async XLA Ops:
  2.1 8.9 %collective-permute-start.1 = (bf16[928,128]{1,0:T(8,128)(2,1)S(1)}, bf16[928,128]{1,0:T(8,128)(2,1)S(1)}, u32[]{:S(2)}, u32[]{:S(2)}) collective-permute-start(bf16[928,128]{1,0:T(8,128)(2,1)S(1)} %slice_select_fusion), channel_id=1, source_target_pairs={{0,8},{8,0},{1,9},{9,1},{2,10},{10,2},{3,11},{11,3},{4,12},{12,4},... | collective-permute-start | bytes 712712 | tf_op jit(solution)/shard_map/ppermute | solution.py:35
  6.5 26.4 %collective-permute-start.6 = (bf16[1856,128]{1,0:T(8,128)(2,1)S(1)}, bf16[1856,128]{1,0:T(8,128)(2,1)S(1)}, u32[]{:S(2)}, u32[]{:S(2)}) collective-permute-start(bf16[1856,128]{1,0:T(8,128)(2,1)S(1)} %get-tuple-element.102), channel_id=1, source_target_pairs={{0,4},{4,0},{1,5},{5,1},{2,6},{6,2},{3,7},{7,3},{8,12},{12,8},{9,1... | collective-permute-start | bytes 1425416 | tf_op jit(solution)/shard_map/ppermute | solution.py:35
  11.0 15.2 %collective-permute-start.3 = (bf16[960,128]{1,0:T(8,128)(2,1)S(1)}, bf16[960,128]{1,0:T(8,128)(2,1)S(1)}, u32[]{:S(2)}, u32[]{:S(2)}) collective-permute-start(bf16[960,128]{1,0:T(8,128)(2,1)S(1)} %constant_dynamic-update-slice_fusion.refs_4_), channel_id=1, source_target_pairs={{0,2},{2,0},{1,3},{3,1},{4,6},{6,4},{5,7},{7,5},{8,10},{10,8},{9,1... | collective-permute-start | bytes 737288 | tf_op jit(solution)/shard_map/ppermute | solution.py:35
  12.7 13.5 %collective-permute-start.4 = (bf16[928,128]{1,0:T(8,128)(2,1)S(1)}, bf16[928,128]{1,0:T(8,128)(2,1)S(1)}, u32[]{:S(2)}, u32[]{:S(2)}) collective-permute-start(bf16[928,128]{1,0:T(8,128)(2,1)S(1)} %collective-permute-done.1), channel_id=1, source_target_pairs={{0,4},{4,0},{1,5},{5,1},{2,6},{6,2},{3,7},{7,3},{8,12},{12,8},{9,1... | collective-permute-start | bytes 712712 | tf_op jit(solution)/shard_map/ppermute | solution.py:35
  14.2 11.8 %collective-permute-start = (bf16[2,64,792]{2,1,0:T(8,128)(2,1)S(1)}, bf16[2,64,792]{2,1,0:T(8,128)(2,1)S(1)}, u32[]{:S(2)}, u32[]{:S(2)}) collective-permute-start(bf16[2,64,792]{2,1,0:T(8,128)(2,1)S(1)} %get-tuple-element.98), channel_id=1, source_target_pairs={{0,16},{16,0},{1,17},{17,1},{2,18},{18,2},{3,19},{19,3},{4,20},{20... | collective-permute-start | bytes 608264 | tf_op jit(solution)/shard_map/ppermute | solution.py:35
  16.8 9.2 %collective-permute-start.5 = (s32[2,8]{1,0:T(2,128)S(1)}, s32[2,8]{1,0:T(2,128)S(1)}, u32[]{:S(2)}, u32[]{:S(2)}) collective-permute-start(s32[2,8]{1,0:T(2,128)S(1)} %bitcast.89), channel_id=1, source_target_pairs={{0,16},{16,0},{1,17},{17,1},{2,18},{18,2},{3,19},{19,3},{4,20},{20... | collective-permute-start | bytes 200 | tf_op jit(solution)/shard_map/ppermute | solution.py:35
  26.2 6.3 %collective-permute-start.8 = (bf16[4,32,792]{2,1,0:T(8,128)(2,1)S(1)}, bf16[4,32,792]{2,1,0:T(8,128)(2,1)S(1)}, u32[]{:S(2)}, u32[]{:S(2)}) collective-permute-start(bf16[4,32,792]{2,1,0:T(8,128)(2,1)S(1)} %make_strips.1.s0), channel_id=1, source_target_pairs={{0,2},{2,0},{1,3},{3,1},{4,6},{6,4},{5,7},{7,5},{8,10},{10,8},{9,1... | collective-permute-start | bytes 608264 | tf_op jit(solution)/shard_map/ppermute | solution.py:35
  32.5 6.1 %collective-permute-start.9 = (bf16[928,128]{1,0:T(8,128)(2,1)S(1)}, bf16[928,128]{1,0:T(8,128)(2,1)S(1)}, u32[]{:S(2)}, u32[]{:S(2)}) collective-permute-start(bf16[928,128]{1,0:T(8,128)(2,1)S(1)} %collective-permute-done.4.refs_5_), channel_id=1, source_target_pairs={{0,2},{2,0},{1,3},{3,1},{4,6},{6,4},{5,7},{7,5},{8,10},{10,8},{9,1... | collective-permute-start | bytes 712712 | tf_op jit(solution)/shard_map/ppermute | solution.py:35
  32.9 7.4 %collective-permute-start.11 = (bf16[1856,128]{1,0:T(8,128)(2,1)S(1)}, bf16[1856,128]{1,0:T(8,128)(2,1)S(1)}, u32[]{:S(2)}, u32[]{:S(2)}) collective-permute-start(bf16[1856,128]{1,0:T(8,128)(2,1)S(1)} %collective-permute-done.6.refs_3_), channel_id=1, source_target_pairs={{0,1},{1,0},{2,3},{3,2},{4,5},{5,4},{6,7},{7,6},{8,9},{9,8},{10,11... | collective-permute-start | bytes 1425416 | tf_op jit(solution)/shard_map/ppermute | solution.py:35
  33.4 6.9 %collective-permute-start.14 = (bf16[960,128]{1,0:T(8,128)(2,1)S(1)}, bf16[960,128]{1,0:T(8,128)(2,1)S(1)}, u32[]{:S(2)}, u32[]{:S(2)}) collective-permute-start(bf16[960,128]{1,0:T(8,128)(2,1)S(1)} %collective-permute-done.3.refs_6_), channel_id=1, source_target_pairs={{0,1},{1,0},{2,3},{3,2},{4,5},{5,4},{6,7},{7,6},{8,9},{9,8},{10,11... | collective-permute-start | bytes 737288 | tf_op jit(solution)/shard_map/ppermute | solution.py:35
  38.9 16.5 %collective-permute-start.16 = (bf16[2,64,792]{2,1,0:T(8,128)(2,1)S(1)}, bf16[2,64,792]{2,1,0:T(8,128)(2,1)S(1)}, u32[]{:S(2)}, u32[]{:S(2)}) collective-permute-start(bf16[2,64,792]{2,1,0:T(8,128)(2,1)S(1)} %get-tuple-element.116), channel_id=1, source_target_pairs={{0,16},{16,0},{1,17},{17,1},{2,18},{18,2},{3,19},{19,3},{4,20},{20... | collective-permute-start | bytes 608264 | tf_op jit(solution)/shard_map/ppermute | solution.py:35
  68.8 13.8 %collective-permute-start.22 = (f32[2,4096]{1,0:T(2,128)S(1)}, f32[2,4096]{1,0:T(2,128)S(1)}, u32[]{:S(2)}, u32[]{:S(2)}) collective-permute-start(f32[2,4096]{1,0:T(2,128)S(1)} %get-tuple-element.131), channel_id=1, source_target_pairs={{0,4},{4,0},{1,5},{5,1},{2,6},{6,2},{3,7},{7,3},{8,12},{12,8},{9,1... | collective-permute-start | bytes 98312 | tf_op jit(solution)/shard_map/ppermute | solution.py:35
  70.8 11.9 %collective-permute-start.21 = (bf16[2,64,792]{2,1,0:T(8,128)(2,1)}, bf16[2,64,792]{2,1,0:T(8,128)(2,1)S(1)}, u32[]{:S(2)}, u32[]{:S(2)}) collective-permute-start(bf16[2,64,792]{2,1,0:T(8,128)(2,1)} %copy-done.22), channel_id=1, source_target_pairs={{0,16},{16,0},{1,17},{17,1},{2,18},{18,2},{3,19},{19,3},{4,20},{20... | collective-permute-start | bytes 608264 | tf_op jit(solution)/shard_map/ppermute | solution.py:35
  83.4 8.9 %collective-permute-start.24 = (bf16[4,40,792]{2,1,0:T(8,128)(2,1)S(1)}, bf16[4,40,792]{2,1,0:T(8,128)(2,1)S(1)}, u32[]{:S(2)}, u32[]{:S(2)}) collective-permute-start(bf16[4,40,792]{2,1,0:T(8,128)(2,1)S(1)} %get-tuple-element.135.r0), channel_id=1, source_target_pairs={{0,2},{2,0},{1,3},{3,1},{4,6},{6,4},{5,7},{7,5},{8,10},{10,8},{9,1... | collective-permute-start | bytes 760328 | tf_op jit(solution)/shard_map/ppermute | solution.py:35
  83.9 8.4 %collective-permute-start.23 = (bf16[4,40,792]{2,1,0:T(8,128)(2,1)S(1)}, bf16[4,40,792]{2,1,0:T(8,128)(2,1)S(1)}, u32[]{:S(2)}, u32[]{:S(2)}) collective-permute-start(bf16[4,40,792]{2,1,0:T(8,128)(2,1)S(1)} %get-tuple-element.135.r0), channel_id=1, source_target_pairs={{0,1},{1,0},{2,3},{3,2},{4,5},{5,4},{6,7},{7,6},{8,9},{9,8},{10,11... | collective-permute-start | bytes 760328 | tf_op jit(solution)/shard_map/ppermute | solution.py:35
  92.3 6.4 %collective-permute-start.25 = (bf16[4,2,928,128]{3,2,1,0:T(8,128)(2,1)}, bf16[4,2,928,128]{3,2,1,0:T(8,128)(2,1)S(1)}, u32[]{:S(2)}, u32[]{:S(2)}) collective-permute-start(bf16[4,2,928,128]{3,2,1,0:T(8,128)(2,1)} %get-tuple-element.136), channel_id=1, source_target_pairs={{0,1},{1,0},{2,3},{3,2},{4,5},{5,4},{6,7},{7,6},{8,9},{9,8},{10,11... | collective-permute-start | bytes 5701640 | tf_op jit(solution)/shard_map/ppermute | solution.py:35
  101.1 10.1 %collective-permute-start.29 = (bf16[2,2,368,128]{3,2,1,0:T(8,128)(2,1)S(1)}, bf16[2,2,368,128]{3,2,1,0:T(8,128)(2,1)S(1)}, u32[]{:S(2)}, u32[]{:S(2)}) collective-permute-start(bf16[2,2,368,128]{3,2,1,0:T(8,128)(2,1)S(1)} %slice_bitcast_fusion.6), channel_id=1, source_target_pairs={{0,2},{2,0},{1,3},{3,1},{4,6},{6,4},{5,7},{7,5},{8,10},{10,8},{9,1... | collective-permute-start | bytes 1130504 | tf_op jit(solution)/shard_map/ppermute | solution.py:35
  102.9 9.7 %collective-permute-start.30 = (bf16[2,2,368,128]{3,2,1,0:T(8,128)(2,1)S(1)}, bf16[2,2,368,128]{3,2,1,0:T(8,128)(2,1)S(1)}, u32[]{:S(2)}, u32[]{:S(2)}) collective-permute-start(bf16[2,2,368,128]{3,2,1,0:T(8,128)(2,1)S(1)} %slice_bitcast_fusion.5), channel_id=1, source_target_pairs={{0,4},{4,0},{1,5},{5,1},{2,6},{6,2},{3,7},{7,3},{8,12},{12,8},{9,1... | collective-permute-start | bytes 1130504 | tf_op jit(solution)/shard_map/ppermute | solution.py:35
  102.9 8.1 %collective-permute-start.31 = (bf16[2,2,192,128]{3,2,1,0:T(8,128)(2,1)S(1)}, bf16[2,2,192,128]{3,2,1,0:T(8,128)(2,1)S(1)}, u32[]{:S(2)}, u32[]{:S(2)}) collective-permute-start(bf16[2,2,192,128]{3,2,1,0:T(8,128)(2,1)S(1)} %slice_bitcast_fusion.8), channel_id=1, source_target_pairs={{0,8},{8,0},{1,9},{9,1},{2,10},{10,2},{3,11},{11,3},{4,12},{12,4},... | collective-permute-start | bytes 589832 | tf_op jit(solution)/shard_map/ppermute | solution.py:35
  113.5 8.6 %collective-permute-start.35 = (f32[4,4096]{1,0:T(4,128)S(1)}, f32[4,4096]{1,0:T(4,128)S(1)}, u32[]{:S(2)}, u32[]{:S(2)}) collective-permute-start(f32[4,4096]{1,0:T(4,128)S(1)} %pad_maximum_fusion.2), channel_id=1, source_target_pairs={{0,8},{8,0},{1,9},{9,1},{2,10},{10,2},{3,11},{11,3},{4,12},{12,4},... | collective-permute-start | bytes 196616 | tf_op jit(solution)/shard_map/ppermute | solution.py:35
  119.2 10.2 %collective-permute-start.39 = (bf16[2,64,792]{2,1,0:T(8,128)(2,1)S(1)}, bf16[2,64,792]{2,1,0:T(8,128)(2,1)S(1)}, u32[]{:S(2)}, u32[]{:S(2)}) collective-permute-start(bf16[2,64,792]{2,1,0:T(8,128)(2,1)S(1)} %get-tuple-element.171), channel_id=1, source_target_pairs={{0,16},{16,0},{1,17},{17,1},{2,18},{18,2},{3,19},{19,3},{4,20},{20... | collective-permute-start | bytes 608264 | tf_op jit(solution)/shard_map/ppermute | solution.py:35
  124.1 6.2 %collective-permute-start.36 = (bf16[368,128]{1,0:T(8,128)(2,1)S(1)}, bf16[368,128]{1,0:T(8,128)(2,1)S(1)}, u32[]{:S(2)}, u32[]{:S(2)}) collective-permute-start(bf16[368,128]{1,0:T(8,128)(2,1)S(1)} %fusion.15), channel_id=1, source_target_pairs={{0,8},{8,0},{1,9},{9,1},{2,10},{10,2},{3,11},{11,3},{4,12},{12,4},... | collective-permute-start | bytes 282632 | tf_op jit(solution)/shard_map/ppermute | solution.py:35
  124.3 7.1 %collective-permute-start.37 = (bf16[368,128]{1,0:T(8,128)(2,1)S(1)}, bf16[368,128]{1,0:T(8,128)(2,1)S(1)}, u32[]{:S(2)}, u32[]{:S(2)}) collective-permute-start(bf16[368,128]{1,0:T(8,128)(2,1)S(1)} %fusion.16), channel_id=1, source_target_pairs={{0,8},{8,0},{1,9},{9,1},{2,10},{10,2},{3,11},{11,3},{4,12},{12,4},... | collective-permute-start | bytes 282632 | tf_op jit(solution)/shard_map/ppermute | solution.py:35
  131.5 8.2 %collective-permute-start.40 = (bf16[928,128]{1,0:T(8,128)(2,1)S(1)}, bf16[928,128]{1,0:T(8,128)(2,1)S(1)}, u32[]{:S(2)}, u32[]{:S(2)}) collective-permute-start(bf16[928,128]{1,0:T(8,128)(2,1)S(1)} %pad_maximum_fusion.p0), channel_id=1, source_target_pairs={{0,2},{2,0},{1,3},{3,1},{4,6},{6,4},{5,7},{7,5},{8,10},{10,8},{9,1... | collective-permute-start | bytes 712712 | tf_op jit(solution)/shard_map/ppermute | solution.py:35
  (43 other events, 287.8 us)

commit v3 on v2

--- a/solution.py
+++ b/solution.py
@@ -553,16 +553,23 @@
     )(sc, grad, x3)
 
 
-def input_grad_body(ids, hid_ref, cot_ref, gate_ref, w_ref, inner_ref, rim_ref, grad_ref, pads, part, cols):
+def input_grad_body(ids, hid_ref, cot_ref, gate_ref, w_ref, inner_ref, rim_ref, grad_ref, pads, part, cols, w, sems):
     g = pl.program_id(0)
+
+
+    @pl.when(g == 0)
+    def _():
+        for group in range(3):
+            pltpu.make_async_copy(w_ref.at[group], w.at[group], sems.at[group]).start()
 
     part[...] = jnp.zeros_like(part)
     grad = hidden_slope(hid_ref, cot_ref, gate_ref)
     grad_ref[0] = grad
+    pltpu.make_async_copy(w_ref.at[g], w.at[g], sems.at[g]).wait()
     for dx in range(3):
         cols[...] = jnp.zeros_like(cols)
         for dy in range(3):
-            d = lax.dot_general(grad, w_ref[0, 3 * dy + dx], (((1,), (1,)), ((), ())), preferred_element_type=F32)
+            d = lax.dot_general(grad, w[g, 3 * dy + dx], (((1,), (1,)), ((), ())), preferred_element_type=F32)
             cols[dy : dy + 8] += d.reshape(8, 32, CG)
         part[:, :, dx : dx + 8, :] += cols[...].reshape(10, 4, 8, CG)
     for value in range(3):
@@ -600,13 +607,15 @@
             pl.BlockSpec((1, 256, CG), lambda g: (g, 0, 0)),
             pl.BlockSpec((1, 256, CG), lambda g: (g, 0, 0)),
             pl.BlockSpec((1, 8, CG), lambda g: (g, 0, 0)),
-            pl.BlockSpec((1, 9, CG, CG), lambda g: (g, 0, 0, 0)),
+            HBM,
         ],
         out_specs=(VMEM, VMEM, pl.BlockSpec((1, 256, CG), lambda g: (g, 0, 0))),
         scratch_shapes=[
             pltpu.VMEM((10, 4, 16, HALF), F32),
             pltpu.VMEM((10, 4, 16, CG), F32),
             pltpu.VMEM((10, 32, CG), F32),
+            pltpu.VMEM((3, 9, CG, CG), BF16),
+            pltpu.SemaphoreType.DMA((3,)),
         ],
         compiler_params=params(28),
         cost_estimate=cost(9.5),

time: 145 us -> 147 us (1.014)
  Pallas kernels: 45.8 us -> 47.7 us
    pallas_call x1, Pallas kernels: 6.02 us -> 7.9 us  [input_grad(): pl.pallas_call(input_grad_body, grid=(3,), out_shape=(jax.ShapeDtypeStruc...]
  transfers between devices with their start and end apart: 43 -> 43, of which waited for: 21 -> 21; matrix products, arithmetic and copies ran while one was open for 2% -> 2% of each run, Pallas kernels for 27% -> 28%
where the time goes in v3:
time: 147 us; the launch traced here: 146 us
  Pallas kernels  47.7 us (32%)
  starting transfers between devices  43.9 us (30%)
  waiting for transfers between devices  37.8 us (26%)
  local copies, waits for them, and re-layouts  10.9 us (7%)
  other arithmetic  4.2 us (3%)
  between operations  2.01 us (1%)
    ppermute x40, starting transfers between devices, swap(): return lax.ppermute(value, axis, SWAP)  39.3 us
    ppermute x40, waiting for transfers between devices, swap(): return lax.ppermute(value, axis, SWAP)  35.2 us
    pallas_call x1, Pallas kernels, weight_forward(): pl.pallas_call(functools.partial(weight_body, sizes, plan), out_shape=(ja...  15.1 us
    unnamed x49, local copies, waits for them, and re-layouts  9.31 us
    pallas_call x1, Pallas kernels, input_grad(): pl.pallas_call(input_grad_body, grid=(3,), out_shape=(jax.ShapeDtypeStruc...  7.9 us
    pallas_call x1, Pallas kernels, weight_grad(): pl.pallas_call(functools.partial(weight_grad_body, sizes), grid=(3,), out...  7.16 us
    pallas_call x1, Pallas kernels, place_rows(): pl.pallas_call(functools.partial(rows_body, sizes), out_shape=jax.ShapeDt...  3.19 us
    pallas_call x2, Pallas kernels, join_halves(): pl.pallas_call(join_body, out_shape=jax.ShapeDtypeStruct((128, CH), BF16)...  2.98 us
  transfers between devices with their start and end apart: 43, of which 21 were waited for; matrix products, arithmetic and copies ran while one was open for 2% of the time, Pallas kernels for 28%

profile of v3, /device:TPU:0, one launch (start us, length us, event | category | flops | bytes accessed | tf_op | source)
XLA Modules:
  0.0 146.5 jit_solution(14472925257576216827)
XLA Ops:
  2.1 3.1 %collective-permute-start.1 = (bf16[928,128]{1,0:T(8,128)(2,1)S(1)}, bf16[928,128]{1,0:T(8,128)(2,1)S(1)}, u32[]{:S(2)}, u32[]{:S(2)}) collective-permute-start(bf16[928,128]{1,0:T(8,128)(2,1)S(1)} %slice_select_fusion), channel_id=1, source_target_pairs={{0,8},{8,0},{1,9},{9,1},{2,10},{10,2},{3,11},{11,3},{4,12},{12,4},... | collective-permute-start | bytes 712712 | tf_op jit(solution)/shard_map/ppermute | solution.py:35
  11.0 1.7 %collective-permute-start.3 = (bf16[960,128]{1,0:T(8,128)(2,1)S(1)}, bf16[960,128]{1,0:T(8,128)(2,1)S(1)}, u32[]{:S(2)}, u32[]{:S(2)}) collective-permute-start(bf16[960,128]{1,0:T(8,128)(2,1)S(1)} %constant_dynamic-update-slice_fusion.refs_4_), channel_id=1, source_target_pairs={{0,2},{2,0},{1,3},{3,1},{4,6},{6,4},{5,7},{7,5},{8,10},{10,8},{9,1... | collective-permute-start | bytes 737288 | tf_op jit(solution)/shard_map/ppermute | solution.py:35
  14.2 2.6 %collective-permute-start = (bf16[2,64,792]{2,1,0:T(8,128)(2,1)S(1)}, bf16[2,64,792]{2,1,0:T(8,128)(2,1)S(1)}, u32[]{:S(2)}, u32[]{:S(2)}) collective-permute-start(bf16[2,64,792]{2,1,0:T(8,128)(2,1)S(1)} %get-tuple-element.98), channel_id=1, source_target_pairs={{0,16},{16,0},{1,17},{17,1},{2,18},{18,2},{3,19},{19,3},{4,20},{20... | collective-permute-start | bytes 608264 | tf_op jit(solution)/shard_map/ppermute | solution.py:35
  17.2 8.9 %collective-permute-done.5 = s32[2,8]{1,0:T(2,128)S(1)} collective-permute-done((s32[2,8]{1,0:T(2,128)S(1)}, s32[2,8]{1,0:T(2,128)S(1)}, u32[]{:S(2)}, u32[]{:S(2)}) %collective-permute-start.5) | collective-permute-done | bytes 96 | tf_op jit(solution)/shard_map/ppermute | solution.py:35
  27.7 4.8 %collective-permute-done.8.s2 = bf16[4,32,792]{2,1,0:T(8,128)(2,1)S(1)} collective-permute-done((bf16[4,32,792]{2,1,0:T(8,128)(2,1)S(1)}, bf16[4,32,792]{2,1,0:T(8,128)(2,1)S(1)}, u32[]{:S(2)}, u32[]{:S(2)}) %collective-permute-start.8) | collective-permute-done | bytes 202784 | tf_op jit(solution)/shard_map/ppermute | solution.py:35
  40.3 15.1 %weight_forward.1 = (bf16[3,9,264,264]{3,2,1,0:T(8,128)(2,1)}, f32[3,256,264]{2,1,0:T(8,128)S(1)}, f32[3,8,264]{2,1,0:T(8,128)S(1)}) custom-call(s32[8]{0:T(128)S(1)} %stack.23.sc, bf16[32,128]{1,0:T(8,128)(2,1)S(1)} %collective-permute-done.2.refs_0_, bf16[1856,128]{1,0:T(8,128)(2,1)S(1)} %get-tuple-element.191.refs_1_, ...), custom_call_target="tpu_custom_call" | custom-call | bytes 3240000 | tf_op jit(solution)/shard_map/weight_forward/pallas_call | solution.py:259
  57.3 2.5 %collective-permute-start.20 = (f32[3,8,264]{2,1,0:T(8,128)S(1)}, f32[3,8,264]{2,1,0:T(8,128)S(1)}, u32[]{:S(2)}, u32[]{:S(2)}) collective-permute-start(f32[3,8,264]{2,1,0:T(8,128)S(1)} %add.49.mine_ref), channel_id=1, source_target_pairs={{0,18},{2,16},{16,2},{18,0},{1,19},{3,17},{17,3},{19,1},{4,22},{6,... | collective-permute-start | bytes 76040 | tf_op jit(solution)/shard_map/ppermute | solution.py:802
  64.9 2.1 %gate_stage.1 = (f32[3,8,264]{2,1,0:T(8,128)S(1)}, f32[2,4096]{1,0:T(2,128)S(1)}) custom-call(s32[8]{0:T(128)S(1)} %stack.23.sc, f32[3,8,264]{2,1,0:T(8,128)S(1)} %add.49.mine_ref, f32[3,8,264]{2,1,0:T(8,128)S(1)} %collective-permute-done.18.mine_far_ref, f32[3,8,264]{2,1,0:T(8,128)S(1)} %collective-permute-done.19.other_ref, ...), custom_call_target="tpu_custom_call" | custom-call | bytes 702000 | tf_op jit(solution)/shard_map/gate_stage/pallas_call | solution.py:372
  68.8 2.0 %collective-permute-start.22 = (f32[2,4096]{1,0:T(2,128)S(1)}, f32[2,4096]{1,0:T(2,128)S(1)}, u32[]{:S(2)}, u32[]{:S(2)}) collective-permute-start(f32[2,4096]{1,0:T(2,128)S(1)} %get-tuple-element.131), channel_id=1, source_target_pairs={{0,4},{4,0},{1,5},{5,1},{2,6},{6,2},{3,7},{7,3},{8,12},{12,8},{9,1... | collective-permute-start | bytes 98312 | tf_op jit(solution)/shard_map/ppermute | solution.py:35
  72.0 2.5 %copy-done.2 = bf16[3,9,264,264]{3,2,1,0:T(8,128)(2,1)S(1)} copy-done((bf16[3,9,264,264]{3,2,1,0:T(8,128)(2,1)S(1)}, bf16[3,9,264,264]{3,2,1,0:T(8,128)(2,1)}, u32[]{:S(2)}) %copy-start.2) | copy-done | bytes 3763608
  75.7 7.9 %input_grad.1 = (f32[4,64,792]{2,1,0:T(8,128)S(1)}, bf16[4,40,792]{2,1,0:T(8,128)(2,1)S(1)}, bf16[3,256,264]{2,1,0:T(8,128)(2,1)S(1)}) custom-call(s32[4,8]{1,0:T(4,128)S(1)} %pad_add_fusion.1.ids, f32[3,256,264]{2,1,0:T(8,128)S(1)} %get-tuple-element.117.hid_ref, bf16[3,256,264]{2,1,0:T(8,128)(2,1)S(1)} %copy-done.13, ...), custom_call_target="tpu_custom_call" | custom-call | bytes 1710000 | tf_op jit(solution)/shard_map/input_grad/pallas_call | solution.py:597
  85.6 7.2 %weight_grad.1 = (bf16[4,2,928,128]{3,2,1,0:T(8,128)(2,1)S(1)}, bf16[4,2,928,128]{3,2,1,0:T(8,128)(2,1)}, f32[32,128]{1,0:T(8,128)S(1)}) custom-call(s32[8]{0:T(128)S(1)} %stack.23.sc, bf16[3,256,264]{2,1,0:T(8,128)(2,1)S(1)} %get-tuple-element.132.grad_ref, bf16[3,3,10,32,264]{4,3,2,1,0:T(8,128)(2,1)S(1)} %copy-done.1), custom_call_target="tpu_custom_call" | custom-call | bytes 2142000 | tf_op jit(solution)/shard_map/weight_grad/pallas_call | solution.py:532
  98.7 1.9 %collective-permute-done.26 = f32[32,128]{1,0:T(8,128)S(1)} collective-permute-done((f32[32,128]{1,0:T(8,128)S(1)}, f32[32,128]{1,0:T(8,128)S(1)}, u32[]{:S(2)}, u32[]{:S(2)}) %collective-permute-start.26) | collective-permute-done | bytes 16416 | tf_op jit(solution)/shard_map/ppermute | solution.py:35
  100.7 1.9 %pad_add_fusion = f32[4,2,928,128]{3,2,1,0:T(8,128)S(1)} fusion(f32[4,2,32,128]{3,2,1,0:T(8,128)S(1)} %broadcast_select_fusion.1, bf16[4,2,928,128]{3,2,1,0:T(8,128)(2,1)S(1)} %collective-permute-done.25, bf16[4,2,928,128]{3,2,1,0:T(8,128)(2,1)} %copy-done.3), kind=kLoop, calls=%fused_computation | loop fusion | flops 3801088 | bytes 7733248 | tf_op jit(solution)/shard_map/add | solution.py:826
  103.0 1.8 %collective-permute-start.29 = (bf16[2,2,368,128]{3,2,1,0:T(8,128)(2,1)S(1)}, bf16[2,2,368,128]{3,2,1,0:T(8,128)(2,1)S(1)}, u32[]{:S(2)}, u32[]{:S(2)}) collective-permute-start(bf16[2,2,368,128]{3,2,1,0:T(8,128)(2,1)S(1)} %slice_bitcast_fusion.6), channel_id=1, source_target_pairs={{0,2},{2,0},{1,3},{3,1},{4,6},{6,4},{5,7},{7,5},{8,10},{10,8},{9,1... | collective-permute-start | bytes 1130504 | tf_op jit(solution)/shard_map/ppermute | solution.py:35
  104.8 4.2 %collective-permute-start.31 = (bf16[2,2,192,128]{3,2,1,0:T(8,128)(2,1)S(1)}, bf16[2,2,192,128]{3,2,1,0:T(8,128)(2,1)S(1)}, u32[]{:S(2)}, u32[]{:S(2)}) collective-permute-start(bf16[2,2,192,128]{3,2,1,0:T(8,128)(2,1)S(1)} %slice_bitcast_fusion.8), channel_id=1, source_target_pairs={{0,8},{8,0},{1,9},{9,1},{2,10},{10,2},{3,11},{11,3},{4,12},{12,4},... | collective-permute-start | bytes 589832 | tf_op jit(solution)/shard_map/ppermute | solution.py:35
  109.0 1.9 %add_rims.1 = (bf16[2,64,792]{2,1,0:T(8,128)(2,1)S(1)}, bf16[2,64,792]{2,1,0:T(8,128)(2,1)S(1)}) custom-call(s32[8]{0:T(128)S(1)} %stack.23.sc, bf16[2,64,792]{2,1,0:T(8,128)(2,1)S(1)} %copy-done.9, bf16[2,64,792]{2,1,0:T(8,128)(2,1)S(1)} %copy-done.11, f32[4,64,792]{2,1,0:T(8,128)S(1)} %copy-done.7, bf16[4,40,792]{2,1,0:T(8,128)(2,1)S(1)} %copy-done.17, ...), custom_call_target="tpu_custom_call" | custom-call | bytes 612000 | tf_op jit(solution)/shard_map/add_rims/pallas_call | solution.py:672
  110.9 1.9 %collective-permute-done.31 = bf16[2,2,192,128]{3,2,1,0:T(8,128)(2,1)S(1)} collective-permute-done((bf16[2,2,192,128]{3,2,1,0:T(8,128)(2,1)S(1)}, bf16[2,2,192,128]{3,2,1,0:T(8,128)(2,1)S(1)}, u32[]{:S(2)}, u32[]{:S(2)}) %collective-permute-start.31) | collective-permute-done | bytes 196640 | tf_op jit(solution)/shard_map/ppermute | solution.py:35
  115.4 2.8 %collective-permute-start.35 = (f32[4,4096]{1,0:T(4,128)S(1)}, f32[4,4096]{1,0:T(4,128)S(1)}, u32[]{:S(2)}, u32[]{:S(2)}) collective-permute-start(f32[4,4096]{1,0:T(4,128)S(1)} %pad_maximum_fusion.2), channel_id=1, source_target_pairs={{0,8},{8,0},{1,9},{9,1},{2,10},{10,2},{3,11},{11,3},{4,12},{12,4},... | collective-permute-start | bytes 196616 | tf_op jit(solution)/shard_map/ppermute | solution.py:35
  126.2 1.9 %collective-permute-start.37 = (bf16[368,128]{1,0:T(8,128)(2,1)S(1)}, bf16[368,128]{1,0:T(8,128)(2,1)S(1)}, u32[]{:S(2)}, u32[]{:S(2)}) collective-permute-start(bf16[368,128]{1,0:T(8,128)(2,1)S(1)} %fusion.16), channel_id=1, source_target_pairs={{0,8},{8,0},{1,9},{9,1},{2,10},{10,2},{3,11},{11,3},{4,12},{12,4},... | collective-permute-start | bytes 282632 | tf_op jit(solution)/shard_map/ppermute | solution.py:35
  128.9 2.4 %collective-permute-done.39.b_ref = bf16[2,64,792]{2,1,0:T(8,128)(2,1)S(1)} collective-permute-done((bf16[2,64,792]{2,1,0:T(8,128)(2,1)S(1)}, bf16[2,64,792]{2,1,0:T(8,128)(2,1)S(1)}, u32[]{:S(2)}, u32[]{:S(2)}) %collective-permute-start.39) | collective-permute-done | bytes 202784 | tf_op jit(solution)/shard_map/ppermute | solution.py:35
  134.5 3.0 %outer_stage.1 = (f32[1584,363]{1,0:T(8,128)}, f32[1584,363]{1,0:T(8,128)}) custom-call(f32[8,4096]{1,0:T(8,128)S(1)} %pad_maximum_fusion.1.fin_ref), custom_call_target="tpu_custom_call" | custom-call | bytes 666000 | tf_op jit(solution)/shard_map/outer_stage/pallas_call | solution.py:405
  139.0 2.6 %collective-permute-done.40.p2 = bf16[928,128]{1,0:T(8,128)(2,1)S(1)} collective-permute-done((bf16[928,128]{1,0:T(8,128)(2,1)S(1)}, bf16[928,128]{1,0:T(8,128)(2,1)S(1)}, u32[]{:S(2)}, u32[]{:S(2)}) %collective-permute-start.40) | collective-permute-done | bytes 237600 | tf_op jit(solution)/shard_map/ppermute | solution.py:35
  143.1 3.2 %place_rows.1 = f32[3676,128]{1,0:T(8,128)} custom-call(s32[8]{0:T(128)S(1)} %stack.23.sc, bf16[928,128]{1,0:T(8,128)(2,1)S(1)} %pad_maximum_fusion.p0, bf16[928,128]{1,0:T(8,128)(2,1)S(1)} %collective-permute-done.41.p1, bf16[928,128]{1,0:T(8,128)(2,1)S(1)} %collective-permute-done.40.p2, bf16[928,128]{1,0:T(8,128)(2,1)S(1)} %collective-permute-done.42.p3), custom_call_target="tpu_custom_call" | custom-call | bytes 540000 | tf_op jit(solution)/shard_map/place_rows/pallas_call | solution.py:703
  (161 shorter events, 54.5 us)
Async XLA Ops:
  2.1 8.9 %collective-permute-start.1 = (bf16[928,128]{1,0:T(8,128)(2,1)S(1)}, bf16[928,128]{1,0:T(8,128)(2,1)S(1)}, u32[]{:S(2)}, u32[]{:S(2)}) collective-permute-start(bf16[928,128]{1,0:T(8,128)(2,1)S(1)} %slice_select_fusion), channel_id=1, source_target_pairs={{0,8},{8,0},{1,9},{9,1},{2,10},{10,2},{3,11},{11,3},{4,12},{12,4},... | collective-permute-start | bytes 712712 | tf_op jit(solution)/shard_map/ppermute | solution.py:35
  6.5 26.4 %collective-permute-start.6 = (bf16[1856,128]{1,0:T(8,128)(2,1)S(1)}, bf16[1856,128]{1,0:T(8,128)(2,1)S(1)}, u32[]{:S(2)}, u32[]{:S(2)}) collective-permute-start(bf16[1856,128]{1,0:T(8,128)(2,1)S(1)} %get-tuple-element.102), channel_id=1, source_target_pairs={{0,4},{4,0},{1,5},{5,1},{2,6},{6,2},{3,7},{7,3},{8,12},{12,8},{9,1... | collective-permute-start | bytes 1425416 | tf_op jit(solution)/shard_map/ppermute | solution.py:35
  11.0 15.2 %collective-permute-start.3 = (bf16[960,128]{1,0:T(8,128)(2,1)S(1)}, bf16[960,128]{1,0:T(8,128)(2,1)S(1)}, u32[]{:S(2)}, u32[]{:S(2)}) collective-permute-start(bf16[960,128]{1,0:T(8,128)(2,1)S(1)} %constant_dynamic-update-slice_fusion.refs_4_), channel_id=1, source_target_pairs={{0,2},{2,0},{1,3},{3,1},{4,6},{6,4},{5,7},{7,5},{8,10},{10,8},{9,1... | collective-permute-start | bytes 737288 | tf_op jit(solution)/shard_map/ppermute | solution.py:35
  12.7 13.5 %collective-permute-start.4 = (bf16[928,128]{1,0:T(8,128)(2,1)S(1)}, bf16[928,128]{1,0:T(8,128)(2,1)S(1)}, u32[]{:S(2)}, u32[]{:S(2)}) collective-permute-start(bf16[928,128]{1,0:T(8,128)(2,1)S(1)} %collective-permute-done.1), channel_id=1, source_target_pairs={{0,4},{4,0},{1,5},{5,1},{2,6},{6,2},{3,7},{7,3},{8,12},{12,8},{9,1... | collective-permute-start | bytes 712712 | tf_op jit(solution)/shard_map/ppermute | solution.py:35
  14.2 11.8 %collective-permute-start = (bf16[2,64,792]{2,1,0:T(8,128)(2,1)S(1)}, bf16[2,64,792]{2,1,0:T(8,128)(2,1)S(1)}, u32[]{:S(2)}, u32[]{:S(2)}) collective-permute-start(bf16[2,64,792]{2,1,0:T(8,128)(2,1)S(1)} %get-tuple-element.98), channel_id=1, source_target_pairs={{0,16},{16,0},{1,17},{17,1},{2,18},{18,2},{3,19},{19,3},{4,20},{20... | collective-permute-start | bytes 608264 | tf_op jit(solution)/shard_map/ppermute | solution.py:35
  16.8 9.2 %collective-permute-start.5 = (s32[2,8]{1,0:T(2,128)S(1)}, s32[2,8]{1,0:T(2,128)S(1)}, u32[]{:S(2)}, u32[]{:S(2)}) collective-permute-start(s32[2,8]{1,0:T(2,128)S(1)} %bitcast.89), channel_id=1, source_target_pairs={{0,16},{16,0},{1,17},{17,1},{2,18},{18,2},{3,19},{19,3},{4,20},{20... | collective-permute-start | bytes 200 | tf_op jit(solution)/shard_map/ppermute | solution.py:35
  26.2 6.3 %collective-permute-start.8 = (bf16[4,32,792]{2,1,0:T(8,128)(2,1)S(1)}, bf16[4,32,792]{2,1,0:T(8,128)(2,1)S(1)}, u32[]{:S(2)}, u32[]{:S(2)}) collective-permute-start(bf16[4,32,792]{2,1,0:T(8,128)(2,1)S(1)} %make_strips.1.s0), channel_id=1, source_target_pairs={{0,2},{2,0},{1,3},{3,1},{4,6},{6,4},{5,7},{7,5},{8,10},{10,8},{9,1... | collective-permute-start | bytes 608264 | tf_op jit(solution)/shard_map/ppermute | solution.py:35
  32.5 6.1 %collective-permute-start.9 = (bf16[928,128]{1,0:T(8,128)(2,1)S(1)}, bf16[928,128]{1,0:T(8,128)(2,1)S(1)}, u32[]{:S(2)}, u32[]{:S(2)}) collective-permute-start(bf16[928,128]{1,0:T(8,128)(2,1)S(1)} %collective-permute-done.4.refs_5_), channel_id=1, source_target_pairs={{0,2},{2,0},{1,3},{3,1},{4,6},{6,4},{5,7},{7,5},{8,10},{10,8},{9,1... | collective-permute-start | bytes 712712 | tf_op jit(solution)/shard_map/ppermute | solution.py:35
  32.9 7.4 %collective-permute-start.11 = (bf16[1856,128]{1,0:T(8,128)(2,1)S(1)}, bf16[1856,128]{1,0:T(8,128)(2,1)S(1)}, u32[]{:S(2)}, u32[]{:S(2)}) collective-permute-start(bf16[1856,128]{1,0:T(8,128)(2,1)S(1)} %collective-permute-done.6.refs_3_), channel_id=1, source_target_pairs={{0,1},{1,0},{2,3},{3,2},{4,5},{5,4},{6,7},{7,6},{8,9},{9,8},{10,11... | collective-permute-start | bytes 1425416 | tf_op jit(solution)/shard_map/ppermute | solution.py:35
  33.4 6.9 %collective-permute-start.14 = (bf16[960,128]{1,0:T(8,128)(2,1)S(1)}, bf16[960,128]{1,0:T(8,128)(2,1)S(1)}, u32[]{:S(2)}, u32[]{:S(2)}) collective-permute-start(bf16[960,128]{1,0:T(8,128)(2,1)S(1)} %collective-permute-done.3.refs_6_), channel_id=1, source_target_pairs={{0,1},{1,0},{2,3},{3,2},{4,5},{5,4},{6,7},{7,6},{8,9},{9,8},{10,11... | collective-permute-start | bytes 737288 | tf_op jit(solution)/shard_map/ppermute | solution.py:35
  38.9 16.5 %collective-permute-start.16 = (bf16[2,64,792]{2,1,0:T(8,128)(2,1)S(1)}, bf16[2,64,792]{2,1,0:T(8,128)(2,1)S(1)}, u32[]{:S(2)}, u32[]{:S(2)}) collective-permute-start(bf16[2,64,792]{2,1,0:T(8,128)(2,1)S(1)} %get-tuple-element.116), channel_id=1, source_target_pairs={{0,16},{16,0},{1,17},{17,1},{2,18},{18,2},{3,19},{19,3},{4,20},{20... | collective-permute-start | bytes 608264 | tf_op jit(solution)/shard_map/ppermute | solution.py:35
  68.8 15.7 %collective-permute-start.22 = (f32[2,4096]{1,0:T(2,128)S(1)}, f32[2,4096]{1,0:T(2,128)S(1)}, u32[]{:S(2)}, u32[]{:S(2)}) collective-permute-start(f32[2,4096]{1,0:T(2,128)S(1)} %get-tuple-element.131), channel_id=1, source_target_pairs={{0,4},{4,0},{1,5},{5,1},{2,6},{6,2},{3,7},{7,3},{8,12},{12,8},{9,1... | collective-permute-start | bytes 98312 | tf_op jit(solution)/shard_map/ppermute | solution.py:35
  70.8 13.7 %collective-permute-start.21 = (bf16[2,64,792]{2,1,0:T(8,128)(2,1)}, bf16[2,64,792]{2,1,0:T(8,128)(2,1)S(1)}, u32[]{:S(2)}, u32[]{:S(2)}) collective-permute-start(bf16[2,64,792]{2,1,0:T(8,128)(2,1)} %copy-done.22), channel_id=1, source_target_pairs={{0,16},{16,0},{1,17},{17,1},{2,18},{18,2},{3,19},{19,3},{4,20},{20... | collective-permute-start | bytes 608264 | tf_op jit(solution)/shard_map/ppermute | solution.py:35
  85.3 8.7 %collective-permute-start.24 = (bf16[4,40,792]{2,1,0:T(8,128)(2,1)S(1)}, bf16[4,40,792]{2,1,0:T(8,128)(2,1)S(1)}, u32[]{:S(2)}, u32[]{:S(2)}) collective-permute-start(bf16[4,40,792]{2,1,0:T(8,128)(2,1)S(1)} %get-tuple-element.135.r0), channel_id=1, source_target_pairs={{0,2},{2,0},{1,3},{3,1},{4,6},{6,4},{5,7},{7,5},{8,10},{10,8},{9,1... | collective-permute-start | bytes 760328 | tf_op jit(solution)/shard_map/ppermute | solution.py:35
  85.6 8.4 %collective-permute-start.23 = (bf16[4,40,792]{2,1,0:T(8,128)(2,1)S(1)}, bf16[4,40,792]{2,1,0:T(8,128)(2,1)S(1)}, u32[]{:S(2)}, u32[]{:S(2)}) collective-permute-start(bf16[4,40,792]{2,1,0:T(8,128)(2,1)S(1)} %get-tuple-element.135.r0), channel_id=1, source_target_pairs={{0,1},{1,0},{2,3},{3,2},{4,5},{5,4},{6,7},{7,6},{8,9},{9,8},{10,11... | collective-permute-start | bytes 760328 | tf_op jit(solution)/shard_map/ppermute | solution.py:35
  94.0 6.5 %collective-permute-start.25 = (bf16[4,2,928,128]{3,2,1,0:T(8,128)(2,1)}, bf16[4,2,928,128]{3,2,1,0:T(8,128)(2,1)S(1)}, u32[]{:S(2)}, u32[]{:S(2)}) collective-permute-start(bf16[4,2,928,128]{3,2,1,0:T(8,128)(2,1)} %get-tuple-element.136), channel_id=1, source_target_pairs={{0,1},{1,0},{2,3},{3,2},{4,5},{5,4},{6,7},{7,6},{8,9},{9,8},{10,11... | collective-permute-start | bytes 5701640 | tf_op jit(solution)/shard_map/ppermute | solution.py:35
  103.0 10.1 %collective-permute-start.29 = (bf16[2,2,368,128]{3,2,1,0:T(8,128)(2,1)S(1)}, bf16[2,2,368,128]{3,2,1,0:T(8,128)(2,1)S(1)}, u32[]{:S(2)}, u32[]{:S(2)}) collective-permute-start(bf16[2,2,368,128]{3,2,1,0:T(8,128)(2,1)S(1)} %slice_bitcast_fusion.6), channel_id=1, source_target_pairs={{0,2},{2,0},{1,3},{3,1},{4,6},{6,4},{5,7},{7,5},{8,10},{10,8},{9,1... | collective-permute-start | bytes 1130504 | tf_op jit(solution)/shard_map/ppermute | solution.py:35
  104.8 9.7 %collective-permute-start.30 = (bf16[2,2,368,128]{3,2,1,0:T(8,128)(2,1)S(1)}, bf16[2,2,368,128]{3,2,1,0:T(8,128)(2,1)S(1)}, u32[]{:S(2)}, u32[]{:S(2)}) collective-permute-start(bf16[2,2,368,128]{3,2,1,0:T(8,128)(2,1)S(1)} %slice_bitcast_fusion.5), channel_id=1, source_target_pairs={{0,4},{4,0},{1,5},{5,1},{2,6},{6,2},{3,7},{7,3},{8,12},{12,8},{9,1... | collective-permute-start | bytes 1130504 | tf_op jit(solution)/shard_map/ppermute | solution.py:35
  104.8 8.1 %collective-permute-start.31 = (bf16[2,2,192,128]{3,2,1,0:T(8,128)(2,1)S(1)}, bf16[2,2,192,128]{3,2,1,0:T(8,128)(2,1)S(1)}, u32[]{:S(2)}, u32[]{:S(2)}) collective-permute-start(bf16[2,2,192,128]{3,2,1,0:T(8,128)(2,1)S(1)} %slice_bitcast_fusion.8), channel_id=1, source_target_pairs={{0,8},{8,0},{1,9},{9,1},{2,10},{10,2},{3,11},{11,3},{4,12},{12,4},... | collective-permute-start | bytes 589832 | tf_op jit(solution)/shard_map/ppermute | solution.py:35
  115.4 8.6 %collective-permute-start.35 = (f32[4,4096]{1,0:T(4,128)S(1)}, f32[4,4096]{1,0:T(4,128)S(1)}, u32[]{:S(2)}, u32[]{:S(2)}) collective-permute-start(f32[4,4096]{1,0:T(4,128)S(1)} %pad_maximum_fusion.2), channel_id=1, source_target_pairs={{0,8},{8,0},{1,9},{9,1},{2,10},{10,2},{3,11},{11,3},{4,12},{12,4},... | collective-permute-start | bytes 196616 | tf_op jit(solution)/shard_map/ppermute | solution.py:35
  121.1 10.2 %collective-permute-start.39 = (bf16[2,64,792]{2,1,0:T(8,128)(2,1)S(1)}, bf16[2,64,792]{2,1,0:T(8,128)(2,1)S(1)}, u32[]{:S(2)}, u32[]{:S(2)}) collective-permute-start(bf16[2,64,792]{2,1,0:T(8,128)(2,1)S(1)} %get-tuple-element.171), channel_id=1, source_target_pairs={{0,16},{16,0},{1,17},{17,1},{2,18},{18,2},{3,19},{19,3},{4,20},{20... | collective-permute-start | bytes 608264 | tf_op jit(solution)/shard_map/ppermute | solution.py:35
  126.0 6.2 %collective-permute-start.36 = (bf16[368,128]{1,0:T(8,128)(2,1)S(1)}, bf16[368,128]{1,0:T(8,128)(2,1)S(1)}, u32[]{:S(2)}, u32[]{:S(2)}) collective-permute-start(bf16[368,128]{1,0:T(8,128)(2,1)S(1)} %fusion.15), channel_id=1, source_target_pairs={{0,8},{8,0},{1,9},{9,1},{2,10},{10,2},{3,11},{11,3},{4,12},{12,4},... | collective-permute-start | bytes 282632 | tf_op jit(solution)/shard_map/ppermute | solution.py:35
  126.2 7.1 %collective-permute-start.37 = (bf16[368,128]{1,0:T(8,128)(2,1)S(1)}, bf16[368,128]{1,0:T(8,128)(2,1)S(1)}, u32[]{:S(2)}, u32[]{:S(2)}) collective-permute-start(bf16[368,128]{1,0:T(8,128)(2,1)S(1)} %fusion.16), channel_id=1, source_target_pairs={{0,8},{8,0},{1,9},{9,1},{2,10},{10,2},{3,11},{11,3},{4,12},{12,4},... | collective-permute-start | bytes 282632 | tf_op jit(solution)/shard_map/ppermute | solution.py:35
  133.4 8.2 %collective-permute-start.40 = (bf16[928,128]{1,0:T(8,128)(2,1)S(1)}, bf16[928,128]{1,0:T(8,128)(2,1)S(1)}, u32[]{:S(2)}, u32[]{:S(2)}) collective-permute-start(bf16[928,128]{1,0:T(8,128)(2,1)S(1)} %pad_maximum_fusion.p0), channel_id=1, source_target_pairs={{0,2},{2,0},{1,3},{3,1},{4,6},{6,4},{5,7},{7,5},{8,10},{10,8},{9,1... | collective-permute-start | bytes 712712 | tf_op jit(solution)/shard_map/ppermute | solution.py:35
  (43 other events, 287.8 us)
